TPU v7x, 32 devices: a whole 2x2x4 slice. The times are simulated.
32 devices in a mesh: section: 2 (over x), seq: 4 (over z), tp: 4 (over y, core).
Axes of the slice: x: 2, y: 2, z: 4, core: 2. Of those that a mesh axis runs over, the one named last changes fastest.
Arguments:
- layer_input: bfloat16 [2, 1024, 8192], P('section', 'seq', 'tp'), may hold values from -200 to 200, as said below
- norm_gain: float32 [2, 8192], P('section', 'tp'), may hold values from 0.1 to 1.9
- kv_cotangent: bfloat16 [2, 1024, 2048], P('section', 'seq', 'tp'), may hold values from -8 to 8
- kv_weight: bfloat16 [2, 2048, 8192], P('section', 'tp', 'seq'), may hold values from -0.09375 to 0.09375
- mlp_grads: bfloat16 [2, 1024, 8192], P('section', 'seq', 'tp'), may hold values from -6 to 6
- output_cotangent: bfloat16 [1024, 8192], P('seq', 'tp'), may hold values from -6 to 6
- out_weight: bfloat16 [2, 8192, 8192], P('section', 'tp', 'seq'), may hold values from -0.0625 to 0.0625
Outputs:
- attn_grads: bfloat16 [2, 1024, 8192], P('section', 'seq', 'tp')
- input_grads: bfloat16 [2, 1024, 8192], P('section', 'seq', 'tp')
Inputs may be any that keep to these rules, and one draw needn't show every extreme that they name: `layer_input`: real-valued activations.
All inputs are finite; a program needn't handle non-finite values.
Results may differ from a plain program's by a relative error of at most 0.0055.
Values may be sent and summed in bfloat16 or wider, within the bound.
No kernel may reach another device: no remote copies, remote signals or barrier semaphores. Data moves between devices by JAX's collectives and lax.ppermute only.
A program may use at most 128 MiB of HBM per device.

v0:
```python
import jax
import jax.numpy as jnp
from jax import lax
from jax.sharding import PartitionSpec as P

D = 8192


epsilon = 1e-05


def from_behind(block, axis, distance):
    devices = range(lax.axis_size(axis))
    route = [(i - distance, i) for i in devices if i - distance in devices]
    return lax.ppermute(block, axis, route)


def body(layer_input, norm_gain, kv_cotangent, kv_weight, mlp_grads, output_cotangent, out_weight):
    section_index = lax.axis_index("section")
    values = layer_input[0].astype(jnp.float32)
    gain = norm_gain[0]
    cotangent = kv_cotangent[0]
    kv_terms = jnp.dot(
        cotangent,
        lax.all_gather(kv_weight[0], "seq", axis=1, tiled=True),
        preferred_element_type=jnp.float32,
    )
    kv_share = lax.psum_scatter(kv_terms, "tp", scatter_dimension=1, tiled=True)
    squares, intersection = lax.psum(
        (jnp.sum(values * values, axis=1), jnp.sum(gain * kv_share * values, axis=1)), "tp"
    )
    inv_rms = lax.rsqrt(squares / D + epsilon)[:, None]
    norm_back = (
        inv_rms * gain * kv_share
        - values * (inv_rms * inv_rms * inv_rms) * intersection[:, None] / D
    )
    branch = mlp_grads[0].astype(jnp.float32)
    grad_one = output_cotangent.astype(jnp.float32) + branch
    input_one = (grad_one + norm_back).astype(jnp.bfloat16)
    arriving = from_behind(input_one, "section", -1)
    grad_zero = arriving.astype(jnp.float32) + branch
    upstream = section_index == 0
    input_part = jnp.where(upstream, (grad_zero + norm_back).astype(jnp.bfloat16), input_one)
    grad_cast = jnp.where(upstream, grad_zero, grad_one).astype(jnp.bfloat16)
    grad_full = lax.all_gather(grad_cast, "tp", axis=1, tiled=True)
    attn_part = lax.dot_general(
        grad_full,
        lax.all_gather(out_weight[0], "seq", axis=1, tiled=True),
        (((1,), (1,)), ((), ())),
        preferred_element_type=jnp.float32,
    )
    return (attn_part.astype(jnp.bfloat16)[None], input_part[None])


def solution(mesh):
    in_specs = (
        P("section", "seq", "tp"),
        P("section", "tp"),
        P("section", "seq", "tp"),
        P("section", "tp", "seq"),
        P("section", "seq", "tp"),
        P("seq", "tp"),
        P("section", "tp", "seq"),
    )
    out_specs = (P("section", "seq", "tp"), P("section", "seq", "tp"))
    return jax.shard_map(body, mesh=mesh, in_specs=in_specs, out_specs=out_specs, check_vma=False)
```

profile of v0, /device:TPU:0, one launch (start us, length us, event | category | flops | bytes accessed | tf_op | source)
XLA Modules:
  0.0 902.7 jit_solution(2521590300799915843)
XLA Ops:
  7.2 0.0 copy-start
  7.2 0.0 all-gather.8.cloned.1.call-start
  7.2 0.7 all-gather.8.cloned.1.call-update
  7.9 0.0 reduce-scatter.2.cloned.1.call-start
  8.0 154.0 %all-gather.8.cloned.1.call-done = bf16[1,512,8192]{2,1,0:T(8,128)(2,1)} async-done(((bf16[1,512,2048]{2,1,0:T(8,128)(2,1)}), bf16[1,512,8192]{2,1,0:T(8,128)(2,1)}) %all-gather.8.cloned.1.call-update) | async-done | bytes 8388624 | tf_op jit(solution)/shard_map/all_gather | solution.py:25
  162.0 0.0 copy-done
  162.0 9.0 fusion.2
  170.9 0.0 reduce-scatter.2.cloned.1.call-update
  170.9 0.0 copy-start.3
  171.0 0.0 all-gather.6.cloned.1.call-start
  171.0 70.0 %reduce-scatter.2.cloned.1.call-done = f32[256,2048]{1,0:T(8,128)} async-done(((f32[256,8192]{1,0:T(8,128)}), f32[256,2048]{1,0:T(8,128)}) %reduce-scatter.2.cloned.1.call-update) | async-done | bytes 2097168 | tf_op jit(solution)/shard_map/reduce_scatter | solution.py:28
  241.0 2.6 fusion.10
  243.6 5.8 all-reduce
  249.4 3.4 add_convert_fusion.1
  252.7 1.3 collective-permute-start
  254.0 25.8 %collective-permute-done = bf16[256,2048]{1,0:T(8,128)(2,1)} collective-permute-done((bf16[256,2048]{1,0:T(8,128)(2,1)}, bf16[256,2048]{1,0:T(8,128)(2,1)}, u32[]{:S(2)}, u32[]{:S(2)}) %collective-permute-start) | collective-permute-done | bytes 1048608 | tf_op jit(solution)/shard_map/ppermute | solution.py:15
  279.8 3.1 select_convert_fusion
  282.8 0.0 all-gather.6.cloned.1.call-update
  282.9 0.0 all-gather.10.cloned.1.call-start
  282.9 0.5 all-gather.10.cloned.1.call-update
  283.4 4.0 fusion.16
  287.4 29.1 %all-gather.6.cloned.1.call-done = bf16[256,8192]{1,0:T(8,128)(2,1)} async-done(((bf16[256,2048]{1,0:T(8,128)(2,1)}), bf16[256,8192]{1,0:T(8,128)(2,1)}) %all-gather.6.cloned.1.call-update) | async-done | bytes 4194320 | tf_op jit(solution)/shard_map/all_gather | solution.py:45
  316.6 562.9 %all-gather.10.cloned.1.call-done = bf16[1,2048,8192]{2,1,0:T(8,128)(2,1)} async-done(((bf16[1,2048,2048]{2,1,0:T(8,128)(2,1)}), bf16[1,2048,8192]{2,1,0:T(8,128)(2,1)}) %all-gather.10.cloned.1.call-update) | async-done | bytes 33554448 | tf_op jit(solution)/shard_map/all_gather | solution.py:48
  879.5 16.7 %fusion.7 = bf16[1,256,2048]{2,1,0:T(8,128)(2,1)} fusion(bf16[256,8192]{1,0:T(8,128)(2,1)} %all-gather.6.cloned.1.call-done, bf16[1,2048,8192]{2,1,0:T(8,128)(2,1)} %all-gather.10.cloned.1.call-done), kind=kOutput, calls=%fused_computation.10 | convolution fusion | flops 8590458880 | bytes 38797312 | tf_op jit(solution)/shard_map/dot_general | solution.py:46
  (8 shorter events, 0.0 us)
Async XLA Ops:
  7.2 154.8 %copy-start = (bf16[1,256,512]{2,1,0:T(8,128)(2,1)S(1)}, bf16[1,256,512]{2,1,0:T(8,128)(2,1)}, u32[]{:S(2)}) copy-start(bf16[1,256,512]{2,1,0:T(8,128)(2,1)} %param.9) | copy-start | bytes 786436
  7.2 154.8 %all-gather.8.cloned.1.call-start = ((), (), s32[]{:S(2)}) async-start(), calls=%async_computation.3 | async-start | bytes 10485760 | tf_op jit(solution)/shard_map/all_gather | solution.py:25
  7.9 233.1 %reduce-scatter.2.cloned.1.call-start = ((), (), s32[]{:S(2)}) async-start(), calls=%async_computation.1 | async-start | bytes 10485760 | tf_op jit(solution)/shard_map/reduce_scatter | solution.py:28
  170.9 70.1 %copy-start.4 = (f32[1,2048]{1,0:T(1,128)S(1)}, f32[1,2048]{1,0:T(1,128)}, u32[]{:S(2)}) copy-start(f32[1,2048]{1,0:T(1,128)} %param.8) | copy-start | bytes 24580
  170.9 78.4 %copy-start.3 = (bf16[256,2048]{1,0:T(8,128)(2,1)S(1)}, bf16[256,2048]{1,0:T(8,128)(2,1)}, u32[]{:S(2)}) copy-start(bf16[256,2048]{1,0:T(8,128)(2,1)} %param.12) | copy-start | bytes 3145732
  171.0 145.6 %all-gather.6.cloned.1.call-start = ((), (), s32[]{:S(2)}) async-start(), calls=%async_computation.2 | async-start | bytes 5242880 | tf_op jit(solution)/shard_map/all_gather | solution.py:45
  241.0 8.3 copy-start.2
  252.7 27.1 %collective-permute-start = (bf16[256,2048]{1,0:T(8,128)(2,1)}, bf16[256,2048]{1,0:T(8,128)(2,1)}, u32[]{:S(2)}, u32[]{:S(2)}) collective-permute-start(bf16[256,2048]{1,0:T(8,128)(2,1)} %add_convert_fusion.1), channel_id=1, source_target_pairs={{16,0},{17,1},{18,2},{19,3},{20,4},{21,5},{22,6},{23,7},{24,8},{25... | collective-permute-start | bytes 3145736 | tf_op jit(solution)/shard_map/ppermute | solution.py:15
  282.9 596.7 %all-gather.10.cloned.1.call-start = ((), (), s32[]{:S(2)}) async-start(), calls=%async_computation.4 | async-start | bytes 41943040 | tf_op jit(solution)/shard_map/all_gather | solution.py:48
  879.5 16.7 %copy-start.1 = (bf16[1,256,512]{2,1,0:T(8,128)(2,1)S(1)}, bf16[1,256,512]{2,1,0:T(8,128)(2,1)}, u32[]{:S(2)}) copy-start(bf16[1,256,512]{2,1,0:T(8,128)(2,1)} %param.9) | copy-start | bytes 786436
Sparse Core Ops, SparseCore 0:
  9.6 152.3 all-gather.7
  171.1 69.9 reduce-scatter.1
  283.0 33.5 all-gather.5
  318.1 561.3 all-gather.9
where the time goes:
time: 903 us
  waiting for transfers between devices  843 us (93%)
  matrix products  25.6 us (3%)
  between operations  13.8 us (2%)
  other arithmetic  13 us (1%)
    all_gather x1, waiting for transfers between devices, body(): lax.all_gather(out_weight[0], 'seq', axis=1, tiled=True)  563 us
    all_gather x1, waiting for transfers between devices, body(): lax.all_gather(kv_weight[0], 'seq', axis=1, tiled=True)  154 us
    reduce_scatter x1, waiting for transfers between devices, body(): kv_share = lax.psum_scatter(kv_terms, 'tp', scatter_dimension=1, tiled=True)  70 us
    all_gather x1, waiting for transfers between devices, body(): grad_full = lax.all_gather(grad_cast, 'tp', axis=1, tiled=True)  29.1 us
    ppermute x1, waiting for transfers between devices, from_behind(): return lax.ppermute(block, axis, route)  25.8 us
  transfers between devices with their start and end apart: 5, of which 5 were waited for; matrix products, arithmetic and copies ran while one was open for 0% of the time, Pallas kernels for 0%

commit v1 on v0

v1 whole, which is shorter than its diff:
```python
import jax
import jax.numpy as jnp
from jax import lax
from jax.experimental import pallas as pl
from jax.experimental.pallas import tpu as pltpu
from jax.sharding import PartitionSpec as P

D = 8192


epsilon = 1e-05
CORES = 2
CHUNKS = 2


def from_behind(block, axis, distance):
    devices = range(lax.axis_size(axis))
    route = [(i - distance, i) for i in devices if i - distance in devices]
    return lax.ppermute(block, axis, route)


def sizes():
    seq, tp = lax.axis_size("seq"), lax.axis_size("tp")
    assert seq % tp == 0 and tp % CORES == 0
    return seq, tp, seq // tp


def over_rows(block, turn):
    tp = lax.axis_size("tp")
    return lax.ppermute(block, "tp", [(t, (t + turn * CORES) % tp) for t in range(tp)])


def over_cores(block):
    tp = lax.axis_size("tp")
    return lax.ppermute(block, "tp", [(t, t ^ 1) for t in range(tp)])


def exchange(block, axis):
    return lax.all_to_all(block, axis, 0, 0)


def to_slabs(block):
    seq, tp, ratio = sizes()
    tokens, width = block.shape
    parts = exchange(block.reshape(tp, tokens // tp, width), "tp")
    if ratio > 1:
        parts = parts.reshape(tp, tokens // tp, ratio, width // ratio).transpose(0, 2, 1, 3)
    return exchange(parts.reshape(seq, tokens // tp, width // ratio), "seq")


def from_slabs(block):
    seq, tp, ratio = sizes()
    _, tokens, width = block.shape
    parts = exchange(block, "seq")
    if ratio > 1:
        parts = parts.reshape(tp, ratio, tokens, width).transpose(0, 2, 1, 3)
    return exchange(parts.reshape(tp, tokens, width * ratio), "tp")


def gain_slab(gain):
    seq, tp, ratio = sizes()
    place, lane = lax.axis_index("seq"), lax.axis_index("tp")
    width = gain.shape[1] // ratio
    own = lax.dynamic_slice_in_dim(gain, place % ratio * width, width, 1)
    route = []
    for q in range(seq):
        for t in range(tp):
            to = (t * ratio + q % ratio, q // ratio)
            if to != (q, t):
                route.append((q * tp + t, to[0] * tp + to[1]))
    moved = lax.ppermute(own, ("seq", "tp"), route)
    stays = (place == lane * ratio + place % ratio) & (lane == place // ratio)
    return jnp.where(stays, own, moved)


def gather_seq(block):
    seq = lax.axis_size("seq")
    place = lax.axis_index("seq")
    arrived = [block]
    for turn in range(1, seq):
        route = [(q, (q + turn) % seq) for q in range(seq)]
        arrived.append(lax.ppermute(block, "seq", route))
    return jnp.stack([lax.select_n((place - q) % seq, *arrived) for q in range(seq)], axis=0)


def norm_backward(values, gain, kv_share, axes):
    squares, intersection = lax.psum(
        (jnp.sum(values * values, axis=-1), jnp.sum(gain * kv_share * values, axis=-1)), axes
    )
    inv_rms = lax.rsqrt(squares / D + epsilon)[..., None]
    return (
        inv_rms * gain * kv_share
        - values * (inv_rms * inv_rms * inv_rms) * intersection[..., None] / D
    )


def product_kernel(*refs):
    *pieces, weight, out, rows = refs
    seq, depth, width = pieces[0].shape

    @pl.when(pl.program_id(0) == 0)
    def _():
        for i, piece in enumerate(pieces):
            rows[i] = piece[...]

    terms = lax.dot_general(
        rows[...].reshape(-1, width),
        weight[...],
        (((1,), (1,)), ((), ())),
        preferred_element_type=jnp.float32,
    )
    for i in range(len(pieces)):
        for q in range(seq):
            start = (i * seq + q) * depth
            out[q, i] = terms[start : start + depth]


def product(pieces, weight):
    seq, depth, width = pieces[0].shape
    heads = weight.shape[0]
    block = min(512, heads)
    n = len(pieces)
    return pl.pallas_call(
        product_kernel,
        out_shape=jax.ShapeDtypeStruct((seq, n, depth, heads), jnp.float32),
        grid=(heads // block,),
        in_specs=[pl.BlockSpec((seq, depth, width), lambda i: (0, 0, 0)) for _ in pieces]
        + [pl.BlockSpec((block, width), lambda i: (i, 0))],
        out_specs=pl.BlockSpec((seq, n, depth, block), lambda i: (0, 0, 0, i)),
        scratch_shapes=[pltpu.VMEM((n, seq, depth, width), pieces[0].dtype)],
        compiler_params=pltpu.CompilerParams(
            dimension_semantics=("arbitrary",), vmem_limit_bytes=40 * 1024 * 1024
        ),
    )(*pieces, weight)


def body(layer_input, norm_gain, kv_cotangent, kv_weight, mlp_grads, output_cotangent, out_weight):
    seq, tp, ratio = sizes()
    row = tp // CORES
    upstream = lax.axis_index("section") == 0
    place, lane = lax.axis_index("seq"), lax.axis_index("tp")
    here, core = lane // CORES, lane % CORES
    tokens = kv_cotangent.shape[1]

    mixed = kv_cotangent[0].reshape(row, CORES, tokens // tp, -1)
    kept = lax.dynamic_index_in_dim(mixed, core, 1, keepdims=False)
    given = lax.dynamic_index_in_dim(mixed, 1 - core, 1, keepdims=False)
    cotangent = gather_seq(jnp.concatenate([kept, over_cores(given)], axis=2))
    weights = jnp.concatenate([kv_weight[0], over_cores(kv_weight[0])], axis=0)

    values = to_slabs(layer_input[0])
    branch = mlp_grads[0].astype(jnp.float32)
    grad_one = output_cotangent.astype(jnp.float32) + branch
    base_home = jnp.where(upstream, mlp_grads[0], grad_one.astype(jnp.bfloat16))
    base = to_slabs(base_home)
    gain = gain_slab(norm_gain)
    width = gain.shape[1]

    def kv_of(turn):
        part = lax.dynamic_index_in_dim(cotangent, (here + turn) % row, 1, keepdims=False)
        terms = jnp.dot(
            part.reshape(-1, part.shape[-1]), weights, preferred_element_type=jnp.float32
        )
        return terms.reshape(seq, tokens // tp, width)

    given = [over_rows(kv_of(turn).astype(jnp.bfloat16), turn) for turn in range(1, row)]
    kv_share = kv_of(0)
    for terms in given:
        kv_share = kv_share + terms.astype(jnp.float32)

    norm_back = norm_backward(values.astype(jnp.float32), gain, kv_share, "seq")
    input_one = (base.astype(jnp.float32) + norm_back).astype(jnp.bfloat16)

    depth = tokens // tp // CHUNKS

    def cut(array, c):
        return array[:, c * depth : (c + 1) * depth]

    arrivals = [from_behind(cut(input_one, c), "section", -1) for c in range(CHUNKS)]
    home = from_slabs(norm_back.astype(jnp.bfloat16))
    blocks_of = []
    for c in range(CHUNKS):
        part = cut(base, c)
        arriving = arrivals[c]
        if c > 0:
            arriving, blocks[-1] = lax.optimization_barrier((arriving, blocks[-1]))
        grad_zero = arriving.astype(jnp.float32) + part.astype(jnp.float32)
        grad = jnp.where(upstream, grad_zero.astype(jnp.bfloat16), part)
        blocks = [over_rows(grad, turn) if turn else grad for turn in range(row)]
        blocks_of.append(blocks)
    attn_parts = []
    for c, blocks in enumerate(blocks_of):
        pieces = [half for block in blocks for half in (block, over_cores(block))]
        terms = product(pieces, out_weight[0])
        total = None
        for step in range(1, seq + 1):
            mine = lax.dynamic_index_in_dim(terms, (place - step) % seq, 0, keepdims=False)
            if total is not None:
                mine = mine + total.astype(jnp.float32)
            mine = mine.astype(jnp.bfloat16)
            if step < seq:
                total = lax.ppermute(mine, "seq", [(q, (q + 1) % seq) for q in range(seq)])
        attn_parts.append(mine)
    attn_part = jnp.concatenate(attn_parts, axis=1)
    order = []
    for t in range(tp):
        which = (here - t // CORES) % row * CORES + (lane + t) % CORES
        order.append(lax.dynamic_index_in_dim(attn_part, which, 0, keepdims=False))
    attn_part = jnp.concatenate(order, axis=0)

    home = home.reshape(tokens, -1).astype(jnp.float32)
    own = (grad_one + home).astype(jnp.bfloat16)
    arrived = from_behind(own, "section", -1)
    input_zero = (arrived.astype(jnp.float32) + branch + home).astype(jnp.bfloat16)
    input_part = jnp.where(upstream, input_zero, own)
    return (attn_part[None], input_part[None])


def solution(mesh):
    in_specs = (
        P("section", "seq", "tp"),
        P("section", "tp"),
        P("section", "seq", "tp"),
        P("section", "tp", "seq"),
        P("section", "seq", "tp"),
        P("seq", "tp"),
        P("section", "tp", "seq"),
    )
    out_specs = (P("section", "seq", "tp"), P("section", "seq", "tp"))
    return jax.shard_map(body, mesh=mesh, in_specs=in_specs, out_specs=out_specs, check_vma=False)
```

time: 903 us -> 273 us (0.30)
  waiting for transfers between devices: 843 us -> 153 us
  starting transfers between devices: 1.44 us -> 48.5 us
  matrix products: 25.6 us -> 9.08 us
  Pallas kernels: 0 us -> 15.1 us
  between operations: 13.8 us -> 1.01 us
  other arithmetic: 13 us -> 23.5 us
  blocking collectives: 5.76 us -> 14.9 us
    all_gather x3 -> x0, waiting for transfers between devices: 746 us -> none  [the longest x1 563 us: body(): lax.all_gather(out_weight[0], 'seq', axis=1, tiled=True)]
    ppermute x0 -> x19, waiting for transfers between devices: none -> 108 us  [the longest x6 42.8 us: body(): total = lax.ppermute(mine, 'seq', [(q, (q + 1) % seq) for q in range(seq)])]
    reduce_scatter x1 -> x0, waiting for transfers between devices: 70 us -> none  [body(): kv_share = lax.psum_scatter(kv_terms, 'tp', scatter_dimension=1, tiled=True)]
    all_to_all x0 -> x6, starting transfers between devices: none -> 30.1 us  [exchange(): return lax.all_to_all(block, axis, 0, 0)]
    all_to_all x0 -> x6, waiting for transfers between devices: none -> 28.2 us  [exchange(): return lax.all_to_all(block, axis, 0, 0)]
    dot_general x2, matrix products: 25.6 us -> 9.08 us  [kv_of(): jnp.dot(part.reshape(-1, part.shape[-1]), weights, preferred_element_type...]
    pallas_call x0 -> x2, Pallas kernels: none -> 15.1 us  [product(): pl.pallas_call(product_kernel, out_shape=jax.ShapeDtypeStruct((seq, n, de...]
    ppermute x0 -> x19, starting transfers between devices: none -> 14.5 us  [the longest x3 5.9 us: gather_seq(): arrived.append(lax.ppermute(block, 'seq', route))]
  transfers between devices with their start and end apart: 5 -> 28, of which waited for: 5 -> 16; matrix products, arithmetic and copies ran while one was open for 0% -> 10% of each run, Pallas kernels for 0% -> 6%
where the time goes in v1:
time: 273 us; the launch traced here: 272 us
  waiting for transfers between devices  153 us (56%)
  starting transfers between devices  48.5 us (18%)
  other arithmetic  23.5 us (9%)
  Pallas kernels  15.1 us (6%)
  blocking collectives  14.9 us (5%)
  matrix products  9.08 us (3%)
  local copies, waits for them, and re-layouts  6.24 us (2%)
    ppermute x6, waiting for transfers between devices, body(): total = lax.ppermute(mine, 'seq', [(q, (q + 1) % seq) for q in range(seq)])  42.8 us
    ppermute x3, waiting for transfers between devices, gather_seq(): arrived.append(lax.ppermute(block, 'seq', route))  37.5 us
    all_to_all x6, starting transfers between devices, exchange(): return lax.all_to_all(block, axis, 0, 0)  30.1 us
    all_to_all x6, waiting for transfers between devices, exchange(): return lax.all_to_all(block, axis, 0, 0)  28.2 us
    ppermute x3, waiting for transfers between devices, over_rows(): lax.ppermute(block, 'tp', [(t, (t + turn * CORES) % tp) for t in range(tp)])  27.7 us
    ppermute x3, waiting for transfers between devices, from_behind(): return lax.ppermute(block, axis, route)  17.1 us
    pallas_call x2, Pallas kernels, product(): pl.pallas_call(product_kernel, out_shape=jax.ShapeDtypeStruct((seq, n, de...  15.1 us
    psum x1, blocking collectives, norm_backward(): lax.psum((jnp.sum(values * values, axis=-1), jnp.sum(gain * kv_share * va...  14.9 us
  transfers between devices with their start and end apart: 28, of which 16 were waited for; matrix products, arithmetic and copies ran while one was open for 10% of the time, Pallas kernels for 6%

profile of v1, /device:TPU:0, one launch (start us, length us, event | category | flops | bytes accessed | tf_op | source)
XLA Modules:
  0.0 271.6 jit_solution(10715247575708367518)
XLA Ops:
  0.7 4.4 %all-to-all-start.2 = ((bf16[4,64,2048]{2,1,0:T(8,128)(2,1)}), bf16[4,64,2048]{2,1,0:T(8,128)(2,1)}, u32[]{:S(2)}, u32[]{:S(2)}) async-start(bf16[4,64,2048]{2,1,0:T(8,128)(2,1)} %bitcast.96), calls=%async_computation.2 | async-start | bytes 2097152 | tf_op jit(solution)/shard_map/all_to_all | solution.py:39
  6.9 13.3 %all-to-all-done.2 = bf16[4,64,2048]{2,1,0:T(8,128)(2,1)} async-done(((bf16[4,64,2048]{2,1,0:T(8,128)(2,1)}), bf16[4,64,2048]{2,1,0:T(8,128)(2,1)}, u32[]{:S(2)}, u32[]{:S(2)}) %all-to-all-start.2) | async-done | bytes 1048608 | tf_op jit(solution)/shard_map/all_to_all | solution.py:39
  20.2 4.3 %all-to-all-start = ((bf16[4,64,2048]{2,1,0:T(8,128)(2,1)}), bf16[4,64,2048]{2,1,0:T(8,128)(2,1)}, u32[]{:S(2)}, u32[]{:S(2)}) async-start(bf16[4,64,2048]{2,1,0:T(8,128)(2,1)} %bitcast.1), calls=%async_computation | async-start | bytes 2097152 | tf_op jit(solution)/shard_map/all_to_all | solution.py:39
  25.0 14.0 %all-to-all-done = bf16[4,64,2048]{2,1,0:T(8,128)(2,1)} async-done(((bf16[4,64,2048]{2,1,0:T(8,128)(2,1)}), bf16[4,64,2048]{2,1,0:T(8,128)(2,1)}, u32[]{:S(2)}, u32[]{:S(2)}) %all-to-all-start) | async-done | bytes 1048608 | tf_op jit(solution)/shard_map/all_to_all | solution.py:39
  39.0 5.7 %all-to-all-start.3 = ((bf16[4,64,2048]{2,1,0:T(8,128)(2,1)}), bf16[4,64,2048]{2,1,0:T(8,128)(2,1)S(1)}, u32[]{:S(2)}, u32[]{:S(2)}) async-start(bf16[4,64,2048]{2,1,0:T(8,128)(2,1)} %all-to-all-done.2), calls=%async_computation.3 | async-start | bytes 2097152 | tf_op jit(solution)/shard_map/all_to_all | solution.py:39
  50.6 22.3 %collective-permute-done.2 = bf16[2,64,1024]{2,1,0:T(8,128)(2,1)S(1)} collective-permute-done((bf16[2,64,1024]{2,1,0:T(8,128)(2,1)S(1)}, bf16[2,64,1024]{2,1,0:T(8,128)(2,1)S(1)}, u32[]{:S(2)}, u32[]{:S(2)}) %collective-permute-start.2) | collective-permute-done | bytes 262176 | tf_op jit(solution)/shard_map/ppermute | solution.py:82
  72.9 15.2 %collective-permute-done.3 = bf16[2,64,1024]{2,1,0:T(8,128)(2,1)S(1)} collective-permute-done((bf16[2,64,1024]{2,1,0:T(8,128)(2,1)S(1)}, bf16[2,64,1024]{2,1,0:T(8,128)(2,1)S(1)}, u32[]{:S(2)}, u32[]{:S(2)}) %collective-permute-start.3) | collective-permute-done | bytes 262176 | tf_op jit(solution)/shard_map/ppermute | solution.py:82
  89.9 3.8 %fusion.3 = bf16[4,64,2048]{2,1,0:T(8,128)(2,1)} fusion(bf16[512,2048]{1,0:T(8,128)(2,1)} %collective-permute-done.5, bf16[512,2048]{1,0:T(8,128)(2,1)S(1)} %bitcast.102, bf16[4,2,64,1024]{3,2,0,1:T(8,128)(2,1)S(1)} %pad_maximum_fusion, s32[]{:T(128)S(6)} %select_n.319), kind=kOutput, calls=%fused_computation.11 | convolution fusion | flops 1082654720 | bytes 5767172 | tf_op jit(solution)/shard_map/dot_general | solution.py:161
  94.3 7.3 %all-to-all-start.1 = ((bf16[4,64,2048]{2,1,0:T(8,128)(2,1)}), bf16[4,64,2048]{2,1,0:T(8,128)(2,1)S(1)}, u32[]{:S(2)}, u32[]{:S(2)}) async-start(bf16[4,64,2048]{2,1,0:T(8,128)(2,1)} %all-to-all-done), calls=%async_computation.1 | async-start | bytes 2097152 | tf_op jit(solution)/shard_map/all_to_all | solution.py:39
  102.3 14.7 %collective-permute-done.6 = bf16[4,64,2048]{2,1,0:T(8,128)(2,1)} collective-permute-done((bf16[4,64,2048]{2,1,0:T(8,128)(2,1)}, bf16[4,64,2048]{2,1,0:T(8,128)(2,1)}, u32[]{:S(2)}, u32[]{:S(2)}) %collective-permute-start.6) | collective-permute-done | bytes 1048608 | tf_op jit(solution)/shard_map/ppermute | solution.py:30
  117.1 5.2 %fusion.6 = (f32[4,64]{1,0:T(4,128)S(1)}, f32[4,64]{1,0:T(4,128)S(1)}, f32[4,64,2048]{2,1,0:T(8,128)}) fusion(bf16[4,64,2048]{2,1,0:T(8,128)(2,1)S(1)} %all-to-all-done.3, f32[2048]{0:T(1024)S(1)} %bitcast.98, bf16[4,64,2048]{2,1,0:T(8,128)(2,1)} %collective-permute-done.6, bf16[512,2048]{1,0:T(8,128)(2,1)} %collective-permute-done.5, ...), kind=kOutput, calls=%fused_computation.14 | convolution fusion | flops 1086324224 | bytes 8923140 | tf_op jit(solution)/shard_map/dot_general | solution.py:161
  122.3 14.9 %all-reduce = (f32[4,64]{1,0:T(4,128)S(1)}, f32[4,64]{1,0:T(4,128)S(1)}) all-reduce(f32[4,64]{1,0:T(4,128)S(1)} %get-tuple-element.7, f32[4,64]{1,0:T(4,128)S(1)} %get-tuple-element.6), channel_id=1, replica_groups=mesh['section'=2,'seq'=4,'tp'=4] {'seq'}, use_global_device_ids=true, to_apply=%region_3.4 | all-reduce | flops 512 | bytes 4096 | tf_op jit(solution)/shard_map/psum | solution.py:87
  143.3 14.0 %collective-permute-done.7 = bf16[4,32,2048]{2,1,0:T(8,128)(2,1)S(1)} collective-permute-done((bf16[4,32,2048]{2,1,0:T(8,128)(2,1)S(1)}, bf16[4,32,2048]{2,1,0:T(8,128)(2,1)S(1)}, u32[]{:S(2)}, u32[]{:S(2)}) %collective-permute-start.7) | collective-permute-done | bytes 524320 | tf_op jit(solution)/shard_map/ppermute | solution.py:19
  157.4 3.5 %collective-permute-start.10 = (bf16[4,32,2048]{2,1,0:T(8,128)(2,1)S(1)}, bf16[4,32,2048]{2,1,0:T(8,128)(2,1)S(1)}, u32[]{:S(2)}, u32[]{:S(2)}) collective-permute-start(bf16[4,32,2048]{2,1,0:T(8,128)(2,1)S(1)} %fusion.22.refs_0_), channel_id=1, source_target_pairs={{0,2},{1,3},{2,0},{3,1},{4,6},{5,7},{6,4},{7,5},{8,10},{9,11},{10,... | collective-permute-start | bytes 1572872 | tf_op jit(solution)/shard_map/ppermute | solution.py:30
  160.9 4.2 %all-to-all-start.4 = ((bf16[4,64,2048]{2,1,0:T(8,128)(2,1)}), bf16[4,64,2048]{2,1,0:T(8,128)(2,1)}, u32[]{:S(2)}, u32[]{:S(2)}) async-start(bf16[4,64,2048]{2,1,0:T(8,128)(2,1)} %get-tuple-element.10), calls=%async_computation.4 | async-start | bytes 2097152 | tf_op jit(solution)/shard_map/all_to_all | solution.py:39
  171.9 10.3 %collective-permute-done.16.refs_2_ = bf16[4,32,2048]{2,1,0:T(8,128)(2,1)S(1)} collective-permute-done((bf16[4,32,2048]{2,1,0:T(8,128)(2,1)S(1)}, bf16[4,32,2048]{2,1,0:T(8,128)(2,1)S(1)}, u32[]{:S(2)}, u32[]{:S(2)}) %collective-permute-start.16) | collective-permute-done | bytes 524320 | tf_op jit(solution)/shard_map/ppermute | solution.py:30
  182.3 7.7 %shard_map.86 = f32[4,4,32,2048]{3,2,1,0:T(8,128)S(1)} custom-call(bf16[4,32,2048]{2,1,0:T(8,128)(2,1)S(1)} %fusion.22.refs_0_, bf16[4,32,2048]{2,1,0:T(8,128)(2,1)} %collective-permute-done.8.refs_1_, bf16[4,32,2048]{2,1,0:T(8,128)(2,1)S(1)} %collective-permute-done.10.refs_2_, bf16[4,32,2048]{2,1,0:T(8,128)(2,1)} %collective-permute-done.11.refs_3_, ...), custom_call_target="tpu_custom_call" | custom-call | tf_op jit(solution)/shard_map/pallas_call | solution.py:123
  193.2 4.3 %all-to-all-start.5 = ((bf16[4,64,2048]{2,1,0:T(8,128)(2,1)}), bf16[4,64,2048]{2,1,0:T(8,128)(2,1)}, u32[]{:S(2)}, u32[]{:S(2)}) async-start(bf16[4,64,2048]{2,1,0:T(8,128)(2,1)} %all-to-all-done.4), calls=%async_computation.5 | async-start | bytes 2097152 | tf_op jit(solution)/shard_map/all_to_all | solution.py:39
  197.6 7.4 %shard_map.87 = f32[4,4,32,2048]{3,2,1,0:T(8,128)S(1)} custom-call(bf16[4,32,2048]{2,1,0:T(8,128)(2,1)S(1)} %fusion.23.refs_0_, bf16[4,32,2048]{2,1,0:T(8,128)(2,1)S(1)} %collective-permute-done.15.refs_1_, bf16[4,32,2048]{2,1,0:T(8,128)(2,1)S(1)} %collective-permute-done.16.refs_2_, bf16[4,32,2048]{2,1,0:T(8,128)(2,1)S(1)} %collective-permute-done.17.refs_3_, ...), custom_call_target="tpu_custom_call" | custom-call | tf_op jit(solution)/shard_map/pallas_call | solution.py:123
  216.1 8.7 %collective-permute-done.18 = bf16[4,32,2048]{2,1,0:T(8,128)(2,1)} collective-permute-done((bf16[4,32,2048]{2,1,0:T(8,128)(2,1)}, bf16[4,32,2048]{2,1,0:T(8,128)(2,1)}, u32[]{:S(2)}, u32[]{:S(2)}) %collective-permute-start.18) | collective-permute-done | bytes 524320 | tf_op jit(solution)/shard_map/ppermute | solution.py:202
  227.0 8.9 %collective-permute-done.13 = bf16[4,32,2048]{2,1,0:T(8,128)(2,1)} collective-permute-done((bf16[4,32,2048]{2,1,0:T(8,128)(2,1)}, bf16[4,32,2048]{2,1,0:T(8,128)(2,1)}, u32[]{:S(2)}, u32[]{:S(2)}) %collective-permute-start.13) | collective-permute-done | bytes 524320 | tf_op jit(solution)/shard_map/ppermute | solution.py:202
  238.2 8.9 %collective-permute-done.19 = bf16[4,32,2048]{2,1,0:T(8,128)(2,1)} collective-permute-done((bf16[4,32,2048]{2,1,0:T(8,128)(2,1)}, bf16[4,32,2048]{2,1,0:T(8,128)(2,1)}, u32[]{:S(2)}, u32[]{:S(2)}) %collective-permute-start.19) | collective-permute-done | bytes 524320 | tf_op jit(solution)/shard_map/ppermute | solution.py:202
  248.7 9.7 %collective-permute-done.14 = bf16[4,32,2048]{2,1,0:T(8,128)(2,1)} collective-permute-done((bf16[4,32,2048]{2,1,0:T(8,128)(2,1)}, bf16[4,32,2048]{2,1,0:T(8,128)(2,1)}, u32[]{:S(2)}, u32[]{:S(2)}) %collective-permute-start.14) | collective-permute-done | bytes 524320 | tf_op jit(solution)/shard_map/ppermute | solution.py:202
  262.9 6.2 %collective-permute-done.20 = bf16[4,32,2048]{2,1,0:T(8,128)(2,1)S(1)} collective-permute-done((bf16[4,32,2048]{2,1,0:T(8,128)(2,1)S(1)}, bf16[4,32,2048]{2,1,0:T(8,128)(2,1)S(1)}, u32[]{:S(2)}, u32[]{:S(2)}) %collective-permute-start.20) | collective-permute-done | bytes 524320 | tf_op jit(solution)/shard_map/ppermute | solution.py:202
  (79 shorter events, 51.7 us)
Async XLA Ops:
  0.7 19.6 %all-to-all-start.2 = ((bf16[4,64,2048]{2,1,0:T(8,128)(2,1)}), bf16[4,64,2048]{2,1,0:T(8,128)(2,1)}, u32[]{:S(2)}, u32[]{:S(2)}) async-start(bf16[4,64,2048]{2,1,0:T(8,128)(2,1)} %bitcast.96), calls=%async_computation.2 | async-start | bytes 2097152 | tf_op jit(solution)/shard_map/all_to_all | solution.py:39
  5.0 83.7 %collective-permute-start.5 = (bf16[512,2048]{1,0:T(8,128)(2,1)}, bf16[512,2048]{1,0:T(8,128)(2,1)}, u32[]{:S(2)}, u32[]{:S(2)}) collective-permute-start(bf16[512,2048]{1,0:T(8,128)(2,1)} %bitcast.100), channel_id=1, source_target_pairs={{0,1},{1,0},{2,3},{3,2},{4,5},{5,4},{6,7},{7,6},{8,9},{9,8},{10,11... | collective-permute-start | bytes 6291464 | tf_op jit(solution)/shard_map/ppermute | solution.py:35
  20.2 18.8 %all-to-all-start = ((bf16[4,64,2048]{2,1,0:T(8,128)(2,1)}), bf16[4,64,2048]{2,1,0:T(8,128)(2,1)}, u32[]{:S(2)}, u32[]{:S(2)}) async-start(bf16[4,64,2048]{2,1,0:T(8,128)(2,1)} %bitcast.1), calls=%async_computation | async-start | bytes 2097152 | tf_op jit(solution)/shard_map/all_to_all | solution.py:39
  24.5 20.1 %collective-permute-start.1 = (bf16[2,64,512]{2,1,0:T(8,128)(2,1)S(1)}, bf16[2,64,512]{2,1,0:T(8,128)(2,1)S(1)}, u32[]{:S(2)}, u32[]{:S(2)}) collective-permute-start(bf16[2,64,512]{2,1,0:T(8,128)(2,1)S(1)} %get-tuple-element.22), channel_id=1, source_target_pairs={{0,1},{1,0},{2,3},{3,2},{4,5},{5,4},{6,7},{7,6},{8,9},{9,8},{10,11... | collective-permute-start | bytes 393224 | tf_op jit(solution)/shard_map/ppermute | solution.py:35
  39.0 55.3 %all-to-all-start.3 = ((bf16[4,64,2048]{2,1,0:T(8,128)(2,1)}), bf16[4,64,2048]{2,1,0:T(8,128)(2,1)S(1)}, u32[]{:S(2)}, u32[]{:S(2)}) async-start(bf16[4,64,2048]{2,1,0:T(8,128)(2,1)} %all-to-all-done.2), calls=%async_computation.3 | async-start | bytes 2097152 | tf_op jit(solution)/shard_map/all_to_all | solution.py:39
  44.7 28.2 %collective-permute-start.2 = (bf16[2,64,1024]{2,1,0:T(8,128)(2,1)S(1)}, bf16[2,64,1024]{2,1,0:T(8,128)(2,1)S(1)}, u32[]{:S(2)}, u32[]{:S(2)}) collective-permute-start(bf16[2,64,1024]{2,1,0:T(8,128)(2,1)S(1)} %pad_maximum_fusion.1), channel_id=1, source_target_pairs={{0,4},{4,8},{8,12},{12,0},{1,5},{5,9},{9,13},{13,1},{2,6},{6,10},{... | collective-permute-start | bytes 786440 | tf_op jit(solution)/shard_map/ppermute | solution.py:82
  46.8 41.3 %collective-permute-start.3 = (bf16[2,64,1024]{2,1,0:T(8,128)(2,1)S(1)}, bf16[2,64,1024]{2,1,0:T(8,128)(2,1)S(1)}, u32[]{:S(2)}, u32[]{:S(2)}) collective-permute-start(bf16[2,64,1024]{2,1,0:T(8,128)(2,1)S(1)} %pad_maximum_fusion.1), channel_id=1, source_target_pairs={{0,8},{4,12},{8,0},{12,4},{1,9},{5,13},{9,1},{13,5},{2,10},{6,14},... | collective-permute-start | bytes 786440 | tf_op jit(solution)/shard_map/ppermute | solution.py:82
  49.1 39.0 %collective-permute-start.4 = (bf16[2,64,1024]{2,1,0:T(8,128)(2,1)S(1)}, bf16[2,64,1024]{2,1,0:T(8,128)(2,1)S(1)}, u32[]{:S(2)}, u32[]{:S(2)}) collective-permute-start(bf16[2,64,1024]{2,1,0:T(8,128)(2,1)S(1)} %pad_maximum_fusion.1), channel_id=1, source_target_pairs={{0,12},{4,0},{8,4},{12,8},{1,13},{5,1},{9,5},{13,9},{2,14},{6,2},{... | collective-permute-start | bytes 786440 | tf_op jit(solution)/shard_map/ppermute | solution.py:82
  93.7 23.4 %collective-permute-start.6 = (bf16[4,64,2048]{2,1,0:T(8,128)(2,1)}, bf16[4,64,2048]{2,1,0:T(8,128)(2,1)}, u32[]{:S(2)}, u32[]{:S(2)}) collective-permute-start(bf16[4,64,2048]{2,1,0:T(8,128)(2,1)} %fusion.3), channel_id=1, source_target_pairs={{0,2},{1,3},{2,0},{3,1},{4,6},{5,7},{6,4},{7,5},{8,10},{9,11},{10,... | collective-permute-start | bytes 3145736 | tf_op jit(solution)/shard_map/ppermute | solution.py:30
  94.3 42.9 %all-to-all-start.1 = ((bf16[4,64,2048]{2,1,0:T(8,128)(2,1)}), bf16[4,64,2048]{2,1,0:T(8,128)(2,1)S(1)}, u32[]{:S(2)}, u32[]{:S(2)}) async-start(bf16[4,64,2048]{2,1,0:T(8,128)(2,1)} %all-to-all-done), calls=%async_computation.1 | async-start | bytes 2097152 | tf_op jit(solution)/shard_map/all_to_all | solution.py:39
  140.7 16.6 %collective-permute-start.7 = (bf16[4,32,2048]{2,1,0:T(8,128)(2,1)S(1)}, bf16[4,32,2048]{2,1,0:T(8,128)(2,1)S(1)}, u32[]{:S(2)}, u32[]{:S(2)}) collective-permute-start(bf16[4,32,2048]{2,1,0:T(8,128)(2,1)S(1)} %get-tuple-element.17), channel_id=1, source_target_pairs={{16,0},{17,1},{18,2},{19,3},{20,4},{21,5},{22,6},{23,7},{24,8},{25... | collective-permute-start | bytes 1572872 | tf_op jit(solution)/shard_map/ppermute | solution.py:19
  142.0 26.3 %collective-permute-start.9 = (bf16[4,32,2048]{2,1,0:T(8,128)(2,1)S(1)}, bf16[4,32,2048]{2,1,0:T(8,128)(2,1)S(1)}, u32[]{:S(2)}, u32[]{:S(2)}) collective-permute-start(bf16[4,32,2048]{2,1,0:T(8,128)(2,1)S(1)} %get-tuple-element.16), channel_id=1, source_target_pairs={{16,0},{17,1},{18,2},{19,3},{20,4},{21,5},{22,6},{23,7},{24,8},{25... | collective-permute-start | bytes 1572872 | tf_op jit(solution)/shard_map/ppermute | solution.py:19
  157.4 13.5 %collective-permute-start.10 = (bf16[4,32,2048]{2,1,0:T(8,128)(2,1)S(1)}, bf16[4,32,2048]{2,1,0:T(8,128)(2,1)S(1)}, u32[]{:S(2)}, u32[]{:S(2)}) collective-permute-start(bf16[4,32,2048]{2,1,0:T(8,128)(2,1)S(1)} %fusion.22.refs_0_), channel_id=1, source_target_pairs={{0,2},{1,3},{2,0},{3,1},{4,6},{5,7},{6,4},{7,5},{8,10},{9,11},{10,... | collective-permute-start | bytes 1572872 | tf_op jit(solution)/shard_map/ppermute | solution.py:30
  160.9 32.4 %all-to-all-start.4 = ((bf16[4,64,2048]{2,1,0:T(8,128)(2,1)}), bf16[4,64,2048]{2,1,0:T(8,128)(2,1)}, u32[]{:S(2)}, u32[]{:S(2)}) async-start(bf16[4,64,2048]{2,1,0:T(8,128)(2,1)} %get-tuple-element.10), calls=%async_computation.4 | async-start | bytes 2097152 | tf_op jit(solution)/shard_map/all_to_all | solution.py:39
  171.9 25.6 %collective-permute-start.15 = (bf16[4,32,2048]{2,1,0:T(8,128)(2,1)S(1)}, bf16[4,32,2048]{2,1,0:T(8,128)(2,1)S(1)}, u32[]{:S(2)}, u32[]{:S(2)}) collective-permute-start(bf16[4,32,2048]{2,1,0:T(8,128)(2,1)S(1)} %fusion.23.refs_0_), channel_id=1, source_target_pairs={{0,1},{1,0},{2,3},{3,2},{4,5},{5,4},{6,7},{7,6},{8,9},{9,8},{10,11... | collective-permute-start | bytes 1572872 | tf_op jit(solution)/shard_map/ppermute | solution.py:35
  182.2 15.3 %collective-permute-start.17 = (bf16[4,32,2048]{2,1,0:T(8,128)(2,1)S(1)}, bf16[4,32,2048]{2,1,0:T(8,128)(2,1)S(1)}, u32[]{:S(2)}, u32[]{:S(2)}) collective-permute-start(bf16[4,32,2048]{2,1,0:T(8,128)(2,1)S(1)} %collective-permute-done.16.refs_2_), channel_id=1, source_target_pairs={{0,1},{1,0},{2,3},{3,2},{4,5},{5,4},{6,7},{7,6},{8,9},{9,8},{10,11... | collective-permute-start | bytes 1572872 | tf_op jit(solution)/shard_map/ppermute | solution.py:35
  192.1 16.2 %collective-permute-start.12 = (bf16[4,32,2048]{2,1,0:T(8,128)(2,1)S(1)}, bf16[4,32,2048]{2,1,0:T(8,128)(2,1)S(1)}, u32[]{:S(2)}, u32[]{:S(2)}) collective-permute-start(bf16[4,32,2048]{2,1,0:T(8,128)(2,1)S(1)} %fusion.24), channel_id=1, source_target_pairs={{0,4},{4,8},{8,12},{12,0},{1,5},{5,9},{9,13},{13,1},{2,6},{6,10},{... | collective-permute-start | bytes 1572872 | tf_op jit(solution)/shard_map/ppermute | solution.py:202
  193.2 18.8 %all-to-all-start.5 = ((bf16[4,64,2048]{2,1,0:T(8,128)(2,1)}), bf16[4,64,2048]{2,1,0:T(8,128)(2,1)}, u32[]{:S(2)}, u32[]{:S(2)}) async-start(bf16[4,64,2048]{2,1,0:T(8,128)(2,1)} %all-to-all-done.4), calls=%async_computation.5 | async-start | bytes 2097152 | tf_op jit(solution)/shard_map/all_to_all | solution.py:39
  207.9 16.8 %collective-permute-start.18 = (bf16[4,32,2048]{2,1,0:T(8,128)(2,1)}, bf16[4,32,2048]{2,1,0:T(8,128)(2,1)}, u32[]{:S(2)}, u32[]{:S(2)}) collective-permute-start(bf16[4,32,2048]{2,1,0:T(8,128)(2,1)} %fusion.25), channel_id=1, source_target_pairs={{0,4},{4,8},{8,12},{12,0},{1,5},{5,9},{9,13},{13,1},{2,6},{6,10},{... | collective-permute-start | bytes 1572872 | tf_op jit(solution)/shard_map/ppermute | solution.py:202
  210.4 25.6 %collective-permute-start.13 = (bf16[4,32,2048]{2,1,0:T(8,128)(2,1)}, bf16[4,32,2048]{2,1,0:T(8,128)(2,1)}, u32[]{:S(2)}, u32[]{:S(2)}) collective-permute-start(bf16[4,32,2048]{2,1,0:T(8,128)(2,1)} %fusion.18), channel_id=1, source_target_pairs={{0,4},{4,8},{8,12},{12,0},{1,5},{5,9},{9,13},{13,1},{2,6},{6,10},{... | collective-permute-start | bytes 1572872 | tf_op jit(solution)/shard_map/ppermute | solution.py:202
  214.8 45.2 %collective-permute-start.21 = (bf16[256,2048]{1,0:T(8,128)(2,1)}, bf16[256,2048]{1,0:T(8,128)(2,1)S(1)}, u32[]{:S(2)}, u32[]{:S(2)}) collective-permute-start(bf16[256,2048]{1,0:T(8,128)(2,1)} %fusion.4), channel_id=1, source_target_pairs={{16,0},{17,1},{18,2},{19,3},{20,4},{21,5},{22,6},{23,7},{24,8},{25... | collective-permute-start | bytes 3145736 | tf_op jit(solution)/shard_map/ppermute | solution.py:19
  227.0 20.2 %collective-permute-start.19 = (bf16[4,32,2048]{2,1,0:T(8,128)(2,1)}, bf16[4,32,2048]{2,1,0:T(8,128)(2,1)}, u32[]{:S(2)}, u32[]{:S(2)}) collective-permute-start(bf16[4,32,2048]{2,1,0:T(8,128)(2,1)} %fusion.15), channel_id=1, source_target_pairs={{0,4},{4,8},{8,12},{12,0},{1,5},{5,9},{9,13},{13,1},{2,6},{6,10},{... | collective-permute-start | bytes 1572872 | tf_op jit(solution)/shard_map/ppermute | solution.py:202
  238.2 20.2 %collective-permute-start.14 = (bf16[4,32,2048]{2,1,0:T(8,128)(2,1)}, bf16[4,32,2048]{2,1,0:T(8,128)(2,1)}, u32[]{:S(2)}, u32[]{:S(2)}) collective-permute-start(bf16[4,32,2048]{2,1,0:T(8,128)(2,1)} %fusion.19), channel_id=1, source_target_pairs={{0,4},{4,8},{8,12},{12,0},{1,5},{5,9},{9,13},{13,1},{2,6},{6,10},{... | collective-permute-start | bytes 1572872 | tf_op jit(solution)/shard_map/ppermute | solution.py:202
  248.7 20.4 %collective-permute-start.20 = (bf16[4,32,2048]{2,1,0:T(8,128)(2,1)S(1)}, bf16[4,32,2048]{2,1,0:T(8,128)(2,1)S(1)}, u32[]{:S(2)}, u32[]{:S(2)}) collective-permute-start(bf16[4,32,2048]{2,1,0:T(8,128)(2,1)S(1)} %fusion.16), channel_id=1, source_target_pairs={{0,4},{4,8},{8,12},{12,0},{1,5},{5,9},{9,13},{13,1},{2,6},{6,10},{... | collective-permute-start | bytes 1572872 | tf_op jit(solution)/shard_map/ppermute | solution.py:202
  (13 other events, 86.0 us)

commit v2 on v1

--- a/solution.py
+++ b/solution.py
@@ -19,6 +19,10 @@
     return lax.ppermute(block, axis, route)
 
 
+def after(value, *others):
+    return lax.optimization_barrier((value, *others))[0]
+
+
 def sizes():
     seq, tp = lax.axis_size("seq"), lax.axis_size("tp")
     assert seq % tp == 0 and tp % CORES == 0
@@ -39,22 +43,67 @@
     return lax.all_to_all(block, axis, 0, 0)
 
 
-def to_slabs(block):
+def mix_tokens(blocks):
+    tp = lax.axis_size("tp")
+    tokens, width = blocks[0].shape
+    stacked = jnp.stack([block.reshape(tp, tokens // tp, width) for block in blocks], axis=1)
+    return exchange(stacked, "tp")
+
+
+def to_slabs(parts):
     seq, tp, ratio = sizes()
-    tokens, width = block.shape
-    parts = exchange(block.reshape(tp, tokens // tp, width), "tp")
+    _, count, tokens, width = parts.shape
     if ratio > 1:
-        parts = parts.reshape(tp, tokens // tp, ratio, width // ratio).transpose(0, 2, 1, 3)
-    return exchange(parts.reshape(seq, tokens // tp, width // ratio), "seq")
-
-
-def from_slabs(block):
+        parts = parts.reshape(tp, count, tokens, ratio, width // ratio).transpose(0, 3, 1, 2, 4)
+    return exchange(parts.reshape(seq, count, tokens, width // ratio), "seq")
+
+
+def slabs_by_permutes(blocks):
+    seq, tp, _ = sizes()
+    place, lane = lax.axis_index("seq"), lax.axis_index("tp")
+    here, core = lane // CORES, lane % CORES
+    tokens, width = blocks[0].shape
+    stacked = jnp.stack(
+        [block.reshape(tp // CORES, CORES, tokens // tp, width) for block in blocks], axis=2
+    )
+    near = lax.dynamic_index_in_dim(stacked, here, 0, keepdims=False)
+    far = over_rows(lax.dynamic_index_in_dim(stacked, 1 - here, 0, keepdims=False), 1)
+    return near, far
+
+
+def spread(near, far):
+    seq, tp, _ = sizes()
+    place, lane = lax.axis_index("seq"), lax.axis_index("tp")
+    here, core = lane // CORES, lane % CORES
+    arrived = []
+    for j in range(seq):
+        slot = place ^ j
+        piece = jnp.where(
+            slot // CORES == here,
+            lax.dynamic_index_in_dim(near, slot % CORES, 0, keepdims=False),
+            lax.dynamic_index_in_dim(far, slot % CORES, 0, keepdims=False),
+        )
+        route = []
+        for q in range(seq):
+            for t in range(tp):
+                to = (t % CORES + (q ^ j) // CORES * CORES, t // CORES * CORES + (q ^ j) % CORES)
+                if to != (q, t):
+                    route.append((q * tp + t, to[0] * tp + to[1]))
+        moved = lax.ppermute(piece, ("seq", "tp"), route)
+        if j == 0:
+            moved = jnp.where(core == place % CORES, piece, moved)
+        arrived.append(moved)
+    slot = place // CORES * CORES + core
+    return jnp.stack([lax.select_n(slot ^ q, *arrived) for q in range(seq)], axis=0)
+
+
+def mix_features(block):
     seq, tp, ratio = sizes()
     _, tokens, width = block.shape
     parts = exchange(block, "seq")
     if ratio > 1:
         parts = parts.reshape(tp, ratio, tokens, width).transpose(0, 2, 1, 3)
-    return exchange(parts.reshape(tp, tokens, width * ratio), "tp")
+    return parts.reshape(tp, tokens, width * ratio)
 
 
 def gain_slab(gain):
@@ -95,24 +144,30 @@
 
 
 def product_kernel(*refs):
-    *pieces, weight, out, rows = refs
+    *pieces, weight, out, rows, blocks, sems = refs
     seq, depth, width = pieces[0].shape
-
-    @pl.when(pl.program_id(0) == 0)
-    def _():
-        for i, piece in enumerate(pieces):
-            rows[i] = piece[...]
-
-    terms = lax.dot_general(
-        rows[...].reshape(-1, width),
-        weight[...],
-        (((1,), (1,)), ((), ())),
-        preferred_element_type=jnp.float32,
-    )
-    for i in range(len(pieces)):
-        for q in range(seq):
-            start = (i * seq + q) * depth
-            out[q, i] = terms[start : start + depth]
+    count, block, _ = blocks.shape
+
+    def copy(b):
+        part = weight.at[pl.ds(b * block, block)]
+        return pltpu.make_async_copy(part, blocks.at[b], sems.at[b])
+
+    for b in range(count):
+        copy(b).start()
+    for i, piece in enumerate(pieces):
+        rows[i] = piece[...]
+    for b in range(count):
+        copy(b).wait()
+        terms = lax.dot_general(
+            rows[...].reshape(-1, width),
+            blocks[b],
+            (((1,), (1,)), ((), ())),
+            preferred_element_type=jnp.float32,
+        ).astype(out.dtype)
+        for i in range(len(pieces)):
+            for q in range(seq):
+                start = (i * seq + q) * depth
+                out[q, i, :, b * block : (b + 1) * block] = terms[start : start + depth]
 
 
 def product(pieces, weight):
@@ -122,15 +177,21 @@
     n = len(pieces)
     return pl.pallas_call(
         product_kernel,
-        out_shape=jax.ShapeDtypeStruct((seq, n, depth, heads), jnp.float32),
-        grid=(heads // block,),
-        in_specs=[pl.BlockSpec((seq, depth, width), lambda i: (0, 0, 0)) for _ in pieces]
-        + [pl.BlockSpec((block, width), lambda i: (i, 0))],
-        out_specs=pl.BlockSpec((seq, n, depth, block), lambda i: (0, 0, 0, i)),
-        scratch_shapes=[pltpu.VMEM((n, seq, depth, width), pieces[0].dtype)],
-        compiler_params=pltpu.CompilerParams(
-            dimension_semantics=("arbitrary",), vmem_limit_bytes=40 * 1024 * 1024
+        out_shape=jax.ShapeDtypeStruct((seq, n, depth, heads), jnp.bfloat16),
+        in_specs=[pl.BlockSpec(memory_space=pltpu.VMEM) for _ in pieces]
+        + [pl.BlockSpec(memory_space=pltpu.HBM)],
+        out_specs=pl.BlockSpec(memory_space=pltpu.VMEM),
+        cost_estimate=pl.CostEstimate(
+            flops=2 * n * seq * depth * width * heads,
+            bytes_accessed=2 * heads * width + 2 * n * seq * depth * (heads + width),
+            transcendentals=0,
         ),
+        scratch_shapes=[
+            pltpu.VMEM((n, seq, depth, width), pieces[0].dtype),
+            pltpu.VMEM((heads // block, block, width), weight.dtype),
+            pltpu.SemaphoreType.DMA((heads // block,)),
+        ],
+        compiler_params=pltpu.CompilerParams(vmem_limit_bytes=24 * 1024 * 1024),
     )(*pieces, weight)
 
 
@@ -145,14 +206,13 @@
     mixed = kv_cotangent[0].reshape(row, CORES, tokens // tp, -1)
     kept = lax.dynamic_index_in_dim(mixed, core, 1, keepdims=False)
     given = lax.dynamic_index_in_dim(mixed, 1 - core, 1, keepdims=False)
-    cotangent = gather_seq(jnp.concatenate([kept, over_cores(given)], axis=2))
+    given = over_cores(given)
+    cotangent = gather_seq(jnp.concatenate([kept, given], axis=2))
     weights = jnp.concatenate([kv_weight[0], over_cores(kv_weight[0])], axis=0)
 
-    values = to_slabs(layer_input[0])
     branch = mlp_grads[0].astype(jnp.float32)
     grad_one = output_cotangent.astype(jnp.float32) + branch
     base_home = jnp.where(upstream, mlp_grads[0], grad_one.astype(jnp.bfloat16))
-    base = to_slabs(base_home)
     gain = gain_slab(norm_gain)
     width = gain.shape[1]
 
@@ -163,8 +223,17 @@
         )
         return terms.reshape(seq, tokens // tp, width)
 
-    given = [over_rows(kv_of(turn).astype(jnp.bfloat16), turn) for turn in range(1, row)]
-    kv_share = kv_of(0)
+    given = [kv_of(turn).astype(jnp.bfloat16) for turn in range(1, row)]
+    blocks = [layer_input[0], base_home]
+    if seq == tp == 2 * CORES:
+        near, far = slabs_by_permutes(blocks)
+        far = after(far, *given)
+        slabs = spread(near, far)
+    else:
+        slabs = to_slabs(mix_tokens(blocks))
+    given = [over_rows(terms, turn) for turn, terms in enumerate(given, 1)]
+    kv_share, slabs = lax.optimization_barrier((kv_of(0), slabs))
+    values, base = slabs[:, 0], slabs[:, 1]
     for terms in given:
         kv_share = kv_share + terms.astype(jnp.float32)
 
@@ -177,30 +246,35 @@
         return array[:, c * depth : (c + 1) * depth]
 
     arrivals = [from_behind(cut(input_one, c), "section", -1) for c in range(CHUNKS)]
-    home = from_slabs(norm_back.astype(jnp.bfloat16))
+    home = mix_features(norm_back.astype(jnp.bfloat16))
     blocks_of = []
     for c in range(CHUNKS):
         part = cut(base, c)
         arriving = arrivals[c]
         if c > 0:
-            arriving, blocks[-1] = lax.optimization_barrier((arriving, blocks[-1]))
+            arriving = after(arriving, blocks[-1])
         grad_zero = arriving.astype(jnp.float32) + part.astype(jnp.float32)
         grad = jnp.where(upstream, grad_zero.astype(jnp.bfloat16), part)
         blocks = [over_rows(grad, turn) if turn else grad for turn in range(row)]
         blocks_of.append(blocks)
     attn_parts = []
     for c, blocks in enumerate(blocks_of):
+        if c == 0:
+            blocks[-1] = after(blocks[-1], home)
+        else:
+            blocks[-1] = after(blocks[-1], attn_parts[-1][0])
         pieces = [half for block in blocks for half in (block, over_cores(block))]
         terms = product(pieces, out_weight[0])
-        total = None
-        for step in range(1, seq + 1):
+        first = lax.dynamic_index_in_dim(terms, (place - 1) % seq, 0, keepdims=False)
+        attn_parts.append([first, terms])
+    home = after(home, attn_parts[-1][0])
+    for c, (mine, terms) in enumerate(attn_parts):
+        for step in range(2, seq + 1):
+            total = lax.ppermute(mine, "seq", [(q, (q + 1) % seq) for q in range(seq)])
             mine = lax.dynamic_index_in_dim(terms, (place - step) % seq, 0, keepdims=False)
-            if total is not None:
-                mine = mine + total.astype(jnp.float32)
+            mine = mine.astype(jnp.float32) + total.astype(jnp.float32)
             mine = mine.astype(jnp.bfloat16)
-            if step < seq:
-                total = lax.ppermute(mine, "seq", [(q, (q + 1) % seq) for q in range(seq)])
-        attn_parts.append(mine)
+        attn_parts[c] = mine
     attn_part = jnp.concatenate(attn_parts, axis=1)
     order = []
     for t in range(tp):
@@ -208,7 +282,7 @@
         order.append(lax.dynamic_index_in_dim(attn_part, which, 0, keepdims=False))
     attn_part = jnp.concatenate(order, axis=0)
 
-    home = home.reshape(tokens, -1).astype(jnp.float32)
+    home = exchange(home, "tp").reshape(tokens, -1).astype(jnp.float32)
     own = (grad_one + home).astype(jnp.bfloat16)
     arrived = from_behind(own, "section", -1)
     input_zero = (arrived.astype(jnp.float32) + branch + home).astype(jnp.bfloat16)

time: 273 us -> 238 us (0.87)
  waiting for transfers between devices: 153 us -> 125 us
  starting transfers between devices: 48.5 us -> 34.6 us
  local copies, waits for them, and re-layouts: 6.24 us -> 12.3 us
  other arithmetic: 23.5 us -> 29 us
  Pallas kernels: 15.1 us -> 11.7 us
  blocking collectives: 14.9 us -> 18.3 us
  matrix products: 9.08 us -> 5.71 us
    ppermute x0 -> x4, waiting for transfers between devices: none -> 28.2 us  [spread(): moved = lax.ppermute(piece, ('seq', 'tp'), route)]
    all_to_all x6 -> x2, waiting for transfers between devices: 28.2 us -> 0.01 us  [exchange(): return lax.all_to_all(block, axis, 0, 0)]
    ppermute x3, waiting for transfers between devices: 37.5 us -> 14.1 us  [gather_seq(): arrived.append(lax.ppermute(block, 'seq', route))]
    all_to_all x6 -> x2, starting transfers between devices: 30.1 us -> 8.65 us  [exchange(): return lax.all_to_all(block, axis, 0, 0)]
    ppermute x3 -> x4, waiting for transfers between devices: 27.7 us -> 12.4 us  [over_rows(): lax.ppermute(block, 'tp', [(t, (t + turn * CORES) % tp) for t in range(tp)])]
    ppermute x3, waiting for transfers between devices: 17.1 us -> 23.3 us  [from_behind(): return lax.ppermute(block, axis, route)]
    ppermute x0 -> x4, starting transfers between devices: none -> 5.6 us  [spread(): moved = lax.ppermute(piece, ('seq', 'tp'), route)]
    pallas_call x2, Pallas kernels: 15.1 us -> 11.7 us  [product(): pl.pallas_call(product_kernel, out_shape=jax.ShapeDtypeStruct((seq, n, de...]
  transfers between devices with their start and end apart: 28 -> 29, of which waited for: 16 -> 17; matrix products, arithmetic and copies ran while one was open for 10% -> 13% of each run, Pallas kernels for 6% -> 5%
where the time goes in v2:
time: 238 us; the launch traced here: 237 us
  waiting for transfers between devices  125 us (53%)
  starting transfers between devices  34.6 us (15%)
  other arithmetic  29 us (12%)
  blocking collectives  18.3 us (8%)
  local copies, waits for them, and re-layouts  12.3 us (5%)
  Pallas kernels  11.7 us (5%)
  matrix products  5.71 us (2%)
    ppermute x6, waiting for transfers between devices, body(): total = lax.ppermute(mine, 'seq', [(q, (q + 1) % seq) for q in range(seq)])  45.5 us
    ppermute x4, waiting for transfers between devices, spread(): moved = lax.ppermute(piece, ('seq', 'tp'), route)  28.2 us
    ppermute x3, waiting for transfers between devices, from_behind(): return lax.ppermute(block, axis, route)  23.3 us
    psum x1, blocking collectives, norm_backward(): lax.psum((jnp.sum(values * values, axis=-1), jnp.sum(gain * kv_share * va...  18.3 us
    ppermute x3, waiting for transfers between devices, gather_seq(): arrived.append(lax.ppermute(block, 'seq', route))  14.1 us
    ppermute x4, waiting for transfers between devices, over_rows(): lax.ppermute(block, 'tp', [(t, (t + turn * CORES) % tp) for t in range(tp)])  12.4 us
    pallas_call x2, Pallas kernels, product(): pl.pallas_call(product_kernel, out_shape=jax.ShapeDtypeStruct((seq, n, de...  11.7 us
    convert_element_type x6, other arithmetic, body(): mine = mine.astype(jnp.bfloat16)  9.46 us
  transfers between devices with their start and end apart: 29, of which 17 were waited for; matrix products, arithmetic and copies ran while one was open for 13% of the time, Pallas kernels for 5%

profile of v2, /device:TPU:0, one launch (start us, length us, event | category | flops | bytes accessed | tf_op | source)
XLA Modules:
  0.0 237.5 jit_solution(17470955252690940765)
XLA Ops:
  5.9 4.0 %collective-permute-start.2 = (bf16[2,64,1024]{2,1,0:T(8,128)(2,1)}, bf16[2,64,1024]{2,1,0:T(8,128)(2,1)}, u32[]{:S(2)}, u32[]{:S(2)}) collective-permute-start(bf16[2,64,1024]{2,1,0:T(8,128)(2,1)} %pad_maximum_fusion.2), channel_id=1, source_target_pairs={{0,8},{4,12},{8,0},{12,4},{1,9},{5,13},{9,1},{13,5},{2,10},{6,14},... | collective-permute-start | bytes 786440 | tf_op jit(solution)/shard_map/ppermute | solution.py:131
  14.4 8.7 %collective-permute-done.2 = bf16[2,64,1024]{2,1,0:T(8,128)(2,1)} collective-permute-done((bf16[2,64,1024]{2,1,0:T(8,128)(2,1)}, bf16[2,64,1024]{2,1,0:T(8,128)(2,1)}, u32[]{:S(2)}, u32[]{:S(2)}) %collective-permute-start.2) | collective-permute-done | bytes 262176 | tf_op jit(solution)/shard_map/ppermute | solution.py:131
  23.8 5.4 %collective-permute-done.1 = bf16[2,64,1024]{2,1,0:T(8,128)(2,1)} collective-permute-done((bf16[2,64,1024]{2,1,0:T(8,128)(2,1)}, bf16[2,64,1024]{2,1,0:T(8,128)(2,1)}, u32[]{:S(2)}, u32[]{:S(2)}) %collective-permute-start.1) | collective-permute-done | bytes 262176 | tf_op jit(solution)/shard_map/ppermute | solution.py:131
  37.6 4.8 %collective-permute-start.8 = (bf16[2,64,2048]{2,1,0:T(8,128)(2,1)S(1)}, bf16[2,64,2048]{2,1,0:T(8,128)(2,1)S(1)}, u32[]{:S(2)}, u32[]{:S(2)}) collective-permute-start(bf16[2,64,2048]{2,1,0:T(8,128)(2,1)S(1)} %fusion.35), channel_id=1, source_target_pairs={{0,8},{1,12},{2,10},{3,14},{4,9},{5,13},{6,11},{7,15},{8,0},{9,4},... | collective-permute-start | bytes 1572872 | tf_op jit(solution)/shard_map/ppermute | solution.py:92
  45.1 2.9 %fusion.1 = f32[4,64,2048]{2,1,0:T(8,128)S(1)} fusion(bf16[512,2048]{1,0:T(8,128)(2,1)} %collective-permute-done.4, bf16[512,2048]{1,0:T(8,128)(2,1)S(1)} %bitcast.152, bf16[4,2,64,1024]{3,2,0,1:T(8,128)(2,1)S(1)} %pad_maximum_fusion.1, s32[]{:T(128)S(6)} %select_n.530), kind=kOutput, calls=%fused_computation.15 | convolution fusion | flops 1082130432 | bytes 6815748 | tf_op jit(solution)/shard_map/dot_general | solution.py:221
  48.0 28.2 %collective-permute-done.8 = bf16[2,64,2048]{2,1,0:T(8,128)(2,1)S(1)} collective-permute-done((bf16[2,64,2048]{2,1,0:T(8,128)(2,1)S(1)}, bf16[2,64,2048]{2,1,0:T(8,128)(2,1)S(1)}, u32[]{:S(2)}, u32[]{:S(2)}) %collective-permute-start.8) | collective-permute-done | bytes 524320 | tf_op jit(solution)/shard_map/ppermute | solution.py:92
  77.6 18.3 %all-reduce = (f32[4,64]{1,0:T(4,128)S(1)}, f32[4,64]{1,0:T(4,128)S(1)}) all-reduce(f32[4,64]{1,0:T(4,128)S(1)} %get-tuple-element.17, f32[4,64]{1,0:T(4,128)S(1)} %get-tuple-element.16), channel_id=1, replica_groups=mesh['section'=2,'seq'=4,'tp'=4] {'seq'}, use_global_device_ids=true, to_apply=%region_3.4 | all-reduce | flops 512 | bytes 4096 | tf_op jit(solution)/shard_map/psum | solution.py:136
  95.9 3.8 %fusion.48 = (bf16[4,64,2048]{2,1,0:T(8,128)(2,1)}, bf16[4,64,2048]{2,1,0:T(8,128)(2,1)}) fusion(f32[4,64]{1,0:T(4,128)S(1)} %get-tuple-element.18, f32[4,64]{1,0:T(4,128)S(1)} %get-tuple-element.42, bf16[4,2,64,2048]{3,2,0,1:T(8,128)(2,1)S(1)} %pad_maximum_fusion, f32[4,64,2048]{2,1,0:T(8,128)} %copy-done.9, ...), kind=kLoop, calls=%fused_computation.102 | loop fusion | flops 6815744 | bytes 7351296 | tf_op jit(solution)/shard_map/convert_element_type | solution.py:249
  99.7 4.4 %all-to-all-start = ((bf16[4,64,2048]{2,1,0:T(8,128)(2,1)}), bf16[4,64,2048]{2,1,0:T(8,128)(2,1)}, u32[]{:S(2)}, u32[]{:S(2)}) async-start(bf16[4,64,2048]{2,1,0:T(8,128)(2,1)} %get-tuple-element.22), calls=%async_computation | async-start | bytes 2097152 | tf_op jit(solution)/shard_map/all_to_all | solution.py:43
  106.4 13.9 %collective-permute-done.12 = bf16[4,32,2048]{2,1,0:T(8,128)(2,1)S(1)} collective-permute-done((bf16[4,32,2048]{2,1,0:T(8,128)(2,1)S(1)}, bf16[4,32,2048]{2,1,0:T(8,128)(2,1)S(1)}, u32[]{:S(2)}, u32[]{:S(2)}) %collective-permute-start.12) | collective-permute-done | bytes 524320 | tf_op jit(solution)/shard_map/ppermute | solution.py:19
  124.5 9.8 %collective-permute-done.14.refs_2_ = bf16[4,32,2048]{2,1,0:T(8,128)(2,1)S(1)} collective-permute-done((bf16[4,32,2048]{2,1,0:T(8,128)(2,1)S(1)}, bf16[4,32,2048]{2,1,0:T(8,128)(2,1)S(1)}, u32[]{:S(2)}, u32[]{:S(2)}) %collective-permute-start.14) | collective-permute-done | bytes 524320 | tf_op jit(solution)/shard_map/ppermute | solution.py:34
  134.3 3.5 %collective-permute-done.19 = bf16[4,32,2048]{2,1,0:T(8,128)(2,1)S(1)} collective-permute-done((bf16[4,32,2048]{2,1,0:T(8,128)(2,1)}, bf16[4,32,2048]{2,1,0:T(8,128)(2,1)S(1)}, u32[]{:S(2)}, u32[]{:S(2)}) %collective-permute-start.19) | collective-permute-done | bytes 524320 | tf_op jit(solution)/shard_map/ppermute | solution.py:19
  141.1 3.4 %copy-done.1 = bf16[1,2048,2048]{2,1,0:T(8,128)(2,1)S(1)} copy-done((bf16[1,2048,2048]{2,1,0:T(8,128)(2,1)S(1)}, bf16[1,2048,2048]{2,1,0:T(8,128)(2,1)}, u32[]{:S(2)}) %copy-start.1) | copy-done | bytes 8388632
  146.6 5.9 %shard_map.86 = bf16[4,4,32,2048]{3,2,1,0:T(8,128)(2,1)S(1)} custom-call(bf16[4,32,2048]{2,1,0:T(8,128)(2,1)S(1)} %fusion.22.refs_0_, bf16[4,32,2048]{2,1,0:T(8,128)(2,1)S(1)} %copy-done.3, bf16[4,32,2048]{2,1,0:T(8,128)(2,1)S(1)} %collective-permute-done.14.refs_2_, bf16[4,32,2048]{2,1,0:T(8,128)(2,1)S(1)} %copy-done.5, bf16[2048,2048]{1,0:T(8,128)(2,1)S(1)} %bitcast.139), custom_call_target="tpu_custom_call" | custom-call | flops 4294967296 | bytes 12582912 | tf_op jit(solution)/shard_map/pallas_call | solution.py:178
  155.4 5.9 %shard_map.87 = bf16[4,4,32,2048]{3,2,1,0:T(8,128)(2,1)S(1)} custom-call(bf16[4,32,2048]{2,1,0:T(8,128)(2,1)S(1)} %fusion.23.refs_0_, bf16[4,32,2048]{2,1,0:T(8,128)(2,1)S(1)} %collective-permute-done.20.refs_1_, bf16[4,32,2048]{2,1,0:T(8,128)(2,1)S(1)} %collective-permute-done.21.refs_2_, bf16[4,32,2048]{2,1,0:T(8,128)(2,1)S(1)} %collective-permute-done.22.refs_3_, ...), custom_call_target="tpu_custom_call" | custom-call | flops 4294967296 | bytes 12582912 | tf_op jit(solution)/shard_map/pallas_call | solution.py:178
  164.8 5.4 %collective-permute-done.16 = bf16[4,32,2048]{2,1,0:T(8,128)(2,1)S(1)} collective-permute-done((bf16[4,32,2048]{2,1,0:T(8,128)(2,1)}, bf16[4,32,2048]{2,1,0:T(8,128)(2,1)S(1)}, u32[]{:S(2)}, u32[]{:S(2)}) %collective-permute-start.16) | collective-permute-done | bytes 524320 | tf_op jit(solution)/shard_map/ppermute | solution.py:273
  171.2 10.3 %collective-permute-done.23 = bf16[4,32,2048]{2,1,0:T(8,128)(2,1)S(1)} collective-permute-done((bf16[4,32,2048]{2,1,0:T(8,128)(2,1)}, bf16[4,32,2048]{2,1,0:T(8,128)(2,1)S(1)}, u32[]{:S(2)}, u32[]{:S(2)}) %collective-permute-start.23) | collective-permute-done | bytes 524320 | tf_op jit(solution)/shard_map/ppermute | solution.py:273
  183.4 4.3 %all-to-all-start.1 = ((bf16[4,64,2048]{2,1,0:T(8,128)(2,1)}), bf16[4,64,2048]{2,1,0:T(8,128)(2,1)}, u32[]{:S(2)}, u32[]{:S(2)}) async-start(bf16[4,64,2048]{2,1,0:T(8,128)(2,1)} %all-to-all-done), calls=%async_computation.1 | async-start | bytes 2097152 | tf_op jit(solution)/shard_map/all_to_all | solution.py:43
  187.7 5.1 %collective-permute-done.17 = bf16[4,32,2048]{2,1,0:T(8,128)(2,1)} collective-permute-done((bf16[4,32,2048]{2,1,0:T(8,128)(2,1)}, bf16[4,32,2048]{2,1,0:T(8,128)(2,1)}, u32[]{:S(2)}, u32[]{:S(2)}) %collective-permute-start.17) | collective-permute-done | bytes 524320 | tf_op jit(solution)/shard_map/ppermute | solution.py:273
  194.8 9.3 %collective-permute-done.24 = bf16[4,32,2048]{2,1,0:T(8,128)(2,1)} collective-permute-done((bf16[4,32,2048]{2,1,0:T(8,128)(2,1)}, bf16[4,32,2048]{2,1,0:T(8,128)(2,1)}, u32[]{:S(2)}, u32[]{:S(2)}) %collective-permute-start.24) | collective-permute-done | bytes 524320 | tf_op jit(solution)/shard_map/ppermute | solution.py:273
  209.5 5.7 %collective-permute-done.18 = bf16[4,32,2048]{2,1,0:T(8,128)(2,1)} collective-permute-done((bf16[4,32,2048]{2,1,0:T(8,128)(2,1)}, bf16[4,32,2048]{2,1,0:T(8,128)(2,1)}, u32[]{:S(2)}, u32[]{:S(2)}) %collective-permute-start.18) | collective-permute-done | bytes 524320 | tf_op jit(solution)/shard_map/ppermute | solution.py:273
  216.5 9.7 %collective-permute-done.25 = bf16[4,32,2048]{2,1,0:T(8,128)(2,1)} collective-permute-done((bf16[4,32,2048]{2,1,0:T(8,128)(2,1)}, bf16[4,32,2048]{2,1,0:T(8,128)(2,1)}, u32[]{:S(2)}, u32[]{:S(2)}) %collective-permute-start.25) | collective-permute-done | bytes 524320 | tf_op jit(solution)/shard_map/ppermute | solution.py:273
  228.6 5.9 %collective-permute-done.26 = bf16[256,2048]{1,0:T(8,128)(2,1)S(1)} collective-permute-done((bf16[256,2048]{1,0:T(8,128)(2,1)S(1)}, bf16[256,2048]{1,0:T(8,128)(2,1)S(1)}, u32[]{:S(2)}, u32[]{:S(2)}) %collective-permute-start.26) | collective-permute-done | bytes 1048608 | tf_op jit(solution)/shard_map/ppermute | solution.py:19
  234.5 2.9 %fusion.13 = bf16[1,256,2048]{2,1,0:T(8,128)(2,1)} fusion(bf16[256,2048]{1,0:T(8,128)(2,1)S(1)} %collective-permute-done.26, bf16[4,64,2048]{2,1,0:T(8,128)(2,1)} %all-to-all-done.1, bf16[1,256,2048]{2,1,0:T(8,128)(2,1)S(1)} %copy-done.8, pred[]{:T(512)S(6)} %eq.60, bf16[256,2048]{1,0:T(8,128)(2,1)S(1)} %copy-done.7), kind=kLoop, calls=%fused_computation.42 | loop fusion | flops 5767168 | bytes 5242881 | tf_op jit(solution)/shard_map/broadcast_in_dim | solution.py:290
  (99 shorter events, 55.2 us)
Async XLA Ops:
  0.6 31.4 %collective-permute-start.4 = (bf16[512,2048]{1,0:T(8,128)(2,1)}, bf16[512,2048]{1,0:T(8,128)(2,1)}, u32[]{:S(2)}, u32[]{:S(2)}) collective-permute-start(bf16[512,2048]{1,0:T(8,128)(2,1)} %bitcast.150), channel_id=1, source_target_pairs={{0,1},{1,0},{2,3},{3,2},{4,5},{5,4},{6,7},{7,6},{8,9},{9,8},{10,11... | collective-permute-start | bytes 6291464 | tf_op jit(solution)/shard_map/ppermute | solution.py:39
  5.9 17.2 %collective-permute-start.2 = (bf16[2,64,1024]{2,1,0:T(8,128)(2,1)}, bf16[2,64,1024]{2,1,0:T(8,128)(2,1)}, u32[]{:S(2)}, u32[]{:S(2)}) collective-permute-start(bf16[2,64,1024]{2,1,0:T(8,128)(2,1)} %pad_maximum_fusion.2), channel_id=1, source_target_pairs={{0,8},{4,12},{8,0},{12,4},{1,9},{5,13},{9,1},{13,5},{2,10},{6,14},... | collective-permute-start | bytes 786440 | tf_op jit(solution)/shard_map/ppermute | solution.py:131
  11.2 18.0 %collective-permute-start.1 = (bf16[2,64,1024]{2,1,0:T(8,128)(2,1)}, bf16[2,64,1024]{2,1,0:T(8,128)(2,1)}, u32[]{:S(2)}, u32[]{:S(2)}) collective-permute-start(bf16[2,64,1024]{2,1,0:T(8,128)(2,1)} %pad_maximum_fusion.2), channel_id=1, source_target_pairs={{0,4},{4,8},{8,12},{12,0},{1,5},{5,9},{9,13},{13,1},{2,6},{6,10},{... | collective-permute-start | bytes 786440 | tf_op jit(solution)/shard_map/ppermute | solution.py:131
  12.9 24.6 %collective-permute-start.5 = (bf16[2,2,64,2048]{3,2,1,0:T(8,128)(2,1)}, bf16[2,2,64,2048]{3,2,1,0:T(8,128)(2,1)S(1)}, u32[]{:S(2)}, u32[]{:S(2)}) collective-permute-start(bf16[2,2,64,2048]{3,2,1,0:T(8,128)(2,1)} %fusion.15), channel_id=1, source_target_pairs={{0,2},{1,3},{2,0},{3,1},{4,6},{5,7},{6,4},{7,5},{8,10},{9,11},{10,... | collective-permute-start | bytes 3145736 | tf_op jit(solution)/shard_map/ppermute | solution.py:34
  23.1 20.3 %collective-permute-start.10 = (f32[1,2048]{1,0:T(1,128)S(1)}, f32[1,2048]{1,0:T(1,128)S(1)}, u32[]{:S(2)}, u32[]{:S(2)}) collective-permute-start(f32[1,2048]{1,0:T(1,128)S(1)} %copy-done.12), channel_id=1, source_target_pairs={{1,4},{2,8},{3,12},{4,1},{6,9},{7,13},{8,2},{9,6},{11,14},{12,3},{... | collective-permute-start | bytes 24584 | tf_op jit(solution)/shard_map/ppermute | solution.py:120
  37.6 38.7 %collective-permute-start.8 = (bf16[2,64,2048]{2,1,0:T(8,128)(2,1)S(1)}, bf16[2,64,2048]{2,1,0:T(8,128)(2,1)S(1)}, u32[]{:S(2)}, u32[]{:S(2)}) collective-permute-start(bf16[2,64,2048]{2,1,0:T(8,128)(2,1)S(1)} %fusion.35), channel_id=1, source_target_pairs={{0,8},{1,12},{2,10},{3,14},{4,9},{5,13},{6,11},{7,15},{8,0},{9,4},... | collective-permute-start | bytes 1572872 | tf_op jit(solution)/shard_map/ppermute | solution.py:92
  42.5 33.8 %collective-permute-start.9 = (bf16[2,64,2048]{2,1,0:T(8,128)(2,1)S(1)}, bf16[2,64,2048]{2,1,0:T(8,128)(2,1)S(1)}, u32[]{:S(2)}, u32[]{:S(2)}) collective-permute-start(bf16[2,64,2048]{2,1,0:T(8,128)(2,1)S(1)} %get-tuple-element.25), channel_id=1, source_target_pairs={{0,9},{1,13},{2,11},{3,15},{4,8},{5,12},{6,10},{7,14},{8,1},{9,5},... | collective-permute-start | bytes 1572872 | tf_op jit(solution)/shard_map/ppermute | solution.py:92
  42.6 33.7 %collective-permute-start.7 = (bf16[2,64,2048]{2,1,0:T(8,128)(2,1)S(1)}, bf16[2,64,2048]{2,1,0:T(8,128)(2,1)S(1)}, u32[]{:S(2)}, u32[]{:S(2)}) collective-permute-start(bf16[2,64,2048]{2,1,0:T(8,128)(2,1)S(1)} %get-tuple-element.26), channel_id=1, source_target_pairs={{0,1},{1,5},{2,3},{3,7},{4,0},{5,4},{6,2},{7,6},{8,9},{9,13},{10,1... | collective-permute-start | bytes 1572872 | tf_op jit(solution)/shard_map/ppermute | solution.py:92
  42.7 33.6 %collective-permute-start.6 = (bf16[2,64,2048]{2,1,0:T(8,128)(2,1)S(1)}, bf16[2,64,2048]{2,1,0:T(8,128)(2,1)S(1)}, u32[]{:S(2)}, u32[]{:S(2)}) collective-permute-start(bf16[2,64,2048]{2,1,0:T(8,128)(2,1)S(1)} %get-tuple-element.24), channel_id=1, source_target_pairs={{1,4},{3,6},{4,1},{6,3},{9,12},{11,14},{12,9},{14,11},{17,20},{19,... | collective-permute-start | bytes 1572872 | tf_op jit(solution)/shard_map/ppermute | solution.py:92
  43.4 33.5 %collective-permute-start.11 = (bf16[4,64,2048]{2,1,0:T(8,128)(2,1)S(1)}, bf16[4,64,2048]{2,1,0:T(8,128)(2,1)S(1)}, u32[]{:S(2)}, u32[]{:S(2)}) collective-permute-start(bf16[4,64,2048]{2,1,0:T(8,128)(2,1)S(1)} %fusion.2), channel_id=1, source_target_pairs={{0,2},{1,3},{2,0},{3,1},{4,6},{5,7},{6,4},{7,5},{8,10},{9,11},{10,... | collective-permute-start | bytes 3145736 | tf_op jit(solution)/shard_map/ppermute | solution.py:34
  99.7 34.6 %all-to-all-start = ((bf16[4,64,2048]{2,1,0:T(8,128)(2,1)}), bf16[4,64,2048]{2,1,0:T(8,128)(2,1)}, u32[]{:S(2)}, u32[]{:S(2)}) async-start(bf16[4,64,2048]{2,1,0:T(8,128)(2,1)} %get-tuple-element.22), calls=%async_computation | async-start | bytes 2097152 | tf_op jit(solution)/shard_map/all_to_all | solution.py:43
  105.0 15.2 %collective-permute-start.12 = (bf16[4,32,2048]{2,1,0:T(8,128)(2,1)S(1)}, bf16[4,32,2048]{2,1,0:T(8,128)(2,1)S(1)}, u32[]{:S(2)}, u32[]{:S(2)}) collective-permute-start(bf16[4,32,2048]{2,1,0:T(8,128)(2,1)S(1)} %get-tuple-element.35), channel_id=1, source_target_pairs={{16,0},{17,1},{18,2},{19,3},{20,4},{21,5},{22,6},{23,7},{24,8},{25... | collective-permute-start | bytes 1572872 | tf_op jit(solution)/shard_map/ppermute | solution.py:19
  123.0 14.9 %collective-permute-start.19 = (bf16[4,32,2048]{2,1,0:T(8,128)(2,1)}, bf16[4,32,2048]{2,1,0:T(8,128)(2,1)S(1)}, u32[]{:S(2)}, u32[]{:S(2)}) collective-permute-start(bf16[4,32,2048]{2,1,0:T(8,128)(2,1)} %get-tuple-element.34), channel_id=1, source_target_pairs={{16,0},{17,1},{18,2},{19,3},{20,4},{21,5},{22,6},{23,7},{24,8},{25... | collective-permute-start | bytes 1572872 | tf_op jit(solution)/shard_map/ppermute | solution.py:19
  124.4 15.1 %collective-permute-start.13 = (bf16[4,32,2048]{2,1,0:T(8,128)(2,1)S(1)}, bf16[4,32,2048]{2,1,0:T(8,128)(2,1)S(1)}, u32[]{:S(2)}, u32[]{:S(2)}) collective-permute-start(bf16[4,32,2048]{2,1,0:T(8,128)(2,1)S(1)} %fusion.22.refs_0_), channel_id=1, source_target_pairs={{0,1},{1,0},{2,3},{3,2},{4,5},{5,4},{6,7},{7,6},{8,9},{9,8},{10,11... | collective-permute-start | bytes 1572872 | tf_op jit(solution)/shard_map/ppermute | solution.py:39
  139.1 15.8 %collective-permute-start.20 = (bf16[4,32,2048]{2,1,0:T(8,128)(2,1)S(1)}, bf16[4,32,2048]{2,1,0:T(8,128)(2,1)S(1)}, u32[]{:S(2)}, u32[]{:S(2)}) collective-permute-start(bf16[4,32,2048]{2,1,0:T(8,128)(2,1)S(1)} %fusion.23.refs_0_), channel_id=1, source_target_pairs={{0,1},{1,0},{2,3},{3,2},{4,5},{5,4},{6,7},{7,6},{8,9},{9,8},{10,11... | collective-permute-start | bytes 1572872 | tf_op jit(solution)/shard_map/ppermute | solution.py:39
  139.2 14.3 %collective-permute-start.21 = (bf16[4,32,2048]{2,1,0:T(8,128)(2,1)S(1)}, bf16[4,32,2048]{2,1,0:T(8,128)(2,1)S(1)}, u32[]{:S(2)}, u32[]{:S(2)}) collective-permute-start(bf16[4,32,2048]{2,1,0:T(8,128)(2,1)S(1)} %fusion.23.refs_0_), channel_id=1, source_target_pairs={{0,2},{1,3},{2,0},{3,1},{4,6},{5,7},{6,4},{7,5},{8,10},{9,11},{10,... | collective-permute-start | bytes 1572872 | tf_op jit(solution)/shard_map/ppermute | solution.py:34
  153.5 16.7 %collective-permute-start.16 = (bf16[4,32,2048]{2,1,0:T(8,128)(2,1)}, bf16[4,32,2048]{2,1,0:T(8,128)(2,1)S(1)}, u32[]{:S(2)}, u32[]{:S(2)}) collective-permute-start(bf16[4,32,2048]{2,1,0:T(8,128)(2,1)} %dynamic-slice_bitcast_fusion.1), channel_id=1, source_target_pairs={{0,4},{4,8},{8,12},{12,0},{1,5},{5,9},{9,13},{13,1},{2,6},{6,10},{... | collective-permute-start | bytes 1572872 | tf_op jit(solution)/shard_map/ppermute | solution.py:273
  163.5 18.0 %collective-permute-start.23 = (bf16[4,32,2048]{2,1,0:T(8,128)(2,1)}, bf16[4,32,2048]{2,1,0:T(8,128)(2,1)S(1)}, u32[]{:S(2)}, u32[]{:S(2)}) collective-permute-start(bf16[4,32,2048]{2,1,0:T(8,128)(2,1)} %dynamic-slice_bitcast_fusion), channel_id=1, source_target_pairs={{0,4},{4,8},{8,12},{12,0},{1,5},{5,9},{9,13},{13,1},{2,6},{6,10},{... | collective-permute-start | bytes 1572872 | tf_op jit(solution)/shard_map/ppermute | solution.py:273
  171.2 21.7 %collective-permute-start.17 = (bf16[4,32,2048]{2,1,0:T(8,128)(2,1)}, bf16[4,32,2048]{2,1,0:T(8,128)(2,1)}, u32[]{:S(2)}, u32[]{:S(2)}) collective-permute-start(bf16[4,32,2048]{2,1,0:T(8,128)(2,1)} %fusion.19), channel_id=1, source_target_pairs={{0,4},{4,8},{8,12},{12,0},{1,5},{5,9},{9,13},{13,1},{2,6},{6,10},{... | collective-permute-start | bytes 1572872 | tf_op jit(solution)/shard_map/ppermute | solution.py:273
  183.4 20.6 %collective-permute-start.24 = (bf16[4,32,2048]{2,1,0:T(8,128)(2,1)}, bf16[4,32,2048]{2,1,0:T(8,128)(2,1)}, u32[]{:S(2)}, u32[]{:S(2)}) collective-permute-start(bf16[4,32,2048]{2,1,0:T(8,128)(2,1)} %fusion.16), channel_id=1, source_target_pairs={{0,4},{4,8},{8,12},{12,0},{1,5},{5,9},{9,13},{13,1},{2,6},{6,10},{... | collective-permute-start | bytes 1572872 | tf_op jit(solution)/shard_map/ppermute | solution.py:273
  183.4 22.7 %all-to-all-start.1 = ((bf16[4,64,2048]{2,1,0:T(8,128)(2,1)}), bf16[4,64,2048]{2,1,0:T(8,128)(2,1)}, u32[]{:S(2)}, u32[]{:S(2)}) async-start(bf16[4,64,2048]{2,1,0:T(8,128)(2,1)} %all-to-all-done), calls=%async_computation.1 | async-start | bytes 2097152 | tf_op jit(solution)/shard_map/all_to_all | solution.py:43
  194.8 20.5 %collective-permute-start.18 = (bf16[4,32,2048]{2,1,0:T(8,128)(2,1)}, bf16[4,32,2048]{2,1,0:T(8,128)(2,1)}, u32[]{:S(2)}, u32[]{:S(2)}) collective-permute-start(bf16[4,32,2048]{2,1,0:T(8,128)(2,1)} %fusion.20), channel_id=1, source_target_pairs={{0,4},{4,8},{8,12},{12,0},{1,5},{5,9},{9,13},{13,1},{2,6},{6,10},{... | collective-permute-start | bytes 1572872 | tf_op jit(solution)/shard_map/ppermute | solution.py:273
  206.2 20.0 %collective-permute-start.25 = (bf16[4,32,2048]{2,1,0:T(8,128)(2,1)}, bf16[4,32,2048]{2,1,0:T(8,128)(2,1)}, u32[]{:S(2)}, u32[]{:S(2)}) collective-permute-start(bf16[4,32,2048]{2,1,0:T(8,128)(2,1)} %fusion.17), channel_id=1, source_target_pairs={{0,4},{4,8},{8,12},{12,0},{1,5},{5,9},{9,13},{13,1},{2,6},{6,10},{... | collective-permute-start | bytes 1572872 | tf_op jit(solution)/shard_map/ppermute | solution.py:273
  208.2 26.3 %collective-permute-start.26 = (bf16[256,2048]{1,0:T(8,128)(2,1)S(1)}, bf16[256,2048]{1,0:T(8,128)(2,1)S(1)}, u32[]{:S(2)}, u32[]{:S(2)}) collective-permute-start(bf16[256,2048]{1,0:T(8,128)(2,1)S(1)} %fusion.3), channel_id=1, source_target_pairs={{16,0},{17,1},{18,2},{19,3},{20,4},{21,5},{22,6},{23,7},{24,8},{25... | collective-permute-start | bytes 3145736 | tf_op jit(solution)/shard_map/ppermute | solution.py:19
  (19 other events, 155.3 us)

commit v3 on v2

--- a/solution.py
+++ b/solution.py
@@ -132,10 +132,10 @@
     return jnp.stack([lax.select_n((place - q) % seq, *arrived) for q in range(seq)], axis=0)
 
 
-def norm_backward(values, gain, kv_share, axes):
-    squares, intersection = lax.psum(
-        (jnp.sum(values * values, axis=-1), jnp.sum(gain * kv_share * values, axis=-1)), axes
-    )
+def norm_backward(values, gain, kv_share):
+    sums = jnp.stack([jnp.sum(values * values, axis=-1), jnp.sum(gain * kv_share * values, axis=-1)])
+    short = lax.axis_size("seq") <= 2 * CORES
+    squares, intersection = jnp.sum(gather_seq(sums), axis=0) if short else lax.psum(sums, "seq")
     inv_rms = lax.rsqrt(squares / D + epsilon)[..., None]
     return (
         inv_rms * gain * kv_share
@@ -144,30 +144,24 @@
 
 
 def product_kernel(*refs):
-    *pieces, weight, out, rows, blocks, sems = refs
+    *pieces, weight, out, rows = refs
     seq, depth, width = pieces[0].shape
-    count, block, _ = blocks.shape
-
-    def copy(b):
-        part = weight.at[pl.ds(b * block, block)]
-        return pltpu.make_async_copy(part, blocks.at[b], sems.at[b])
-
-    for b in range(count):
-        copy(b).start()
-    for i, piece in enumerate(pieces):
-        rows[i] = piece[...]
-    for b in range(count):
-        copy(b).wait()
-        terms = lax.dot_general(
-            rows[...].reshape(-1, width),
-            blocks[b],
-            (((1,), (1,)), ((), ())),
-            preferred_element_type=jnp.float32,
-        ).astype(out.dtype)
-        for i in range(len(pieces)):
-            for q in range(seq):
-                start = (i * seq + q) * depth
-                out[q, i, :, b * block : (b + 1) * block] = terms[start : start + depth]
+
+    @pl.when(pl.program_id(0) == 0)
+    def _():
+        for i, piece in enumerate(pieces):
+            rows[i] = piece[...]
+
+    terms = lax.dot_general(
+        rows[...].reshape(-1, width),
+        weight[...],
+        (((1,), (1,)), ((), ())),
+        preferred_element_type=jnp.float32,
+    ).astype(out.dtype)
+    for i in range(len(pieces)):
+        for q in range(seq):
+            start = (i * seq + q) * depth
+            out[q, i] = terms[start : start + depth]
 
 
 def product(pieces, weight):
@@ -178,20 +172,19 @@
     return pl.pallas_call(
         product_kernel,
         out_shape=jax.ShapeDtypeStruct((seq, n, depth, heads), jnp.bfloat16),
-        in_specs=[pl.BlockSpec(memory_space=pltpu.VMEM) for _ in pieces]
-        + [pl.BlockSpec(memory_space=pltpu.HBM)],
-        out_specs=pl.BlockSpec(memory_space=pltpu.VMEM),
+        grid=(heads // block,),
+        in_specs=[pl.BlockSpec((seq, depth, width), lambda i: (0, 0, 0)) for _ in pieces]
+        + [pl.BlockSpec((block, width), lambda i: (i, 0))],
+        out_specs=pl.BlockSpec((seq, n, depth, block), lambda i: (0, 0, 0, i)),
         cost_estimate=pl.CostEstimate(
             flops=2 * n * seq * depth * width * heads,
-            bytes_accessed=2 * heads * width + 2 * n * seq * depth * (heads + width),
+            bytes_accessed=2 * heads * width + 2 * n * seq * depth * heads,
             transcendentals=0,
         ),
-        scratch_shapes=[
-            pltpu.VMEM((n, seq, depth, width), pieces[0].dtype),
-            pltpu.VMEM((heads // block, block, width), weight.dtype),
-            pltpu.SemaphoreType.DMA((heads // block,)),
-        ],
-        compiler_params=pltpu.CompilerParams(vmem_limit_bytes=24 * 1024 * 1024),
+        scratch_shapes=[pltpu.VMEM((n, seq, depth, width), pieces[0].dtype)],
+        compiler_params=pltpu.CompilerParams(
+            dimension_semantics=("arbitrary",), vmem_limit_bytes=44 * 1024 * 1024
+        ),
     )(*pieces, weight)
 
 
@@ -237,7 +230,7 @@
     for terms in given:
         kv_share = kv_share + terms.astype(jnp.float32)
 
-    norm_back = norm_backward(values.astype(jnp.float32), gain, kv_share, "seq")
+    norm_back = norm_backward(values.astype(jnp.float32), gain, kv_share)
     input_one = (base.astype(jnp.float32) + norm_back).astype(jnp.bfloat16)
 
     depth = tokens // tp // CHUNKS
@@ -245,8 +238,9 @@
     def cut(array, c):
         return array[:, c * depth : (c + 1) * depth]
 
-    arrivals = [from_behind(cut(input_one, c), "section", -1) for c in range(CHUNKS)]
-    home = mix_features(norm_back.astype(jnp.bfloat16))
+    leaving = [cut(input_one, c) for c in range(CHUNKS)]
+    arrivals = [from_behind(part, "section", -1) for part in leaving]
+    home = mix_features(after(norm_back.astype(jnp.bfloat16), leaving[-1]))
     blocks_of = []
     for c in range(CHUNKS):
         part = cut(base, c)
@@ -259,18 +253,25 @@
         blocks_of.append(blocks)
     attn_parts = []
     for c, blocks in enumerate(blocks_of):
-        if c == 0:
-            blocks[-1] = after(blocks[-1], home)
-        else:
+        if c > 0:
             blocks[-1] = after(blocks[-1], attn_parts[-1][0])
         pieces = [half for block in blocks for half in (block, over_cores(block))]
         terms = product(pieces, out_weight[0])
         first = lax.dynamic_index_in_dim(terms, (place - 1) % seq, 0, keepdims=False)
+        if c == 0:
+            first = after(first, home)
         attn_parts.append([first, terms])
-    home = after(home, attn_parts[-1][0])
+    home = exchange(after(home, attn_parts[-1][0]), "tp")
+    home = home.reshape(tokens, -1).astype(jnp.float32)
+    own = (grad_one + home).astype(jnp.bfloat16)
+    arrived = from_behind(own, "section", -1)
     for c, (mine, terms) in enumerate(attn_parts):
         for step in range(2, seq + 1):
             total = lax.ppermute(mine, "seq", [(q, (q + 1) % seq) for q in range(seq)])
+            if c == 0 and step == 3:
+                total = after(total, own)
+            if c == CHUNKS - 1 and step == seq:
+                total = after(total, arrived)
             mine = lax.dynamic_index_in_dim(terms, (place - step) % seq, 0, keepdims=False)
             mine = mine.astype(jnp.float32) + total.astype(jnp.float32)
             mine = mine.astype(jnp.bfloat16)
@@ -282,9 +283,6 @@
         order.append(lax.dynamic_index_in_dim(attn_part, which, 0, keepdims=False))
     attn_part = jnp.concatenate(order, axis=0)
 
-    home = exchange(home, "tp").reshape(tokens, -1).astype(jnp.float32)
-    own = (grad_one + home).astype(jnp.bfloat16)
-    arrived = from_behind(own, "section", -1)
     input_zero = (arrived.astype(jnp.float32) + branch + home).astype(jnp.bfloat16)
     input_part = jnp.where(upstream, input_zero, own)
     return (attn_part[None], input_part[None])

time: 238 us -> 221 us (0.929)
  blocking collectives: 18.3 us -> 0 us
  Pallas kernels: 11.7 us -> 14.9 us
  local copies, waits for them, and re-layouts: 12.3 us -> 9.13 us
    psum x1 -> x0, blocking collectives: 18.3 us -> none  [norm_backward(): lax.psum((jnp.sum(values * values, axis=-1), jnp.sum(gain * kv_share * va...]
    ppermute x4, waiting for transfers between devices: 28.2 us -> 40 us  [spread(): moved = lax.ppermute(piece, ('seq', 'tp'), route)]
    ppermute x3, waiting for transfers between devices: 23.3 us -> 14.4 us  [from_behind(): return lax.ppermute(block, axis, route)]
    ppermute x4, waiting for transfers between devices: 12.4 us -> 4.71 us  [over_rows(): lax.ppermute(block, 'tp', [(t, (t + turn * CORES) % tp) for t in range(tp)])]
    ppermute x3 -> x6, waiting for transfers between devices: 14.1 us -> 19.5 us  [gather_seq(): arrived.append(lax.ppermute(block, 'seq', route))]
    pallas_call x2, Pallas kernels: 11.7 us -> 14.9 us  [product(): pl.pallas_call(product_kernel, out_shape=jax.ShapeDtypeStruct((seq, n, de...]
    ppermute x6, waiting for transfers between devices: 45.5 us -> 42.6 us  [body(): total = lax.ppermute(mine, 'seq', [(q, (q + 1) % seq) for q in range(seq)])]
    ppermute x3 -> x6, starting transfers between devices: 5.98 us -> 8.89 us  [gather_seq(): arrived.append(lax.ppermute(block, 'seq', route))]
  transfers between devices with their start and end apart: 29 -> 32, of which waited for: 17 -> 20; matrix products, arithmetic and copies ran while one was open for 13% -> 14% of each run, Pallas kernels for 5% -> 7%
where the time goes in v3:
time: 221 us; the launch traced here: 219 us
  waiting for transfers between devices  126 us (57%)
  starting transfers between devices  34.1 us (15%)
  other arithmetic  28.9 us (13%)
  Pallas kernels  14.9 us (7%)
  local copies, waits for them, and re-layouts  9.13 us (4%)
  matrix products  5.72 us (3%)
    ppermute x6, waiting for transfers between devices, body(): total = lax.ppermute(mine, 'seq', [(q, (q + 1) % seq) for q in range(seq)])  42.6 us
    ppermute x4, waiting for transfers between devices, spread(): moved = lax.ppermute(piece, ('seq', 'tp'), route)  40 us
    ppermute x6, waiting for transfers between devices, gather_seq(): arrived.append(lax.ppermute(block, 'seq', route))  19.5 us
    pallas_call x2, Pallas kernels, product(): pl.pallas_call(product_kernel, out_shape=jax.ShapeDtypeStruct((seq, n, de...  14.9 us
    ppermute x3, waiting for transfers between devices, from_behind(): return lax.ppermute(block, axis, route)  14.4 us
    convert_element_type x6, other arithmetic, body(): mine = mine.astype(jnp.bfloat16)  10.7 us
    ppermute x6, starting transfers between devices, gather_seq(): arrived.append(lax.ppermute(block, 'seq', route))  8.89 us
    all_to_all x2, starting transfers between devices, exchange(): return lax.all_to_all(block, axis, 0, 0)  8.52 us
  transfers between devices with their start and end apart: 32, of which 20 were waited for; matrix products, arithmetic and copies ran while one was open for 14% of the time, Pallas kernels for 7%

profile of v3, /device:TPU:0, one launch (start us, length us, event | category | flops | bytes accessed | tf_op | source)
XLA Modules:
  0.0 219.5 jit_solution(16718385240186746486)
XLA Ops:
  5.9 4.0 %collective-permute-start.2 = (bf16[2,64,1024]{2,1,0:T(8,128)(2,1)}, bf16[2,64,1024]{2,1,0:T(8,128)(2,1)}, u32[]{:S(2)}, u32[]{:S(2)}) collective-permute-start(bf16[2,64,1024]{2,1,0:T(8,128)(2,1)} %pad_maximum_fusion.2), channel_id=1, source_target_pairs={{0,8},{4,12},{8,0},{12,4},{1,9},{5,13},{9,1},{13,5},{2,10},{6,14},... | collective-permute-start | bytes 786440 | tf_op jit(solution)/shard_map/ppermute | solution.py:131
  14.4 8.7 %collective-permute-done.2 = bf16[2,64,1024]{2,1,0:T(8,128)(2,1)} collective-permute-done((bf16[2,64,1024]{2,1,0:T(8,128)(2,1)}, bf16[2,64,1024]{2,1,0:T(8,128)(2,1)}, u32[]{:S(2)}, u32[]{:S(2)}) %collective-permute-start.2) | collective-permute-done | bytes 262176 | tf_op jit(solution)/shard_map/ppermute | solution.py:131
  23.8 5.4 %collective-permute-done.1 = bf16[2,64,1024]{2,1,0:T(8,128)(2,1)} collective-permute-done((bf16[2,64,1024]{2,1,0:T(8,128)(2,1)}, bf16[2,64,1024]{2,1,0:T(8,128)(2,1)}, u32[]{:S(2)}, u32[]{:S(2)}) %collective-permute-start.1) | collective-permute-done | bytes 262176 | tf_op jit(solution)/shard_map/ppermute | solution.py:131
  32.2 2.9 %fusion.2 = bf16[4,64,2048]{2,1,0:T(8,128)(2,1)S(1)} fusion(bf16[512,2048]{1,0:T(8,128)(2,1)} %collective-permute-done.4, bf16[512,2048]{1,0:T(8,128)(2,1)S(1)} %bitcast.163, bf16[4,2,64,1024]{3,2,0,1:T(8,128)(2,1)S(1)} %pad_maximum_fusion.1, s32[]{:T(128)S(6)} %select_n.639), kind=kOutput, calls=%fused_computation.20 | convolution fusion | flops 1082654720 | bytes 5767172 | tf_op jit(solution)/shard_map/dot_general | solution.py:214
  35.1 2.4 %collective-permute-done.5 = bf16[2,2,64,2048]{3,2,1,0:T(8,128)(2,1)S(1)} collective-permute-done((bf16[2,2,64,2048]{3,2,1,0:T(8,128)(2,1)}, bf16[2,2,64,2048]{3,2,1,0:T(8,128)(2,1)S(1)}, u32[]{:S(2)}, u32[]{:S(2)}) %collective-permute-start.5) | collective-permute-done | bytes 1048608 | tf_op jit(solution)/shard_map/ppermute | solution.py:34
  37.7 4.4 %collective-permute-start.9 = (bf16[2,64,2048]{2,1,0:T(8,128)(2,1)S(1)}, bf16[2,64,2048]{2,1,0:T(8,128)(2,1)S(1)}, u32[]{:S(2)}, u32[]{:S(2)}) collective-permute-start(bf16[2,64,2048]{2,1,0:T(8,128)(2,1)S(1)} %get-tuple-element.29), channel_id=1, source_target_pairs={{0,9},{1,13},{2,11},{3,15},{4,8},{5,12},{6,10},{7,14},{8,1},{9,5},... | collective-permute-start | bytes 1572872 | tf_op jit(solution)/shard_map/ppermute | solution.py:92
  45.1 2.9 %fusion.1 = f32[4,64,2048]{2,1,0:T(8,128)S(1)} fusion(bf16[512,2048]{1,0:T(8,128)(2,1)} %collective-permute-done.4, bf16[512,2048]{1,0:T(8,128)(2,1)S(1)} %bitcast.164, bf16[4,2,64,1024]{3,2,0,1:T(8,128)(2,1)S(1)} %pad_maximum_fusion.1, s32[]{:T(128)S(6)} %select_n.622), kind=kOutput, calls=%fused_computation.15 | convolution fusion | flops 1082130432 | bytes 6815748 | tf_op jit(solution)/shard_map/dot_general | solution.py:214
  48.0 6.5 %collective-permute-done.9 = bf16[2,64,2048]{2,1,0:T(8,128)(2,1)S(1)} collective-permute-done((bf16[2,64,2048]{2,1,0:T(8,128)(2,1)S(1)}, bf16[2,64,2048]{2,1,0:T(8,128)(2,1)S(1)}, u32[]{:S(2)}, u32[]{:S(2)}) %collective-permute-start.9) | collective-permute-done | bytes 524320 | tf_op jit(solution)/shard_map/ppermute | solution.py:92
  55.8 32.2 %collective-permute-done.8 = bf16[2,64,2048]{2,1,0:T(8,128)(2,1)S(1)} collective-permute-done((bf16[2,64,2048]{2,1,0:T(8,128)(2,1)S(1)}, bf16[2,64,2048]{2,1,0:T(8,128)(2,1)S(1)}, u32[]{:S(2)}, u32[]{:S(2)}) %collective-permute-start.8) | collective-permute-done | bytes 524320 | tf_op jit(solution)/shard_map/ppermute | solution.py:92
  89.5 2.8 %collective-permute-start.14 = (f32[2,4,64]{2,1,0:T(4,128)S(1)}, f32[2,4,64]{2,1,0:T(4,128)S(1)}, u32[]{:S(2)}, u32[]{:S(2)}) collective-permute-start(f32[2,4,64]{2,1,0:T(4,128)S(1)} %pad_maximum_fusion.3), channel_id=1, source_target_pairs={{0,12},{4,0},{8,4},{12,8},{1,13},{5,1},{9,5},{13,9},{2,14},{6,2},{... | collective-permute-start | bytes 6152 | tf_op jit(solution)/shard_map/ppermute | solution.py:131
  93.9 3.8 %collective-permute-done.12 = f32[2,4,64]{2,1,0:T(4,128)S(1)} collective-permute-done((f32[2,4,64]{2,1,0:T(4,128)S(1)}, f32[2,4,64]{2,1,0:T(4,128)S(1)}, u32[]{:S(2)}, u32[]{:S(2)}) %collective-permute-start.12) | collective-permute-done | bytes 2080 | tf_op jit(solution)/shard_map/ppermute | solution.py:131
  101.1 11.1 %collective-permute-done.15 = bf16[4,32,2048]{2,1,0:T(8,128)(2,1)S(1)} collective-permute-done((bf16[4,32,2048]{2,1,0:T(8,128)(2,1)S(1)}, bf16[4,32,2048]{2,1,0:T(8,128)(2,1)S(1)}, u32[]{:S(2)}, u32[]{:S(2)}) %collective-permute-start.15) | collective-permute-done | bytes 524320 | tf_op jit(solution)/shard_map/ppermute | solution.py:19
  115.4 4.3 %all-to-all-start = ((bf16[4,64,2048]{2,1,0:T(8,128)(2,1)}), bf16[4,64,2048]{2,1,0:T(8,128)(2,1)}, u32[]{:S(2)}, u32[]{:S(2)}) async-start(bf16[4,64,2048]{2,1,0:T(8,128)(2,1)} %get-tuple-element.15), calls=%async_computation | async-start | bytes 2097152 | tf_op jit(solution)/shard_map/all_to_all | solution.py:43
  122.1 3.3 %collective-permute-done.21 = bf16[4,32,2048]{2,1,0:T(8,128)(2,1)S(1)} collective-permute-done((bf16[4,32,2048]{2,1,0:T(8,128)(2,1)S(1)}, bf16[4,32,2048]{2,1,0:T(8,128)(2,1)S(1)}, u32[]{:S(2)}, u32[]{:S(2)}) %collective-permute-start.21) | collective-permute-done | bytes 524320 | tf_op jit(solution)/shard_map/ppermute | solution.py:19
  131.7 7.3 %shard_map.86 = bf16[4,4,32,2048]{3,2,1,0:T(8,128)(2,1)S(1)} custom-call(bf16[4,32,2048]{2,1,0:T(8,128)(2,1)S(1)} %fusion.22.refs_0_, bf16[4,32,2048]{2,1,0:T(8,128)(2,1)S(1)} %copy-done.4, bf16[4,32,2048]{2,1,0:T(8,128)(2,1)S(1)} %copy-done.2, bf16[4,32,2048]{2,1,0:T(8,128)(2,1)S(1)} %copy-done.6, bf16[2048,2048]{1,0:T(8,128)(2,1)} %bitcast.160), custom_call_target="tpu_custom_call" | custom-call | flops 4294967296 | bytes 10485760 | tf_op jit(solution)/shard_map/pallas_call | solution.py:172
  143.6 7.6 %shard_map.87 = bf16[4,4,32,2048]{3,2,1,0:T(8,128)(2,1)S(1)} custom-call(bf16[4,32,2048]{2,1,0:T(8,128)(2,1)S(1)} %fusion.23.refs_0_, bf16[4,32,2048]{2,1,0:T(8,128)(2,1)} %collective-permute-done.22.refs_1_, bf16[4,32,2048]{2,1,0:T(8,128)(2,1)} %collective-permute-done.23.refs_2_, bf16[4,32,2048]{2,1,0:T(8,128)(2,1)S(1)} %collective-permute-done.24.refs_3_, ...), custom_call_target="tpu_custom_call" | custom-call | flops 4294967296 | bytes 10485760 | tf_op jit(solution)/shard_map/pallas_call | solution.py:172
  153.4 4.2 %all-to-all-start.1 = ((bf16[4,64,2048]{2,1,0:T(8,128)(2,1)}), bf16[4,64,2048]{2,1,0:T(8,128)(2,1)}, u32[]{:S(2)}, u32[]{:S(2)}) async-start(bf16[4,64,2048]{2,1,0:T(8,128)(2,1)} %all-to-all-done), calls=%async_computation.1 | async-start | bytes 2097152 | tf_op jit(solution)/shard_map/all_to_all | solution.py:43
  160.3 9.9 %collective-permute-done.26 = bf16[4,32,2048]{2,1,0:T(8,128)(2,1)} collective-permute-done((bf16[4,32,2048]{2,1,0:T(8,128)(2,1)}, bf16[4,32,2048]{2,1,0:T(8,128)(2,1)}, u32[]{:S(2)}, u32[]{:S(2)}) %collective-permute-start.26) | collective-permute-done | bytes 524320 | tf_op jit(solution)/shard_map/ppermute | solution.py:270
  172.4 3.1 %fusion.3 = bf16[256,2048]{1,0:T(8,128)(2,1)} fusion(bf16[256,2048]{1,0:T(8,128)(2,1)S(1)} %copy-done.8, bf16[4,64,2048]{2,1,0:T(8,128)(2,1)} %all-to-all-done.1, bf16[1,256,2048]{2,1,0:T(8,128)(2,1)} %param.11), kind=kLoop, calls=%fused_computation.21 | loop fusion | flops 3145728 | bytes 4194304 | tf_op jit(solution)/shard_map/convert_element_type | solution.py:266
  176.7 4.8 %collective-permute-done.20 = bf16[4,32,2048]{2,1,0:T(8,128)(2,1)} collective-permute-done((bf16[4,32,2048]{2,1,0:T(8,128)(2,1)}, bf16[4,32,2048]{2,1,0:T(8,128)(2,1)}, u32[]{:S(2)}, u32[]{:S(2)}) %collective-permute-start.20) | collective-permute-done | bytes 524320 | tf_op jit(solution)/shard_map/ppermute | solution.py:270
  183.5 9.3 %collective-permute-done.27 = bf16[4,32,2048]{2,1,0:T(8,128)(2,1)} collective-permute-done((bf16[4,32,2048]{2,1,0:T(8,128)(2,1)}, bf16[4,32,2048]{2,1,0:T(8,128)(2,1)}, u32[]{:S(2)}, u32[]{:S(2)}) %collective-permute-start.27) | collective-permute-done | bytes 524320 | tf_op jit(solution)/shard_map/ppermute | solution.py:270
  194.9 9.1 %collective-permute-done.25 = bf16[4,32,2048]{2,1,0:T(8,128)(2,1)} collective-permute-done((bf16[4,32,2048]{2,1,0:T(8,128)(2,1)}, bf16[4,32,2048]{2,1,0:T(8,128)(2,1)}, u32[]{:S(2)}, u32[]{:S(2)}) %collective-permute-start.25) | collective-permute-done | bytes 524320 | tf_op jit(solution)/shard_map/ppermute | solution.py:270
  205.1 9.2 %collective-permute-done.28 = bf16[4,32,2048]{2,1,0:T(8,128)(2,1)} collective-permute-done((bf16[4,32,2048]{2,1,0:T(8,128)(2,1)}, bf16[4,32,2048]{2,1,0:T(8,128)(2,1)}, u32[]{:S(2)}, u32[]{:S(2)}) %collective-permute-start.28) | collective-permute-done | bytes 524320 | tf_op jit(solution)/shard_map/ppermute | solution.py:270
  215.8 3.6 %fusion.13 = (bf16[1,256,2048]{2,1,0:T(8,128)(2,1)}, bf16[1,256,2048]{2,1,0:T(8,128)(2,1)}) fusion(bf16[256,2048]{1,0:T(8,128)(2,1)} %collective-permute-done.29, bf16[4,64,2048]{2,1,0:T(8,128)(2,1)} %all-to-all-done.1, bf16[1,256,2048]{2,1,0:T(8,128)(2,1)S(1)} %copy-done.9, pred[]{:T(512)S(6)} %eq.64, bf16[256,2048]{1,0:T(8,128)(2,1)S(1)} %copy-done.8, ...), kind=kLoop, calls=%fused_computation.42 | loop fusion | flops 9961472 | bytes 7340033 | tf_op jit(solution)/shard_map/broadcast_in_dim | solution.py:288
  (104 shorter events, 55.8 us)
Async XLA Ops:
  0.6 31.4 %collective-permute-start.4 = (bf16[512,2048]{1,0:T(8,128)(2,1)}, bf16[512,2048]{1,0:T(8,128)(2,1)}, u32[]{:S(2)}, u32[]{:S(2)}) collective-permute-start(bf16[512,2048]{1,0:T(8,128)(2,1)} %bitcast.162), channel_id=1, source_target_pairs={{0,1},{1,0},{2,3},{3,2},{4,5},{5,4},{6,7},{7,6},{8,9},{9,8},{10,11... | collective-permute-start | bytes 6291464 | tf_op jit(solution)/shard_map/ppermute | solution.py:39
  5.9 17.2 %collective-permute-start.2 = (bf16[2,64,1024]{2,1,0:T(8,128)(2,1)}, bf16[2,64,1024]{2,1,0:T(8,128)(2,1)}, u32[]{:S(2)}, u32[]{:S(2)}) collective-permute-start(bf16[2,64,1024]{2,1,0:T(8,128)(2,1)} %pad_maximum_fusion.2), channel_id=1, source_target_pairs={{0,8},{4,12},{8,0},{12,4},{1,9},{5,13},{9,1},{13,5},{2,10},{6,14},... | collective-permute-start | bytes 786440 | tf_op jit(solution)/shard_map/ppermute | solution.py:131
  9.8 13.9 %collective-permute-start.3 = (bf16[2,64,1024]{2,1,0:T(8,128)(2,1)}, bf16[2,64,1024]{2,1,0:T(8,128)(2,1)}, u32[]{:S(2)}, u32[]{:S(2)}) collective-permute-start(bf16[2,64,1024]{2,1,0:T(8,128)(2,1)} %pad_maximum_fusion.2), channel_id=1, source_target_pairs={{0,12},{4,0},{8,4},{12,8},{1,13},{5,1},{9,5},{13,9},{2,14},{6,2},{... | collective-permute-start | bytes 786440 | tf_op jit(solution)/shard_map/ppermute | solution.py:131
  11.2 18.0 %collective-permute-start.1 = (bf16[2,64,1024]{2,1,0:T(8,128)(2,1)}, bf16[2,64,1024]{2,1,0:T(8,128)(2,1)}, u32[]{:S(2)}, u32[]{:S(2)}) collective-permute-start(bf16[2,64,1024]{2,1,0:T(8,128)(2,1)} %pad_maximum_fusion.2), channel_id=1, source_target_pairs={{0,4},{4,8},{8,12},{12,0},{1,5},{5,9},{9,13},{13,1},{2,6},{6,10},{... | collective-permute-start | bytes 786440 | tf_op jit(solution)/shard_map/ppermute | solution.py:131
  12.9 24.6 %collective-permute-start.5 = (bf16[2,2,64,2048]{3,2,1,0:T(8,128)(2,1)}, bf16[2,2,64,2048]{3,2,1,0:T(8,128)(2,1)S(1)}, u32[]{:S(2)}, u32[]{:S(2)}) collective-permute-start(bf16[2,2,64,2048]{3,2,1,0:T(8,128)(2,1)} %fusion.15), channel_id=1, source_target_pairs={{0,2},{1,3},{2,0},{3,1},{4,6},{5,7},{6,4},{7,5},{8,10},{9,11},{10,... | collective-permute-start | bytes 3145736 | tf_op jit(solution)/shard_map/ppermute | solution.py:34
  23.1 20.3 %collective-permute-start.10 = (f32[1,2048]{1,0:T(1,128)S(1)}, f32[1,2048]{1,0:T(1,128)S(1)}, u32[]{:S(2)}, u32[]{:S(2)}) collective-permute-start(f32[1,2048]{1,0:T(1,128)S(1)} %copy-done.11), channel_id=1, source_target_pairs={{1,4},{2,8},{3,12},{4,1},{6,9},{7,13},{8,2},{9,6},{11,14},{12,3},{... | collective-permute-start | bytes 24584 | tf_op jit(solution)/shard_map/ppermute | solution.py:120
  37.7 16.8 %collective-permute-start.9 = (bf16[2,64,2048]{2,1,0:T(8,128)(2,1)S(1)}, bf16[2,64,2048]{2,1,0:T(8,128)(2,1)S(1)}, u32[]{:S(2)}, u32[]{:S(2)}) collective-permute-start(bf16[2,64,2048]{2,1,0:T(8,128)(2,1)S(1)} %get-tuple-element.29), channel_id=1, source_target_pairs={{0,9},{1,13},{2,11},{3,15},{4,8},{5,12},{6,10},{7,14},{8,1},{9,5},... | collective-permute-start | bytes 1572872 | tf_op jit(solution)/shard_map/ppermute | solution.py:92
  42.1 13.8 %collective-permute-start.7 = (bf16[2,64,2048]{2,1,0:T(8,128)(2,1)S(1)}, bf16[2,64,2048]{2,1,0:T(8,128)(2,1)S(1)}, u32[]{:S(2)}, u32[]{:S(2)}) collective-permute-start(bf16[2,64,2048]{2,1,0:T(8,128)(2,1)S(1)} %get-tuple-element.30), channel_id=1, source_target_pairs={{0,1},{1,5},{2,3},{3,7},{4,0},{5,4},{6,2},{7,6},{8,9},{9,13},{10,1... | collective-permute-start | bytes 1572872 | tf_op jit(solution)/shard_map/ppermute | solution.py:92
  42.1 13.8 %collective-permute-start.6 = (bf16[2,64,2048]{2,1,0:T(8,128)(2,1)S(1)}, bf16[2,64,2048]{2,1,0:T(8,128)(2,1)S(1)}, u32[]{:S(2)}, u32[]{:S(2)}) collective-permute-start(bf16[2,64,2048]{2,1,0:T(8,128)(2,1)S(1)} %get-tuple-element.28), channel_id=1, source_target_pairs={{1,4},{3,6},{4,1},{6,3},{9,12},{11,14},{12,9},{14,11},{17,20},{19,... | collective-permute-start | bytes 1572872 | tf_op jit(solution)/shard_map/ppermute | solution.py:92
  42.9 45.2 %collective-permute-start.8 = (bf16[2,64,2048]{2,1,0:T(8,128)(2,1)S(1)}, bf16[2,64,2048]{2,1,0:T(8,128)(2,1)S(1)}, u32[]{:S(2)}, u32[]{:S(2)}) collective-permute-start(bf16[2,64,2048]{2,1,0:T(8,128)(2,1)S(1)} %fusion.35), channel_id=1, source_target_pairs={{0,8},{1,12},{2,10},{3,14},{4,9},{5,13},{6,11},{7,15},{8,0},{9,4},... | collective-permute-start | bytes 1572872 | tf_op jit(solution)/shard_map/ppermute | solution.py:92
  43.4 45.3 %collective-permute-start.11 = (bf16[4,64,2048]{2,1,0:T(8,128)(2,1)S(1)}, bf16[4,64,2048]{2,1,0:T(8,128)(2,1)S(1)}, u32[]{:S(2)}, u32[]{:S(2)}) collective-permute-start(bf16[4,64,2048]{2,1,0:T(8,128)(2,1)S(1)} %fusion.2), channel_id=1, source_target_pairs={{0,2},{1,3},{2,0},{3,1},{4,6},{5,7},{6,4},{7,5},{8,10},{9,11},{10,... | collective-permute-start | bytes 3145736 | tf_op jit(solution)/shard_map/ppermute | solution.py:34
  99.7 12.5 %collective-permute-start.15 = (bf16[4,32,2048]{2,1,0:T(8,128)(2,1)S(1)}, bf16[4,32,2048]{2,1,0:T(8,128)(2,1)S(1)}, u32[]{:S(2)}, u32[]{:S(2)}) collective-permute-start(bf16[4,32,2048]{2,1,0:T(8,128)(2,1)S(1)} %get-tuple-element.39), channel_id=1, source_target_pairs={{16,0},{17,1},{18,2},{19,3},{20,4},{21,5},{22,6},{23,7},{24,8},{25... | collective-permute-start | bytes 1572872 | tf_op jit(solution)/shard_map/ppermute | solution.py:19
  114.1 11.3 %collective-permute-start.21 = (bf16[4,32,2048]{2,1,0:T(8,128)(2,1)S(1)}, bf16[4,32,2048]{2,1,0:T(8,128)(2,1)S(1)}, u32[]{:S(2)}, u32[]{:S(2)}) collective-permute-start(bf16[4,32,2048]{2,1,0:T(8,128)(2,1)S(1)} %get-tuple-element.38), channel_id=1, source_target_pairs={{16,0},{17,1},{18,2},{19,3},{20,4},{21,5},{22,6},{23,7},{24,8},{25... | collective-permute-start | bytes 1572872 | tf_op jit(solution)/shard_map/ppermute | solution.py:19
  115.4 26.1 %all-to-all-start = ((bf16[4,64,2048]{2,1,0:T(8,128)(2,1)}), bf16[4,64,2048]{2,1,0:T(8,128)(2,1)}, u32[]{:S(2)}, u32[]{:S(2)}) async-start(bf16[4,64,2048]{2,1,0:T(8,128)(2,1)} %get-tuple-element.15), calls=%async_computation | async-start | bytes 2097152 | tf_op jit(solution)/shard_map/all_to_all | solution.py:43
  126.6 14.9 %collective-permute-start.23 = (bf16[4,32,2048]{2,1,0:T(8,128)(2,1)S(1)}, bf16[4,32,2048]{2,1,0:T(8,128)(2,1)}, u32[]{:S(2)}, u32[]{:S(2)}) collective-permute-start(bf16[4,32,2048]{2,1,0:T(8,128)(2,1)S(1)} %fusion.23.refs_0_), channel_id=1, source_target_pairs={{0,2},{1,3},{2,0},{3,1},{4,6},{5,7},{6,4},{7,5},{8,10},{9,11},{10,... | collective-permute-start | bytes 1572872 | tf_op jit(solution)/shard_map/ppermute | solution.py:34
  127.0 14.5 %collective-permute-start.22 = (bf16[4,32,2048]{2,1,0:T(8,128)(2,1)S(1)}, bf16[4,32,2048]{2,1,0:T(8,128)(2,1)}, u32[]{:S(2)}, u32[]{:S(2)}) collective-permute-start(bf16[4,32,2048]{2,1,0:T(8,128)(2,1)S(1)} %fusion.23.refs_0_), channel_id=1, source_target_pairs={{0,1},{1,0},{2,3},{3,2},{4,5},{5,4},{6,7},{7,6},{8,9},{9,8},{10,11... | collective-permute-start | bytes 1572872 | tf_op jit(solution)/shard_map/ppermute | solution.py:39
  141.5 16.5 %collective-permute-start.19 = (bf16[4,32,2048]{2,1,0:T(8,128)(2,1)}, bf16[4,32,2048]{2,1,0:T(8,128)(2,1)}, u32[]{:S(2)}, u32[]{:S(2)}) collective-permute-start(bf16[4,32,2048]{2,1,0:T(8,128)(2,1)} %dynamic-slice_bitcast_fusion.1), channel_id=1, source_target_pairs={{0,4},{4,8},{8,12},{12,0},{1,5},{5,9},{9,13},{13,1},{2,6},{6,10},{... | collective-permute-start | bytes 1572872 | tf_op jit(solution)/shard_map/ppermute | solution.py:270
  153.4 16.9 %collective-permute-start.26 = (bf16[4,32,2048]{2,1,0:T(8,128)(2,1)}, bf16[4,32,2048]{2,1,0:T(8,128)(2,1)}, u32[]{:S(2)}, u32[]{:S(2)}) collective-permute-start(bf16[4,32,2048]{2,1,0:T(8,128)(2,1)} %dynamic-slice_bitcast_fusion), channel_id=1, source_target_pairs={{0,4},{4,8},{8,12},{12,0},{1,5},{5,9},{9,13},{13,1},{2,6},{6,10},{... | collective-permute-start | bytes 1572872 | tf_op jit(solution)/shard_map/ppermute | solution.py:270
  153.4 19.0 %all-to-all-start.1 = ((bf16[4,64,2048]{2,1,0:T(8,128)(2,1)}), bf16[4,64,2048]{2,1,0:T(8,128)(2,1)}, u32[]{:S(2)}, u32[]{:S(2)}) async-start(bf16[4,64,2048]{2,1,0:T(8,128)(2,1)} %all-to-all-done), calls=%async_computation.1 | async-start | bytes 2097152 | tf_op jit(solution)/shard_map/all_to_all | solution.py:43
  159.9 21.6 %collective-permute-start.20 = (bf16[4,32,2048]{2,1,0:T(8,128)(2,1)}, bf16[4,32,2048]{2,1,0:T(8,128)(2,1)}, u32[]{:S(2)}, u32[]{:S(2)}) collective-permute-start(bf16[4,32,2048]{2,1,0:T(8,128)(2,1)} %fusion.19), channel_id=1, source_target_pairs={{0,4},{4,8},{8,12},{12,0},{1,5},{5,9},{9,13},{13,1},{2,6},{6,10},{... | collective-permute-start | bytes 1572872 | tf_op jit(solution)/shard_map/ppermute | solution.py:270
  172.4 20.3 %collective-permute-start.27 = (bf16[4,32,2048]{2,1,0:T(8,128)(2,1)}, bf16[4,32,2048]{2,1,0:T(8,128)(2,1)}, u32[]{:S(2)}, u32[]{:S(2)}) collective-permute-start(bf16[4,32,2048]{2,1,0:T(8,128)(2,1)} %fusion.16), channel_id=1, source_target_pairs={{0,4},{4,8},{8,12},{12,0},{1,5},{5,9},{9,13},{13,1},{2,6},{6,10},{... | collective-permute-start | bytes 1572872 | tf_op jit(solution)/shard_map/ppermute | solution.py:270
  175.4 38.9 %collective-permute-start.29 = (bf16[256,2048]{1,0:T(8,128)(2,1)}, bf16[256,2048]{1,0:T(8,128)(2,1)}, u32[]{:S(2)}, u32[]{:S(2)}) collective-permute-start(bf16[256,2048]{1,0:T(8,128)(2,1)} %fusion.3), channel_id=1, source_target_pairs={{16,0},{17,1},{18,2},{19,3},{20,4},{21,5},{22,6},{23,7},{24,8},{25... | collective-permute-start | bytes 3145736 | tf_op jit(solution)/shard_map/ppermute | solution.py:19
  183.4 20.5 %collective-permute-start.25 = (bf16[4,32,2048]{2,1,0:T(8,128)(2,1)}, bf16[4,32,2048]{2,1,0:T(8,128)(2,1)}, u32[]{:S(2)}, u32[]{:S(2)}) collective-permute-start(bf16[4,32,2048]{2,1,0:T(8,128)(2,1)} %fusion.20), channel_id=1, source_target_pairs={{0,4},{4,8},{8,12},{12,0},{1,5},{5,9},{9,13},{13,1},{2,6},{6,10},{... | collective-permute-start | bytes 1572872 | tf_op jit(solution)/shard_map/ppermute | solution.py:270
  194.8 19.5 %collective-permute-start.28 = (bf16[4,32,2048]{2,1,0:T(8,128)(2,1)}, bf16[4,32,2048]{2,1,0:T(8,128)(2,1)}, u32[]{:S(2)}, u32[]{:S(2)}) collective-permute-start(bf16[4,32,2048]{2,1,0:T(8,128)(2,1)} %fusion.17), channel_id=1, source_target_pairs={{0,4},{4,8},{8,12},{12,0},{1,5},{5,9},{9,13},{13,1},{2,6},{6,10},{... | collective-permute-start | bytes 1572872 | tf_op jit(solution)/shard_map/ppermute | solution.py:270
  (21 other events, 121.8 us)

commit v4 on v3

--- a/solution.py
+++ b/solution.py
@@ -93,8 +93,11 @@
         if j == 0:
             moved = jnp.where(core == place % CORES, piece, moved)
         arrived.append(moved)
-    slot = place // CORES * CORES + core
-    return jnp.stack([lax.select_n(slot ^ q, *arrived) for q in range(seq)], axis=0)
+    return arrived, place // CORES * CORES + core
+
+
+def collect(arrived, slot):
+    return jnp.stack([lax.select_n(slot ^ q, *arrived) for q in range(len(arrived))], axis=0)
 
 
 def mix_features(block):
@@ -124,18 +127,26 @@
 
 def gather_seq(block):
     seq = lax.axis_size("seq")
-    place = lax.axis_index("seq")
     arrived = [block]
     for turn in range(1, seq):
         route = [(q, (q + turn) % seq) for q in range(seq)]
         arrived.append(lax.ppermute(block, "seq", route))
+    return arrived
+
+
+def by_place(arrived):
+    seq = len(arrived)
+    place = lax.axis_index("seq")
     return jnp.stack([lax.select_n((place - q) % seq, *arrived) for q in range(seq)], axis=0)
 
 
-def norm_backward(values, gain, kv_share):
-    sums = jnp.stack([jnp.sum(values * values, axis=-1), jnp.sum(gain * kv_share * values, axis=-1)])
+def local_sums(values, gain, kv_share):
+    return jnp.stack([jnp.sum(values * values, axis=-1), jnp.sum(gain * kv_share * values, axis=-1)])
+
+
+def norm_backward(values, gain, kv_share, sums):
     short = lax.axis_size("seq") <= 2 * CORES
-    squares, intersection = jnp.sum(gather_seq(sums), axis=0) if short else lax.psum(sums, "seq")
+    squares, intersection = jnp.sum(by_place(gather_seq(sums)), axis=0) if short else lax.psum(sums, "seq")
     inv_rms = lax.rsqrt(squares / D + epsilon)[..., None]
     return (
         inv_rms * gain * kv_share
@@ -200,12 +211,15 @@
     kept = lax.dynamic_index_in_dim(mixed, core, 1, keepdims=False)
     given = lax.dynamic_index_in_dim(mixed, 1 - core, 1, keepdims=False)
     given = over_cores(given)
-    cotangent = gather_seq(jnp.concatenate([kept, given], axis=2))
-    weights = jnp.concatenate([kv_weight[0], over_cores(kv_weight[0])], axis=0)
+    arrived = gather_seq(jnp.concatenate([kept, given], axis=2))
+    cotangent = by_place(arrived)
+    other = over_cores(kv_weight[0])
+    weights = jnp.concatenate([kv_weight[0], other], axis=0)
 
     branch = mlp_grads[0].astype(jnp.float32)
     grad_one = output_cotangent.astype(jnp.float32) + branch
-    base_home = jnp.where(upstream, mlp_grads[0], grad_one.astype(jnp.bfloat16))
+    behind = from_behind(mlp_grads[0], "section", -1)
+    by_permutes = seq == tp == 2 * CORES
     gain = gain_slab(norm_gain)
     width = gain.shape[1]
 
@@ -217,40 +231,43 @@
         return terms.reshape(seq, tokens // tp, width)
 
     given = [kv_of(turn).astype(jnp.bfloat16) for turn in range(1, row)]
-    blocks = [layer_input[0], base_home]
-    if seq == tp == 2 * CORES:
-        near, far = slabs_by_permutes(blocks)
-        far = after(far, *given)
-        slabs = spread(near, far)
+    residual = jnp.where(upstream, grad_one + after(behind, *given).astype(jnp.float32), grad_one)
+    residual = after(residual.astype(jnp.bfloat16), *given)
+    if by_permutes:
+        near, far = slabs_by_permutes([layer_input[0]])
+        values = collect(*spread(near, after(far, *given)))[:, 0]
     else:
-        slabs = to_slabs(mix_tokens(blocks))
+        values = to_slabs(mix_tokens([layer_input[0]]))[:, 0]
     given = [over_rows(terms, turn) for turn, terms in enumerate(given, 1)]
-    kv_share, slabs = lax.optimization_barrier((kv_of(0), slabs))
-    values, base = slabs[:, 0], slabs[:, 1]
+    kv_share, values = lax.optimization_barrier((kv_of(0), values))
     for terms in given:
         kv_share = kv_share + terms.astype(jnp.float32)
-
-    norm_back = norm_backward(values.astype(jnp.float32), gain, kv_share)
-    input_one = (base.astype(jnp.float32) + norm_back).astype(jnp.bfloat16)
+    values = values.astype(jnp.float32)
+    sums = local_sums(values, gain, kv_share)
+    if by_permutes:
+        near, far = slabs_by_permutes([residual])
+        arrived, slot = spread(near, after(far, sums))
+    norm_back = norm_backward(values, gain, kv_share, sums).astype(jnp.bfloat16)
+    if by_permutes:
+        base = collect(arrived, after(slot, norm_back))[:, 0]
+    else:
+        base = to_slabs(mix_tokens([residual]))[:, 0]
 
     depth = tokens // tp // CHUNKS
 
     def cut(array, c):
         return array[:, c * depth : (c + 1) * depth]
 
-    leaving = [cut(input_one, c) for c in range(CHUNKS)]
+    leaving = [cut(norm_back, c) for c in range(CHUNKS)]
     arrivals = [from_behind(part, "section", -1) for part in leaving]
-    home = mix_features(after(norm_back.astype(jnp.bfloat16), leaving[-1]))
+    home = mix_features(after(norm_back, leaving[-1]))
+    arriving = jnp.concatenate(arrivals, axis=1).astype(jnp.float32)
+    grad_zero = arriving + base.astype(jnp.float32)
+    grad = jnp.where(upstream, grad_zero.astype(jnp.bfloat16), base)
     blocks_of = []
     for c in range(CHUNKS):
-        part = cut(base, c)
-        arriving = arrivals[c]
-        if c > 0:
-            arriving = after(arriving, blocks[-1])
-        grad_zero = arriving.astype(jnp.float32) + part.astype(jnp.float32)
-        grad = jnp.where(upstream, grad_zero.astype(jnp.bfloat16), part)
-        blocks = [over_rows(grad, turn) if turn else grad for turn in range(row)]
-        blocks_of.append(blocks)
+        part = cut(grad, c)
+        blocks_of.append([over_rows(part, turn) if turn else part for turn in range(row)])
     attn_parts = []
     for c, blocks in enumerate(blocks_of):
         if c > 0:
@@ -265,13 +282,15 @@
     home = home.reshape(tokens, -1).astype(jnp.float32)
     own = (grad_one + home).astype(jnp.bfloat16)
     arrived = from_behind(own, "section", -1)
+    input_zero = (arrived.astype(jnp.float32) + branch + home).astype(jnp.bfloat16)
+    input_part = jnp.where(upstream, input_zero, own)
     for c, (mine, terms) in enumerate(attn_parts):
         for step in range(2, seq + 1):
             total = lax.ppermute(mine, "seq", [(q, (q + 1) % seq) for q in range(seq)])
             if c == 0 and step == 3:
                 total = after(total, own)
             if c == CHUNKS - 1 and step == seq:
-                total = after(total, arrived)
+                total = after(total, input_part)
             mine = lax.dynamic_index_in_dim(terms, (place - step) % seq, 0, keepdims=False)
             mine = mine.astype(jnp.float32) + total.astype(jnp.float32)
             mine = mine.astype(jnp.bfloat16)
@@ -283,8 +302,6 @@
         order.append(lax.dynamic_index_in_dim(attn_part, which, 0, keepdims=False))
     attn_part = jnp.concatenate(order, axis=0)
 
-    input_zero = (arrived.astype(jnp.float32) + branch + home).astype(jnp.bfloat16)
-    input_part = jnp.where(upstream, input_zero, own)
     return (attn_part[None], input_part[None])
 
 

time: 221 us -> 221 us (level)
  starting transfers between devices: 34.1 us -> 58.9 us
  waiting for transfers between devices: 126 us -> 104 us
  other arithmetic: 28.9 us -> 21.9 us
  local copies, waits for them, and re-layouts: 9.13 us -> 13.3 us
    ppermute x4 -> x8, waiting for transfers between devices: 40 us -> 11.9 us  [spread(): moved = lax.ppermute(piece, ('seq', 'tp'), route)]
    ppermute x4 -> x8, starting transfers between devices: 5.63 us -> 18.3 us  [spread(): moved = lax.ppermute(piece, ('seq', 'tp'), route)]
    ppermute x3 -> x4, waiting for transfers between devices: 14.4 us -> 21.4 us  [from_behind(): return lax.ppermute(block, axis, route)]
    ppermute x6, starting transfers between devices: 8.89 us -> 15.1 us  [gather_seq(): arrived.append(lax.ppermute(block, 'seq', route))]
    ppermute x4 -> x5, waiting for transfers between devices: 4.71 us -> 9.84 us  [over_rows(): lax.ppermute(block, 'tp', [(t, (t + turn * CORES) % tp) for t in range(tp)])]
    ppermute x4 -> x5, starting transfers between devices: 5.41 us -> 9.25 us  [over_rows(): lax.ppermute(block, 'tp', [(t, (t + turn * CORES) % tp) for t in range(tp)])]
    ppermute x6, waiting for transfers between devices: 19.5 us -> 16.1 us  [gather_seq(): arrived.append(lax.ppermute(block, 'seq', route))]
    another operation x7 -> x8, other arithmetic: 3.55 us -> 0.88 us  [the longest x3 0.54 us: by_place(): jnp.stack([lax.select_n((place - q) % seq, *arrived) for q in range(seq)]...]
  transfers between devices with their start and end apart: 32 -> 38, of which waited for: 20 -> 18; matrix products, arithmetic and copies ran while one was open for 14% -> 14% of each run, Pallas kernels for 7% -> 7%
where the time goes in v4:
time: 221 us; the launch traced here: 220 us
  waiting for transfers between devices  104 us (47%)
  starting transfers between devices  58.9 us (27%)
  other arithmetic  21.9 us (10%)
  Pallas kernels  14.9 us (7%)
  local copies, waits for them, and re-layouts  13.3 us (6%)
  matrix products  5.72 us (3%)
    ppermute x6, waiting for transfers between devices, body(): total = lax.ppermute(mine, 'seq', [(q, (q + 1) % seq) for q in range(seq)])  40.1 us
    ppermute x4, waiting for transfers between devices, from_behind(): return lax.ppermute(block, axis, route)  21.4 us
    ppermute x8, starting transfers between devices, spread(): moved = lax.ppermute(piece, ('seq', 'tp'), route)  18.3 us
    ppermute x6, waiting for transfers between devices, gather_seq(): arrived.append(lax.ppermute(block, 'seq', route))  16.1 us
    ppermute x6, starting transfers between devices, gather_seq(): arrived.append(lax.ppermute(block, 'seq', route))  15.1 us
    pallas_call x2, Pallas kernels, product(): pl.pallas_call(product_kernel, out_shape=jax.ShapeDtypeStruct((seq, n, de...  14.9 us
    ppermute x8, waiting for transfers between devices, spread(): moved = lax.ppermute(piece, ('seq', 'tp'), route)  11.9 us
    ppermute x5, waiting for transfers between devices, over_rows(): lax.ppermute(block, 'tp', [(t, (t + turn * CORES) % tp) for t in range(tp)])  9.84 us
  transfers between devices with their start and end apart: 38, of which 18 were waited for; matrix products, arithmetic and copies ran while one was open for 14% of the time, Pallas kernels for 7%

profile of v4, /device:TPU:0, one launch (start us, length us, event | category | flops | bytes accessed | tf_op | source)
XLA Modules:
  0.0 219.8 jit_solution(7436126535896683301)
XLA Ops:
  3.4 3.0 %collective-permute-start.5 = (bf16[2,1,64,2048]{3,2,1,0:T(8,128)(2,1)S(1)}, bf16[2,1,64,2048]{3,2,1,0:T(8,128)(2,1)S(1)}, u32[]{:S(2)}, u32[]{:S(2)}) collective-permute-start(bf16[2,1,64,2048]{3,2,1,0:T(8,128)(2,1)S(1)} %dynamic-slice_bitcast_fusion.3), channel_id=1, source_target_pairs={{0,2},{1,3},{2,0},{3,1},{4,6},{5,7},{6,4},{7,5},{8,10},{9,11},{10,... | collective-permute-start | bytes 1572872 | tf_op jit(solution)/shard_map/ppermute | solution.py:34
  7.4 3.9 %collective-permute-start.2 = (bf16[2,64,1024]{2,1,0:T(8,128)(2,1)S(1)}, bf16[2,64,1024]{2,1,0:T(8,128)(2,1)S(1)}, u32[]{:S(2)}, u32[]{:S(2)}) collective-permute-start(bf16[2,64,1024]{2,1,0:T(8,128)(2,1)S(1)} %pad_maximum_fusion.1), channel_id=1, source_target_pairs={{0,8},{4,12},{8,0},{12,4},{1,9},{5,13},{9,1},{13,5},{2,10},{6,14},... | collective-permute-start | bytes 786440 | tf_op jit(solution)/shard_map/ppermute | solution.py:133
  13.4 11.3 %collective-permute-done.2 = bf16[2,64,1024]{2,1,0:T(8,128)(2,1)S(1)} collective-permute-done((bf16[2,64,1024]{2,1,0:T(8,128)(2,1)S(1)}, bf16[2,64,1024]{2,1,0:T(8,128)(2,1)S(1)}, u32[]{:S(2)}, u32[]{:S(2)}) %collective-permute-start.2) | collective-permute-done | bytes 262176 | tf_op jit(solution)/shard_map/ppermute | solution.py:133
  26.0 4.8 %collective-permute-done.3 = bf16[2,64,1024]{2,1,0:T(8,128)(2,1)S(1)} collective-permute-done((bf16[2,64,1024]{2,1,0:T(8,128)(2,1)S(1)}, bf16[2,64,1024]{2,1,0:T(8,128)(2,1)S(1)}, u32[]{:S(2)}, u32[]{:S(2)}) %collective-permute-start.3) | collective-permute-done | bytes 262176 | tf_op jit(solution)/shard_map/ppermute | solution.py:133
  32.6 2.9 %fusion.2 = bf16[4,64,2048]{2,1,0:T(8,128)(2,1)S(1)} fusion(bf16[512,2048]{1,0:T(8,128)(2,1)} %collective-permute-done.4, bf16[512,2048]{1,0:T(8,128)(2,1)S(1)} %bitcast.179, bf16[4,2,64,1024]{3,2,0,1:T(8,128)(2,1)S(1)} %pad_maximum_fusion, s32[]{:T(128)S(6)} %select_n.866), kind=kOutput, calls=%fused_computation.11 | convolution fusion | flops 1082654720 | bytes 5767172 | tf_op jit(solution)/shard_map/dot_general | solution.py:228
  38.5 5.5 %collective-permute-start.8 = (bf16[1,64,2048]{2,1,0:T(8,128)(2,1)S(1)}, bf16[1,64,2048]{2,1,0:T(8,128)(2,1)S(1)}, u32[]{:S(2)}, u32[]{:S(2)}) collective-permute-start(bf16[1,64,2048]{2,1,0:T(8,128)(2,1)S(1)} %get-tuple-element.40), channel_id=1, source_target_pairs={{0,8},{1,12},{2,10},{3,14},{4,9},{5,13},{6,11},{7,15},{8,0},{9,4},... | collective-permute-start | bytes 786440 | tf_op jit(solution)/shard_map/ppermute | solution.py:92
  46.4 6.2 %collective-permute-done.17 = bf16[256,2048]{1,0:T(8,128)(2,1)S(1)} collective-permute-done((bf16[256,2048]{1,0:T(8,128)(2,1)S(1)}, bf16[256,2048]{1,0:T(8,128)(2,1)S(1)}, u32[]{:S(2)}, u32[]{:S(2)}) %collective-permute-start.17) | collective-permute-done | bytes 1048608 | tf_op jit(solution)/shard_map/ppermute | solution.py:19
  62.4 6.3 %collective-permute-start.13 = (f32[2,4,64]{2,1,0:T(4,128)S(1)}, f32[2,4,64]{2,1,0:T(4,128)S(1)}, u32[]{:S(2)}, u32[]{:S(2)}) collective-permute-start(f32[2,4,64]{2,1,0:T(4,128)S(1)} %pad_maximum_fusion.2), channel_id=1, source_target_pairs={{0,8},{4,12},{8,0},{12,4},{1,9},{5,13},{9,1},{13,5},{2,10},{6,14},... | collective-permute-start | bytes 6152 | tf_op jit(solution)/shard_map/ppermute | solution.py:133
  71.8 5.5 %collective-permute-start.21 = (bf16[1,64,2048]{2,1,0:T(8,128)(2,1)S(1)}, bf16[1,64,2048]{2,1,0:T(8,128)(2,1)S(1)}, u32[]{:S(2)}, u32[]{:S(2)}) collective-permute-start(bf16[1,64,2048]{2,1,0:T(8,128)(2,1)S(1)} %get-tuple-element.36), channel_id=1, source_target_pairs={{0,8},{1,12},{2,10},{3,14},{4,9},{5,13},{6,11},{7,15},{8,0},{9,4},... | collective-permute-start | bytes 786440 | tf_op jit(solution)/shard_map/ppermute | solution.py:92
  77.3 3.3 %collective-permute-start.22 = (bf16[1,64,2048]{2,1,0:T(8,128)(2,1)S(1)}, bf16[1,64,2048]{2,1,0:T(8,128)(2,1)S(1)}, u32[]{:S(2)}, u32[]{:S(2)}) collective-permute-start(bf16[1,64,2048]{2,1,0:T(8,128)(2,1)S(1)} %get-tuple-element.35), channel_id=1, source_target_pairs={{0,9},{1,13},{2,11},{3,15},{4,8},{5,12},{6,10},{7,14},{8,1},{9,5},... | collective-permute-start | bytes 786440 | tf_op jit(solution)/shard_map/ppermute | solution.py:92
  85.8 9.6 %collective-permute-done.21 = bf16[1,64,2048]{2,1,0:T(8,128)(2,1)S(1)} collective-permute-done((bf16[1,64,2048]{2,1,0:T(8,128)(2,1)S(1)}, bf16[1,64,2048]{2,1,0:T(8,128)(2,1)S(1)}, u32[]{:S(2)}, u32[]{:S(2)}) %collective-permute-start.21) | collective-permute-done | bytes 262176 | tf_op jit(solution)/shard_map/ppermute | solution.py:92
  99.0 13.2 %collective-permute-done.15 = bf16[4,32,2048]{2,1,0:T(8,128)(2,1)S(1)} collective-permute-done((bf16[4,32,2048]{2,1,0:T(8,128)(2,1)S(1)}, bf16[4,32,2048]{2,1,0:T(8,128)(2,1)S(1)}, u32[]{:S(2)}, u32[]{:S(2)}) %collective-permute-start.15) | collective-permute-done | bytes 524320 | tf_op jit(solution)/shard_map/ppermute | solution.py:19
  113.7 4.3 %all-to-all-start = ((bf16[4,64,2048]{2,1,0:T(8,128)(2,1)}), bf16[4,64,2048]{2,1,0:T(8,128)(2,1)}, u32[]{:S(2)}, u32[]{:S(2)}) async-start(bf16[4,64,2048]{2,1,0:T(8,128)(2,1)} %fusion.10), calls=%async_computation | async-start | bytes 2097152 | tf_op jit(solution)/shard_map/all_to_all | solution.py:43
  118.4 8.3 %collective-permute-done.24.refs_2_ = bf16[4,32,2048]{2,1,0:T(8,128)(2,1)S(1)} collective-permute-done((bf16[4,32,2048]{2,1,0:T(8,128)(2,1)S(1)}, bf16[4,32,2048]{2,1,0:T(8,128)(2,1)S(1)}, u32[]{:S(2)}, u32[]{:S(2)}) %collective-permute-start.24) | collective-permute-done | bytes 524320 | tf_op jit(solution)/shard_map/ppermute | solution.py:34
  134.2 7.3 %shard_map.86 = bf16[4,4,32,2048]{3,2,1,0:T(8,128)(2,1)S(1)} custom-call(bf16[4,32,2048]{2,1,0:T(8,128)(2,1)S(1)} %get-tuple-element.47.refs_0_, bf16[4,32,2048]{2,1,0:T(8,128)(2,1)S(1)} %copy-done.4, bf16[4,32,2048]{2,1,0:T(8,128)(2,1)S(1)} %copy-done.2, bf16[4,32,2048]{2,1,0:T(8,128)(2,1)S(1)} %copy-done.6, bf16[2048,2048]{1,0:T(8,128)(2,1)} %bitcast.176), custom_call_target="tpu_custom_call" | custom-call | flops 4294967296 | bytes 10485760 | tf_op jit(solution)/shard_map/pallas_call | solution.py:183
  146.7 7.6 %shard_map.87 = bf16[4,4,32,2048]{3,2,1,0:T(8,128)(2,1)S(1)} custom-call(bf16[4,32,2048]{2,1,0:T(8,128)(2,1)S(1)} %get-tuple-element.46.refs_0_, bf16[4,32,2048]{2,1,0:T(8,128)(2,1)} %collective-permute-done.28.refs_1_, bf16[4,32,2048]{2,1,0:T(8,128)(2,1)} %collective-permute-done.29.refs_2_, bf16[4,32,2048]{2,1,0:T(8,128)(2,1)S(1)} %collective-permute-done.30.refs_3_, ...), custom_call_target="tpu_custom_call" | custom-call | flops 4294967296 | bytes 10485760 | tf_op jit(solution)/shard_map/pallas_call | solution.py:183
  156.5 4.2 %all-to-all-start.1 = ((bf16[4,64,2048]{2,1,0:T(8,128)(2,1)}), bf16[4,64,2048]{2,1,0:T(8,128)(2,1)}, u32[]{:S(2)}, u32[]{:S(2)}) async-start(bf16[4,64,2048]{2,1,0:T(8,128)(2,1)} %all-to-all-done), calls=%async_computation.1 | async-start | bytes 2097152 | tf_op jit(solution)/shard_map/all_to_all | solution.py:43
  163.3 10.1 %collective-permute-done.32 = bf16[4,32,2048]{2,1,0:T(8,128)(2,1)} collective-permute-done((bf16[4,32,2048]{2,1,0:T(8,128)(2,1)}, bf16[4,32,2048]{2,1,0:T(8,128)(2,1)}, u32[]{:S(2)}, u32[]{:S(2)}) %collective-permute-start.32) | collective-permute-done | bytes 524320 | tf_op jit(solution)/shard_map/ppermute | solution.py:289
  175.5 3.1 %fusion.3 = bf16[256,2048]{1,0:T(8,128)(2,1)} fusion(bf16[256,2048]{1,0:T(8,128)(2,1)} %param.12, bf16[4,64,2048]{2,1,0:T(8,128)(2,1)} %all-to-all-done.1, bf16[1,256,2048]{2,1,0:T(8,128)(2,1)S(1)} %copy-done.8), kind=kLoop, calls=%fused_computation.12 | loop fusion | flops 3145728 | bytes 4194304 | tf_op jit(solution)/shard_map/convert_element_type | solution.py:283
  179.9 4.7 %collective-permute-done.27 = bf16[4,32,2048]{2,1,0:T(8,128)(2,1)} collective-permute-done((bf16[4,32,2048]{2,1,0:T(8,128)(2,1)}, bf16[4,32,2048]{2,1,0:T(8,128)(2,1)}, u32[]{:S(2)}, u32[]{:S(2)}) %collective-permute-start.27) | collective-permute-done | bytes 524320 | tf_op jit(solution)/shard_map/ppermute | solution.py:289
  186.6 9.3 %collective-permute-done.33 = bf16[4,32,2048]{2,1,0:T(8,128)(2,1)} collective-permute-done((bf16[4,32,2048]{2,1,0:T(8,128)(2,1)}, bf16[4,32,2048]{2,1,0:T(8,128)(2,1)}, u32[]{:S(2)}, u32[]{:S(2)}) %collective-permute-start.33) | collective-permute-done | bytes 524320 | tf_op jit(solution)/shard_map/ppermute | solution.py:289
  197.2 9.8 %collective-permute-done.31 = bf16[4,32,2048]{2,1,0:T(8,128)(2,1)} collective-permute-done((bf16[4,32,2048]{2,1,0:T(8,128)(2,1)}, bf16[4,32,2048]{2,1,0:T(8,128)(2,1)}, u32[]{:S(2)}, u32[]{:S(2)}) %collective-permute-start.31) | collective-permute-done | bytes 524320 | tf_op jit(solution)/shard_map/ppermute | solution.py:289
  208.3 3.3 %fusion.13 = bf16[256,2048]{1,0:T(8,128)(2,1)} fusion(bf16[256,2048]{1,0:T(8,128)(2,1)} %collective-permute-done.35, bf16[4,64,2048]{2,1,0:T(8,128)(2,1)} %all-to-all-done.1, pred[]{:T(512)S(6)} %eq.79, bf16[1,256,2048]{2,1,0:T(8,128)(2,1)S(1)} %copy-done.8, bf16[256,2048]{1,0:T(8,128)(2,1)S(1)} %copy-done.10), kind=kLoop, calls=%fused_computation.32 | loop fusion | flops 5767168 | bytes 5242881 | tf_op jit(solution)/shard_map/jit(_where)/select_n | solution.py:286
  211.5 5.9 %collective-permute-done.34 = bf16[4,32,2048]{2,1,0:T(8,128)(2,1)S(1)} collective-permute-done((bf16[4,32,2048]{2,1,0:T(8,128)(2,1)S(1)}, bf16[4,32,2048]{2,1,0:T(8,128)(2,1)S(1)}, u32[]{:S(2)}, u32[]{:S(2)}) %collective-permute-start.34) | collective-permute-done | bytes 524320 | tf_op jit(solution)/shard_map/ppermute | solution.py:289
  (121 shorter events, 65.2 us)
Async XLA Ops:
  0.7 30.7 %collective-permute-start.4 = (bf16[512,2048]{1,0:T(8,128)(2,1)}, bf16[512,2048]{1,0:T(8,128)(2,1)}, u32[]{:S(2)}, u32[]{:S(2)}) collective-permute-start(bf16[512,2048]{1,0:T(8,128)(2,1)} %bitcast.178), channel_id=1, source_target_pairs={{0,1},{1,0},{2,3},{3,2},{4,5},{5,4},{6,7},{7,6},{8,9},{9,8},{10,11... | collective-permute-start | bytes 6291464 | tf_op jit(solution)/shard_map/ppermute | solution.py:39
  3.4 34.9 %collective-permute-start.5 = (bf16[2,1,64,2048]{3,2,1,0:T(8,128)(2,1)S(1)}, bf16[2,1,64,2048]{3,2,1,0:T(8,128)(2,1)S(1)}, u32[]{:S(2)}, u32[]{:S(2)}) collective-permute-start(bf16[2,1,64,2048]{3,2,1,0:T(8,128)(2,1)S(1)} %dynamic-slice_bitcast_fusion.3), channel_id=1, source_target_pairs={{0,2},{1,3},{2,0},{3,1},{4,6},{5,7},{6,4},{7,5},{8,10},{9,11},{10,... | collective-permute-start | bytes 1572872 | tf_op jit(solution)/shard_map/ppermute | solution.py:34
  7.4 17.3 %collective-permute-start.2 = (bf16[2,64,1024]{2,1,0:T(8,128)(2,1)S(1)}, bf16[2,64,1024]{2,1,0:T(8,128)(2,1)S(1)}, u32[]{:S(2)}, u32[]{:S(2)}) collective-permute-start(bf16[2,64,1024]{2,1,0:T(8,128)(2,1)S(1)} %pad_maximum_fusion.1), channel_id=1, source_target_pairs={{0,8},{4,12},{8,0},{12,4},{1,9},{5,13},{9,1},{13,5},{2,10},{6,14},... | collective-permute-start | bytes 786440 | tf_op jit(solution)/shard_map/ppermute | solution.py:133
  11.3 19.4 %collective-permute-start.3 = (bf16[2,64,1024]{2,1,0:T(8,128)(2,1)S(1)}, bf16[2,64,1024]{2,1,0:T(8,128)(2,1)S(1)}, u32[]{:S(2)}, u32[]{:S(2)}) collective-permute-start(bf16[2,64,1024]{2,1,0:T(8,128)(2,1)S(1)} %pad_maximum_fusion.1), channel_id=1, source_target_pairs={{0,12},{4,0},{8,4},{12,8},{1,13},{5,1},{9,5},{13,9},{2,14},{6,2},{... | collective-permute-start | bytes 786440 | tf_op jit(solution)/shard_map/ppermute | solution.py:133
  12.7 18.0 %collective-permute-start.1 = (bf16[2,64,1024]{2,1,0:T(8,128)(2,1)S(1)}, bf16[2,64,1024]{2,1,0:T(8,128)(2,1)S(1)}, u32[]{:S(2)}, u32[]{:S(2)}) collective-permute-start(bf16[2,64,1024]{2,1,0:T(8,128)(2,1)S(1)} %pad_maximum_fusion.1), channel_id=1, source_target_pairs={{0,4},{4,8},{8,12},{12,0},{1,5},{5,9},{9,13},{13,1},{2,6},{6,10},{... | collective-permute-start | bytes 786440 | tf_op jit(solution)/shard_map/ppermute | solution.py:133
  24.7 27.9 %collective-permute-start.17 = (bf16[256,2048]{1,0:T(8,128)(2,1)S(1)}, bf16[256,2048]{1,0:T(8,128)(2,1)S(1)}, u32[]{:S(2)}, u32[]{:S(2)}) collective-permute-start(bf16[256,2048]{1,0:T(8,128)(2,1)S(1)} %bitcast.163), channel_id=1, source_target_pairs={{16,0},{17,1},{18,2},{19,3},{20,4},{21,5},{22,6},{23,7},{24,8},{25... | collective-permute-start | bytes 3145736 | tf_op jit(solution)/shard_map/ppermute | solution.py:19
  35.5 26.2 %collective-permute-start.11 = (bf16[4,64,2048]{2,1,0:T(8,128)(2,1)S(1)}, bf16[4,64,2048]{2,1,0:T(8,128)(2,1)S(1)}, u32[]{:S(2)}, u32[]{:S(2)}) collective-permute-start(bf16[4,64,2048]{2,1,0:T(8,128)(2,1)S(1)} %fusion.2), channel_id=1, source_target_pairs={{0,2},{1,3},{2,0},{3,1},{4,6},{5,7},{6,4},{7,5},{8,10},{9,11},{10,... | collective-permute-start | bytes 3145736 | tf_op jit(solution)/shard_map/ppermute | solution.py:34
  38.5 20.5 %collective-permute-start.8 = (bf16[1,64,2048]{2,1,0:T(8,128)(2,1)S(1)}, bf16[1,64,2048]{2,1,0:T(8,128)(2,1)S(1)}, u32[]{:S(2)}, u32[]{:S(2)}) collective-permute-start(bf16[1,64,2048]{2,1,0:T(8,128)(2,1)S(1)} %get-tuple-element.40), channel_id=1, source_target_pairs={{0,8},{1,12},{2,10},{3,14},{4,9},{5,13},{6,11},{7,15},{8,0},{9,4},... | collective-permute-start | bytes 786440 | tf_op jit(solution)/shard_map/ppermute | solution.py:92
  62.4 18.2 %collective-permute-start.13 = (f32[2,4,64]{2,1,0:T(4,128)S(1)}, f32[2,4,64]{2,1,0:T(4,128)S(1)}, u32[]{:S(2)}, u32[]{:S(2)}) collective-permute-start(f32[2,4,64]{2,1,0:T(4,128)S(1)} %pad_maximum_fusion.2), channel_id=1, source_target_pairs={{0,8},{4,12},{8,0},{12,4},{1,9},{5,13},{9,1},{13,5},{2,10},{6,14},... | collective-permute-start | bytes 6152 | tf_op jit(solution)/shard_map/ppermute | solution.py:133
  71.8 23.7 %collective-permute-start.21 = (bf16[1,64,2048]{2,1,0:T(8,128)(2,1)S(1)}, bf16[1,64,2048]{2,1,0:T(8,128)(2,1)S(1)}, u32[]{:S(2)}, u32[]{:S(2)}) collective-permute-start(bf16[1,64,2048]{2,1,0:T(8,128)(2,1)S(1)} %get-tuple-element.36), channel_id=1, source_target_pairs={{0,8},{1,12},{2,10},{3,14},{4,9},{5,13},{6,11},{7,15},{8,0},{9,4},... | collective-permute-start | bytes 786440 | tf_op jit(solution)/shard_map/ppermute | solution.py:92
  77.3 19.5 %collective-permute-start.22 = (bf16[1,64,2048]{2,1,0:T(8,128)(2,1)S(1)}, bf16[1,64,2048]{2,1,0:T(8,128)(2,1)S(1)}, u32[]{:S(2)}, u32[]{:S(2)}) collective-permute-start(bf16[1,64,2048]{2,1,0:T(8,128)(2,1)S(1)} %get-tuple-element.35), channel_id=1, source_target_pairs={{0,9},{1,13},{2,11},{3,15},{4,8},{5,12},{6,10},{7,14},{8,1},{9,5},... | collective-permute-start | bytes 786440 | tf_op jit(solution)/shard_map/ppermute | solution.py:92
  80.6 16.1 %collective-permute-start.20 = (bf16[1,64,2048]{2,1,0:T(8,128)(2,1)S(1)}, bf16[1,64,2048]{2,1,0:T(8,128)(2,1)S(1)}, u32[]{:S(2)}, u32[]{:S(2)}) collective-permute-start(bf16[1,64,2048]{2,1,0:T(8,128)(2,1)S(1)} %get-tuple-element.37), channel_id=1, source_target_pairs={{0,1},{1,5},{2,3},{3,7},{4,0},{5,4},{6,2},{7,6},{8,9},{9,13},{10,1... | collective-permute-start | bytes 786440 | tf_op jit(solution)/shard_map/ppermute | solution.py:92
  95.4 16.7 %collective-permute-start.15 = (bf16[4,32,2048]{2,1,0:T(8,128)(2,1)S(1)}, bf16[4,32,2048]{2,1,0:T(8,128)(2,1)S(1)}, u32[]{:S(2)}, u32[]{:S(2)}) collective-permute-start(bf16[4,32,2048]{2,1,0:T(8,128)(2,1)S(1)} %get-tuple-element.51), channel_id=1, source_target_pairs={{16,0},{17,1},{18,2},{19,3},{20,4},{21,5},{22,6},{23,7},{24,8},{25... | collective-permute-start | bytes 1572872 | tf_op jit(solution)/shard_map/ppermute | solution.py:19
  113.7 30.8 %all-to-all-start = ((bf16[4,64,2048]{2,1,0:T(8,128)(2,1)}), bf16[4,64,2048]{2,1,0:T(8,128)(2,1)}, u32[]{:S(2)}, u32[]{:S(2)}) async-start(bf16[4,64,2048]{2,1,0:T(8,128)(2,1)} %fusion.10), calls=%async_computation | async-start | bytes 2097152 | tf_op jit(solution)/shard_map/all_to_all | solution.py:43
  127.5 17.1 %collective-permute-start.28 = (bf16[4,32,2048]{2,1,0:T(8,128)(2,1)S(1)}, bf16[4,32,2048]{2,1,0:T(8,128)(2,1)}, u32[]{:S(2)}, u32[]{:S(2)}) collective-permute-start(bf16[4,32,2048]{2,1,0:T(8,128)(2,1)S(1)} %get-tuple-element.46.refs_0_), channel_id=1, source_target_pairs={{0,1},{1,0},{2,3},{3,2},{4,5},{5,4},{6,7},{7,6},{8,9},{9,8},{10,11... | collective-permute-start | bytes 1572872 | tf_op jit(solution)/shard_map/ppermute | solution.py:39
  128.0 16.6 %collective-permute-start.29 = (bf16[4,32,2048]{2,1,0:T(8,128)(2,1)S(1)}, bf16[4,32,2048]{2,1,0:T(8,128)(2,1)}, u32[]{:S(2)}, u32[]{:S(2)}) collective-permute-start(bf16[4,32,2048]{2,1,0:T(8,128)(2,1)S(1)} %get-tuple-element.46.refs_0_), channel_id=1, source_target_pairs={{0,2},{1,3},{2,0},{3,1},{4,6},{5,7},{6,4},{7,5},{8,10},{9,11},{10,... | collective-permute-start | bytes 1572872 | tf_op jit(solution)/shard_map/ppermute | solution.py:34
  144.6 16.5 %collective-permute-start.26 = (bf16[4,32,2048]{2,1,0:T(8,128)(2,1)}, bf16[4,32,2048]{2,1,0:T(8,128)(2,1)}, u32[]{:S(2)}, u32[]{:S(2)}) collective-permute-start(bf16[4,32,2048]{2,1,0:T(8,128)(2,1)} %dynamic-slice_bitcast_fusion.1), channel_id=1, source_target_pairs={{0,4},{4,8},{8,12},{12,0},{1,5},{5,9},{9,13},{13,1},{2,6},{6,10},{... | collective-permute-start | bytes 1572872 | tf_op jit(solution)/shard_map/ppermute | solution.py:289
  156.5 16.9 %collective-permute-start.32 = (bf16[4,32,2048]{2,1,0:T(8,128)(2,1)}, bf16[4,32,2048]{2,1,0:T(8,128)(2,1)}, u32[]{:S(2)}, u32[]{:S(2)}) collective-permute-start(bf16[4,32,2048]{2,1,0:T(8,128)(2,1)} %dynamic-slice_bitcast_fusion), channel_id=1, source_target_pairs={{0,4},{4,8},{8,12},{12,0},{1,5},{5,9},{9,13},{13,1},{2,6},{6,10},{... | collective-permute-start | bytes 1572872 | tf_op jit(solution)/shard_map/ppermute | solution.py:289
  156.5 19.0 %all-to-all-start.1 = ((bf16[4,64,2048]{2,1,0:T(8,128)(2,1)}), bf16[4,64,2048]{2,1,0:T(8,128)(2,1)}, u32[]{:S(2)}, u32[]{:S(2)}) async-start(bf16[4,64,2048]{2,1,0:T(8,128)(2,1)} %all-to-all-done), calls=%async_computation.1 | async-start | bytes 2097152 | tf_op jit(solution)/shard_map/all_to_all | solution.py:43
  163.0 21.6 %collective-permute-start.27 = (bf16[4,32,2048]{2,1,0:T(8,128)(2,1)}, bf16[4,32,2048]{2,1,0:T(8,128)(2,1)}, u32[]{:S(2)}, u32[]{:S(2)}) collective-permute-start(bf16[4,32,2048]{2,1,0:T(8,128)(2,1)} %fusion.17), channel_id=1, source_target_pairs={{0,4},{4,8},{8,12},{12,0},{1,5},{5,9},{9,13},{13,1},{2,6},{6,10},{... | collective-permute-start | bytes 1572872 | tf_op jit(solution)/shard_map/ppermute | solution.py:289
  175.5 20.3 %collective-permute-start.33 = (bf16[4,32,2048]{2,1,0:T(8,128)(2,1)}, bf16[4,32,2048]{2,1,0:T(8,128)(2,1)}, u32[]{:S(2)}, u32[]{:S(2)}) collective-permute-start(bf16[4,32,2048]{2,1,0:T(8,128)(2,1)} %fusion.14), channel_id=1, source_target_pairs={{0,4},{4,8},{8,12},{12,0},{1,5},{5,9},{9,13},{13,1},{2,6},{6,10},{... | collective-permute-start | bytes 1572872 | tf_op jit(solution)/shard_map/ppermute | solution.py:289
  178.6 29.6 %collective-permute-start.35 = (bf16[256,2048]{1,0:T(8,128)(2,1)}, bf16[256,2048]{1,0:T(8,128)(2,1)}, u32[]{:S(2)}, u32[]{:S(2)}) collective-permute-start(bf16[256,2048]{1,0:T(8,128)(2,1)} %fusion.3), channel_id=1, source_target_pairs={{16,0},{17,1},{18,2},{19,3},{20,4},{21,5},{22,6},{23,7},{24,8},{25... | collective-permute-start | bytes 3145736 | tf_op jit(solution)/shard_map/ppermute | solution.py:19
  186.6 20.5 %collective-permute-start.31 = (bf16[4,32,2048]{2,1,0:T(8,128)(2,1)}, bf16[4,32,2048]{2,1,0:T(8,128)(2,1)}, u32[]{:S(2)}, u32[]{:S(2)}) collective-permute-start(bf16[4,32,2048]{2,1,0:T(8,128)(2,1)} %fusion.18), channel_id=1, source_target_pairs={{0,4},{4,8},{8,12},{12,0},{1,5},{5,9},{9,13},{13,1},{2,6},{6,10},{... | collective-permute-start | bytes 1572872 | tf_op jit(solution)/shard_map/ppermute | solution.py:289
  197.2 20.2 %collective-permute-start.34 = (bf16[4,32,2048]{2,1,0:T(8,128)(2,1)S(1)}, bf16[4,32,2048]{2,1,0:T(8,128)(2,1)S(1)}, u32[]{:S(2)}, u32[]{:S(2)}) collective-permute-start(bf16[4,32,2048]{2,1,0:T(8,128)(2,1)S(1)} %fusion.15), channel_id=1, source_target_pairs={{0,4},{4,8},{8,12},{12,0},{1,5},{5,9},{9,13},{13,1},{2,6},{6,10},{... | collective-permute-start | bytes 1572872 | tf_op jit(solution)/shard_map/ppermute | solution.py:289
  (28 other events, 251.5 us)

commit v5 on v4

--- a/solution.py
+++ b/solution.py
@@ -127,16 +127,11 @@
 
 def gather_seq(block):
     seq = lax.axis_size("seq")
+    place = lax.axis_index("seq")
     arrived = [block]
     for turn in range(1, seq):
         route = [(q, (q + turn) % seq) for q in range(seq)]
         arrived.append(lax.ppermute(block, "seq", route))
-    return arrived
-
-
-def by_place(arrived):
-    seq = len(arrived)
-    place = lax.axis_index("seq")
     return jnp.stack([lax.select_n((place - q) % seq, *arrived) for q in range(seq)], axis=0)
 
 
@@ -146,7 +141,7 @@
 
 def norm_backward(values, gain, kv_share, sums):
     short = lax.axis_size("seq") <= 2 * CORES
-    squares, intersection = jnp.sum(by_place(gather_seq(sums)), axis=0) if short else lax.psum(sums, "seq")
+    squares, intersection = jnp.sum(gather_seq(sums), axis=0) if short else lax.psum(sums, "seq")
     inv_rms = lax.rsqrt(squares / D + epsilon)[..., None]
     return (
         inv_rms * gain * kv_share
@@ -211,10 +206,13 @@
     kept = lax.dynamic_index_in_dim(mixed, core, 1, keepdims=False)
     given = lax.dynamic_index_in_dim(mixed, 1 - core, 1, keepdims=False)
     given = over_cores(given)
-    arrived = gather_seq(jnp.concatenate([kept, given], axis=2))
-    cotangent = by_place(arrived)
-    other = over_cores(kv_weight[0])
-    weights = jnp.concatenate([kv_weight[0], other], axis=0)
+    cotangent = gather_seq(
+        jnp.concatenate(
+            [jnp.where(core == 0, kept, given), jnp.where(core == 0, given, kept)], axis=2
+        )
+    )
+    pairs = [[t + core for core in range(CORES)] for t in range(0, tp, CORES)]
+    weights = lax.all_gather(kv_weight[0], "tp", axis=0, axis_index_groups=pairs, tiled=True)
 
     branch = mlp_grads[0].astype(jnp.float32)
     grad_one = output_cotangent.astype(jnp.float32) + branch
@@ -261,23 +259,18 @@
     leaving = [cut(norm_back, c) for c in range(CHUNKS)]
     arrivals = [from_behind(part, "section", -1) for part in leaving]
     home = mix_features(after(norm_back, leaving[-1]))
-    arriving = jnp.concatenate(arrivals, axis=1).astype(jnp.float32)
-    grad_zero = arriving + base.astype(jnp.float32)
-    grad = jnp.where(upstream, grad_zero.astype(jnp.bfloat16), base)
-    blocks_of = []
+    attn_parts = []
     for c in range(CHUNKS):
-        part = cut(grad, c)
-        blocks_of.append([over_rows(part, turn) if turn else part for turn in range(row)])
-    attn_parts = []
-    for c, blocks in enumerate(blocks_of):
-        if c > 0:
-            blocks[-1] = after(blocks[-1], attn_parts[-1][0])
+        part = cut(base, c)
+        arriving = arrivals[c] if c == 0 else after(arrivals[c], attn_parts[-1][0])
+        grad_zero = arriving.astype(jnp.float32) + part.astype(jnp.float32)
+        grad = jnp.where(upstream, grad_zero.astype(jnp.bfloat16), part)
+        blocks = [over_rows(grad, turn) if turn else grad for turn in range(row)]
         pieces = [half for block in blocks for half in (block, over_cores(block))]
         terms = product(pieces, out_weight[0])
         first = lax.dynamic_index_in_dim(terms, (place - 1) % seq, 0, keepdims=False)
-        if c == 0:
-            first = after(first, home)
         attn_parts.append([first, terms])
+    attn_parts[0][0] = after(attn_parts[0][0], home)
     home = exchange(after(home, attn_parts[-1][0]), "tp")
     home = home.reshape(tokens, -1).astype(jnp.float32)
     own = (grad_one + home).astype(jnp.bfloat16)

time: 221 us -> 240 us (1.086)
  between operations: 1.42 us -> 14.8 us
  starting transfers between devices: 58.9 us -> 63.8 us
  other arithmetic: 21.9 us -> 26.7 us
  local copies, waits for them, and re-layouts: 13.3 us -> 9.94 us
    ppermute x5, waiting for transfers between devices: 9.84 us -> 25.9 us  [over_rows(): lax.ppermute(block, 'tp', [(t, (t + turn * CORES) % tp) for t in range(tp)])]
    ppermute x4, waiting for transfers between devices: 21.4 us -> 8.75 us  [from_behind(): return lax.ppermute(block, axis, route)]
    ppermute x6, waiting for transfers between devices: 40.1 us -> 35.4 us  [body(): total = lax.ppermute(mine, 'seq', [(q, (q + 1) % seq) for q in range(seq)])]
    ppermute x6, starting transfers between devices: 0.34 us -> 4.91 us  [body(): total = lax.ppermute(mine, 'seq', [(q, (q + 1) % seq) for q in range(seq)])]
    unnamed x28 -> x30, local copies, waits for them, and re-layouts: 8.18 us -> 5.25 us
  transfers between devices with their start and end apart: 38 -> 38, of which waited for: 18 -> 16; matrix products, arithmetic and copies ran while one was open for 14% -> 14% of each run, Pallas kernels for 7% -> 6%
where the time goes in v5:
time: 240 us; the launch traced here: 238 us
  waiting for transfers between devices  103 us (43%)
  starting transfers between devices  63.8 us (27%)
  other arithmetic  26.7 us (11%)
  Pallas kernels  15 us (6%)
  between operations  14.8 us (6%)
  local copies, waits for them, and re-layouts  9.94 us (4%)
  matrix products  4.73 us (2%)
    ppermute x6, waiting for transfers between devices, body(): total = lax.ppermute(mine, 'seq', [(q, (q + 1) % seq) for q in range(seq)])  35.4 us
    ppermute x5, waiting for transfers between devices, over_rows(): lax.ppermute(block, 'tp', [(t, (t + turn * CORES) % tp) for t in range(tp)])  25.9 us
    ppermute x8, starting transfers between devices, spread(): moved = lax.ppermute(piece, ('seq', 'tp'), route)  17.7 us
    ppermute x6, waiting for transfers between devices, gather_seq(): arrived.append(lax.ppermute(block, 'seq', route))  17.3 us
    pallas_call x2, Pallas kernels, product(): pl.pallas_call(product_kernel, out_shape=jax.ShapeDtypeStruct((seq, n, de...  15 us
    ppermute x6, starting transfers between devices, gather_seq(): arrived.append(lax.ppermute(block, 'seq', route))  14.7 us
    ppermute x8, waiting for transfers between devices, spread(): moved = lax.ppermute(piece, ('seq', 'tp'), route)  13.3 us
    convert_element_type x6, other arithmetic, body(): mine = mine.astype(jnp.bfloat16)  9.81 us
  transfers between devices with their start and end apart: 38, of which 16 were waited for; matrix products, arithmetic and copies ran while one was open for 14% of the time, Pallas kernels for 6%

profile of v5, /device:TPU:0, one launch (start us, length us, event | category | flops | bytes accessed | tf_op | source)
XLA Modules:
  0.0 238.3 jit_solution(7799781381420553718)
XLA Ops:
  14.7 3.9 %collective-permute-start.2 = (bf16[2,64,1024]{2,1,0:T(8,128)(2,1)S(1)}, bf16[2,64,1024]{2,1,0:T(8,128)(2,1)S(1)}, u32[]{:S(2)}, u32[]{:S(2)}) collective-permute-start(bf16[2,64,1024]{2,1,0:T(8,128)(2,1)S(1)} %pad_maximum_fusion.1), channel_id=1, source_target_pairs={{0,8},{4,12},{8,0},{12,4},{1,9},{5,13},{9,1},{13,5},{2,10},{6,14},... | collective-permute-start | bytes 786440 | tf_op jit(solution)/shard_map/ppermute | solution.py:134
  20.6 10.8 %collective-permute-done.2 = bf16[2,64,1024]{2,1,0:T(8,128)(2,1)S(1)} collective-permute-done((bf16[2,64,1024]{2,1,0:T(8,128)(2,1)S(1)}, bf16[2,64,1024]{2,1,0:T(8,128)(2,1)S(1)}, u32[]{:S(2)}, u32[]{:S(2)}) %collective-permute-start.2) | collective-permute-done | bytes 262176 | tf_op jit(solution)/shard_map/ppermute | solution.py:134
  31.5 6.4 %collective-permute-done.3 = bf16[2,64,1024]{2,1,0:T(8,128)(2,1)S(1)} collective-permute-done((bf16[2,64,1024]{2,1,0:T(8,128)(2,1)S(1)}, bf16[2,64,1024]{2,1,0:T(8,128)(2,1)S(1)}, u32[]{:S(2)}, u32[]{:S(2)}) %collective-permute-start.3) | collective-permute-done | bytes 262176 | tf_op jit(solution)/shard_map/ppermute | solution.py:134
  38.5 3.4 %fusion.4 = bf16[4,64,2048]{2,1,0:T(8,128)(2,1)S(1)} fusion(bf16[1,1024,2048]{2,1,0:T(8,128)(2,1)} %all-gather.3.cloned.1.call-done, bf16[4,2,64,1024]{3,2,0,1:T(8,128)(2,1)S(1)} %pad_maximum_fusion, s32[]{:T(128)S(6)} %select_n.885), kind=kOutput, calls=%fused_computation.12 | convolution fusion | flops 1074266112 | bytes 5767172 | tf_op jit(solution)/shard_map/dot_general | solution.py:226
  42.0 3.1 %collective-permute-start.10 = (bf16[4,64,2048]{2,1,0:T(8,128)(2,1)S(1)}, bf16[4,64,2048]{2,1,0:T(8,128)(2,1)S(1)}, u32[]{:S(2)}, u32[]{:S(2)}) collective-permute-start(bf16[4,64,2048]{2,1,0:T(8,128)(2,1)S(1)} %fusion.4), channel_id=1, source_target_pairs={{0,2},{1,3},{2,0},{3,1},{4,6},{5,7},{6,4},{7,5},{8,10},{9,11},{10,... | collective-permute-start | bytes 3145736 | tf_op jit(solution)/shard_map/ppermute | solution.py:34
  46.4 5.3 %collective-permute-start.7 = (bf16[1,64,2048]{2,1,0:T(8,128)(2,1)S(1)}, bf16[1,64,2048]{2,1,0:T(8,128)(2,1)S(1)}, u32[]{:S(2)}, u32[]{:S(2)}) collective-permute-start(bf16[1,64,2048]{2,1,0:T(8,128)(2,1)S(1)} %get-tuple-element.40), channel_id=1, source_target_pairs={{0,8},{1,12},{2,10},{3,14},{4,9},{5,13},{6,11},{7,15},{8,0},{9,4},... | collective-permute-start | bytes 786440 | tf_op jit(solution)/shard_map/ppermute | solution.py:92
  58.6 8.3 %collective-permute-done.7 = bf16[1,64,2048]{2,1,0:T(8,128)(2,1)S(1)} collective-permute-done((bf16[1,64,2048]{2,1,0:T(8,128)(2,1)S(1)}, bf16[1,64,2048]{2,1,0:T(8,128)(2,1)S(1)}, u32[]{:S(2)}, u32[]{:S(2)}) %collective-permute-start.7) | collective-permute-done | bytes 262176 | tf_op jit(solution)/shard_map/ppermute | solution.py:92
  69.7 6.8 %collective-permute-start.12 = (f32[2,4,64]{2,1,0:T(4,128)S(1)}, f32[2,4,64]{2,1,0:T(4,128)S(1)}, u32[]{:S(2)}, u32[]{:S(2)}) collective-permute-start(f32[2,4,64]{2,1,0:T(4,128)S(1)} %pad_maximum_fusion.2), channel_id=1, source_target_pairs={{0,8},{4,12},{8,0},{12,4},{1,9},{5,13},{9,1},{13,5},{2,10},{6,14},... | collective-permute-start | bytes 6152 | tf_op jit(solution)/shard_map/ppermute | solution.py:134
  80.6 5.2 %collective-permute-start.19 = (bf16[1,64,2048]{2,1,0:T(8,128)(2,1)}, bf16[1,64,2048]{2,1,0:T(8,128)(2,1)S(1)}, u32[]{:S(2)}, u32[]{:S(2)}) collective-permute-start(bf16[1,64,2048]{2,1,0:T(8,128)(2,1)} %get-tuple-element.36), channel_id=1, source_target_pairs={{0,8},{1,12},{2,10},{3,14},{4,9},{5,13},{6,11},{7,15},{8,0},{9,4},... | collective-permute-start | bytes 786440 | tf_op jit(solution)/shard_map/ppermute | solution.py:92
  94.7 5.0 %collective-permute-done.19 = bf16[1,64,2048]{2,1,0:T(8,128)(2,1)S(1)} collective-permute-done((bf16[1,64,2048]{2,1,0:T(8,128)(2,1)}, bf16[1,64,2048]{2,1,0:T(8,128)(2,1)S(1)}, u32[]{:S(2)}, u32[]{:S(2)}) %collective-permute-start.19) | collective-permute-done | bytes 262176 | tf_op jit(solution)/shard_map/ppermute | solution.py:92
  100.0 8.7 %collective-permute-done.14 = bf16[4,32,2048]{2,1,0:T(8,128)(2,1)S(1)} collective-permute-done((bf16[4,32,2048]{2,1,0:T(8,128)(2,1)S(1)}, bf16[4,32,2048]{2,1,0:T(8,128)(2,1)S(1)}, u32[]{:S(2)}, u32[]{:S(2)}) %collective-permute-start.14) | collective-permute-done | bytes 524320 | tf_op jit(solution)/shard_map/ppermute | solution.py:19
  112.0 11.2 %collective-permute-done.22.refs_2_ = bf16[4,32,2048]{2,1,0:T(8,128)(2,1)S(1)} collective-permute-done((bf16[4,32,2048]{2,1,0:T(8,128)(2,1)S(1)}, bf16[4,32,2048]{2,1,0:T(8,128)(2,1)S(1)}, u32[]{:S(2)}, u32[]{:S(2)}) %collective-permute-start.22) | collective-permute-done | bytes 524320 | tf_op jit(solution)/shard_map/ppermute | solution.py:34
  124.9 4.3 %all-to-all-start = ((bf16[4,64,2048]{2,1,0:T(8,128)(2,1)}), bf16[4,64,2048]{2,1,0:T(8,128)(2,1)}, u32[]{:S(2)}, u32[]{:S(2)}) async-start(bf16[4,64,2048]{2,1,0:T(8,128)(2,1)} %fusion.14), calls=%async_computation | async-start | bytes 2097152 | tf_op jit(solution)/shard_map/all_to_all | solution.py:43
  132.9 7.4 %shard_map.86 = bf16[4,4,32,2048]{3,2,1,0:T(8,128)(2,1)S(1)} custom-call(bf16[4,32,2048]{2,1,0:T(8,128)(2,1)S(1)} %fusion.23.refs_0_, bf16[4,32,2048]{2,1,0:T(8,128)(2,1)S(1)} %copy-done.2, bf16[4,32,2048]{2,1,0:T(8,128)(2,1)S(1)} %collective-permute-done.22.refs_2_, bf16[4,32,2048]{2,1,0:T(8,128)(2,1)S(1)} %copy-done.4, bf16[2048,2048]{1,0:T(8,128)(2,1)} %bitcast.177), custom_call_target="tpu_custom_call" | custom-call | flops 4294967296 | bytes 10485760 | tf_op jit(solution)/shard_map/pallas_call | solution.py:178
  143.9 12.5 %collective-permute-done.28.refs_2_ = bf16[4,32,2048]{2,1,0:T(8,128)(2,1)S(1)} collective-permute-done((bf16[4,32,2048]{2,1,0:T(8,128)(2,1)S(1)}, bf16[4,32,2048]{2,1,0:T(8,128)(2,1)S(1)}, u32[]{:S(2)}, u32[]{:S(2)}) %collective-permute-start.28) | collective-permute-done | bytes 524320 | tf_op jit(solution)/shard_map/ppermute | solution.py:34
  158.4 7.6 %shard_map.87 = bf16[4,4,32,2048]{3,2,1,0:T(8,128)(2,1)S(1)} custom-call(bf16[4,32,2048]{2,1,0:T(8,128)(2,1)S(1)} %fusion.24.refs_0_, bf16[4,32,2048]{2,1,0:T(8,128)(2,1)} %collective-permute-done.27.refs_1_, bf16[4,32,2048]{2,1,0:T(8,128)(2,1)S(1)} %collective-permute-done.28.refs_2_, bf16[4,32,2048]{2,1,0:T(8,128)(2,1)} %collective-permute-done.29.refs_3_, ...), custom_call_target="tpu_custom_call" | custom-call | flops 4294967296 | bytes 10485760 | tf_op jit(solution)/shard_map/pallas_call | solution.py:178
  169.9 4.4 %all-to-all-start.1 = ((bf16[4,64,2048]{2,1,0:T(8,128)(2,1)}), bf16[4,64,2048]{2,1,0:T(8,128)(2,1)}, u32[]{:S(2)}, u32[]{:S(2)}) async-start(bf16[4,64,2048]{2,1,0:T(8,128)(2,1)} %all-to-all-done), calls=%async_computation.1 | async-start | bytes 2097152 | tf_op jit(solution)/shard_map/all_to_all | solution.py:43
  177.8 7.2 %collective-permute-done.31 = bf16[4,32,2048]{2,1,0:T(8,128)(2,1)} collective-permute-done((bf16[4,32,2048]{2,1,0:T(8,128)(2,1)}, bf16[4,32,2048]{2,1,0:T(8,128)(2,1)}, u32[]{:S(2)}, u32[]{:S(2)}) %collective-permute-start.31) | collective-permute-done | bytes 524320 | tf_op jit(solution)/shard_map/ppermute | solution.py:282
  188.8 3.1 %fusion.7 = bf16[256,2048]{1,0:T(8,128)(2,1)} fusion(bf16[256,2048]{1,0:T(8,128)(2,1)} %param.12, bf16[4,64,2048]{2,1,0:T(8,128)(2,1)} %all-to-all-done.1, bf16[1,256,2048]{2,1,0:T(8,128)(2,1)S(1)} %copy-done.6), kind=kLoop, calls=%fused_computation.13 | loop fusion | flops 3145728 | bytes 4194304 | tf_op jit(solution)/shard_map/convert_element_type | solution.py:276
  193.2 3.1 %collective-permute-done.25 = bf16[4,32,2048]{2,1,0:T(8,128)(2,1)} collective-permute-done((bf16[4,32,2048]{2,1,0:T(8,128)(2,1)}, bf16[4,32,2048]{2,1,0:T(8,128)(2,1)}, u32[]{:S(2)}, u32[]{:S(2)}) %collective-permute-start.25) | collective-permute-done | bytes 524320 | tf_op jit(solution)/shard_map/ppermute | solution.py:282
  198.3 9.3 %collective-permute-done.32 = bf16[4,32,2048]{2,1,0:T(8,128)(2,1)} collective-permute-done((bf16[4,32,2048]{2,1,0:T(8,128)(2,1)}, bf16[4,32,2048]{2,1,0:T(8,128)(2,1)}, u32[]{:S(2)}, u32[]{:S(2)}) %collective-permute-start.32) | collective-permute-done | bytes 524320 | tf_op jit(solution)/shard_map/ppermute | solution.py:282
  208.9 9.8 %collective-permute-done.30 = bf16[4,32,2048]{2,1,0:T(8,128)(2,1)} collective-permute-done((bf16[4,32,2048]{2,1,0:T(8,128)(2,1)}, bf16[4,32,2048]{2,1,0:T(8,128)(2,1)}, u32[]{:S(2)}, u32[]{:S(2)}) %collective-permute-start.30) | collective-permute-done | bytes 524320 | tf_op jit(solution)/shard_map/ppermute | solution.py:282
  220.0 3.3 %fusion.16 = bf16[256,2048]{1,0:T(8,128)(2,1)} fusion(bf16[256,2048]{1,0:T(8,128)(2,1)} %collective-permute-done.34, bf16[4,64,2048]{2,1,0:T(8,128)(2,1)} %all-to-all-done.1, pred[]{:T(512)S(6)} %eq.83, bf16[1,256,2048]{2,1,0:T(8,128)(2,1)S(1)} %copy-done.6, bf16[256,2048]{1,0:T(8,128)(2,1)S(1)} %copy-done.8), kind=kLoop, calls=%fused_computation.31 | loop fusion | flops 5767168 | bytes 5242881 | tf_op jit(solution)/shard_map/jit(_where)/select_n | solution.py:279
  223.2 5.9 %collective-permute-done.33 = bf16[4,32,2048]{2,1,0:T(8,128)(2,1)S(1)} collective-permute-done((bf16[4,32,2048]{2,1,0:T(8,128)(2,1)S(1)}, bf16[4,32,2048]{2,1,0:T(8,128)(2,1)S(1)}, u32[]{:S(2)}, u32[]{:S(2)}) %collective-permute-start.33) | collective-permute-done | bytes 524320 | tf_op jit(solution)/shard_map/ppermute | solution.py:282
  (126 shorter events, 67.5 us)
Async XLA Ops:
  7.2 31.3 %all-gather.3.cloned.1.call-start = ((), (), s32[]{:S(2)}) async-start(), calls=%async_computation.2 | async-start | bytes 6291456 | tf_op jit(solution)/shard_map/all_gather | solution.py:215
  9.5 35.5 %collective-permute-start.4 = (bf16[2,1,64,2048]{3,2,1,0:T(8,128)(2,1)}, bf16[2,1,64,2048]{3,2,1,0:T(8,128)(2,1)}, u32[]{:S(2)}, u32[]{:S(2)}) collective-permute-start(bf16[2,1,64,2048]{3,2,1,0:T(8,128)(2,1)} %dynamic-slice_bitcast_fusion.3), channel_id=1, source_target_pairs={{0,2},{1,3},{2,0},{3,1},{4,6},{5,7},{6,4},{7,5},{8,10},{9,11},{10,... | collective-permute-start | bytes 1572872 | tf_op jit(solution)/shard_map/ppermute | solution.py:34
  13.0 41.3 %collective-permute-start.15 = (bf16[256,2048]{1,0:T(8,128)(2,1)S(1)}, bf16[256,2048]{1,0:T(8,128)(2,1)}, u32[]{:S(2)}, u32[]{:S(2)}) collective-permute-start(bf16[256,2048]{1,0:T(8,128)(2,1)S(1)} %bitcast.163), channel_id=1, source_target_pairs={{16,0},{17,1},{18,2},{19,3},{20,4},{21,5},{22,6},{23,7},{24,8},{25... | collective-permute-start | bytes 3145736 | tf_op jit(solution)/shard_map/ppermute | solution.py:19
  14.7 16.8 %collective-permute-start.2 = (bf16[2,64,1024]{2,1,0:T(8,128)(2,1)S(1)}, bf16[2,64,1024]{2,1,0:T(8,128)(2,1)S(1)}, u32[]{:S(2)}, u32[]{:S(2)}) collective-permute-start(bf16[2,64,1024]{2,1,0:T(8,128)(2,1)S(1)} %pad_maximum_fusion.1), channel_id=1, source_target_pairs={{0,8},{4,12},{8,0},{12,4},{1,9},{5,13},{9,1},{13,5},{2,10},{6,14},... | collective-permute-start | bytes 786440 | tf_op jit(solution)/shard_map/ppermute | solution.py:134
  18.6 19.3 %collective-permute-start.3 = (bf16[2,64,1024]{2,1,0:T(8,128)(2,1)S(1)}, bf16[2,64,1024]{2,1,0:T(8,128)(2,1)S(1)}, u32[]{:S(2)}, u32[]{:S(2)}) collective-permute-start(bf16[2,64,1024]{2,1,0:T(8,128)(2,1)S(1)} %pad_maximum_fusion.1), channel_id=1, source_target_pairs={{0,12},{4,0},{8,4},{12,8},{1,13},{5,1},{9,5},{13,9},{2,14},{6,2},{... | collective-permute-start | bytes 786440 | tf_op jit(solution)/shard_map/ppermute | solution.py:134
  19.9 17.9 %collective-permute-start.1 = (bf16[2,64,1024]{2,1,0:T(8,128)(2,1)S(1)}, bf16[2,64,1024]{2,1,0:T(8,128)(2,1)S(1)}, u32[]{:S(2)}, u32[]{:S(2)}) collective-permute-start(bf16[2,64,1024]{2,1,0:T(8,128)(2,1)S(1)} %pad_maximum_fusion.1), channel_id=1, source_target_pairs={{0,4},{4,8},{8,12},{12,0},{1,5},{5,9},{9,13},{13,1},{2,6},{6,10},{... | collective-permute-start | bytes 786440 | tf_op jit(solution)/shard_map/ppermute | solution.py:134
  42.0 27.0 %collective-permute-start.10 = (bf16[4,64,2048]{2,1,0:T(8,128)(2,1)S(1)}, bf16[4,64,2048]{2,1,0:T(8,128)(2,1)S(1)}, u32[]{:S(2)}, u32[]{:S(2)}) collective-permute-start(bf16[4,64,2048]{2,1,0:T(8,128)(2,1)S(1)} %fusion.4), channel_id=1, source_target_pairs={{0,2},{1,3},{2,0},{3,1},{4,6},{5,7},{6,4},{7,5},{8,10},{9,11},{10,... | collective-permute-start | bytes 3145736 | tf_op jit(solution)/shard_map/ppermute | solution.py:34
  46.4 20.5 %collective-permute-start.7 = (bf16[1,64,2048]{2,1,0:T(8,128)(2,1)S(1)}, bf16[1,64,2048]{2,1,0:T(8,128)(2,1)S(1)}, u32[]{:S(2)}, u32[]{:S(2)}) collective-permute-start(bf16[1,64,2048]{2,1,0:T(8,128)(2,1)S(1)} %get-tuple-element.40), channel_id=1, source_target_pairs={{0,8},{1,12},{2,10},{3,14},{4,9},{5,13},{6,11},{7,15},{8,0},{9,4},... | collective-permute-start | bytes 786440 | tf_op jit(solution)/shard_map/ppermute | solution.py:92
  51.7 15.9 %collective-permute-start.8 = (bf16[1,64,2048]{2,1,0:T(8,128)(2,1)S(1)}, bf16[1,64,2048]{2,1,0:T(8,128)(2,1)S(1)}, u32[]{:S(2)}, u32[]{:S(2)}) collective-permute-start(bf16[1,64,2048]{2,1,0:T(8,128)(2,1)S(1)} %get-tuple-element.39), channel_id=1, source_target_pairs={{0,9},{1,13},{2,11},{3,15},{4,8},{5,12},{6,10},{7,14},{8,1},{9,5},... | collective-permute-start | bytes 786440 | tf_op jit(solution)/shard_map/ppermute | solution.py:92
  69.7 18.3 %collective-permute-start.12 = (f32[2,4,64]{2,1,0:T(4,128)S(1)}, f32[2,4,64]{2,1,0:T(4,128)S(1)}, u32[]{:S(2)}, u32[]{:S(2)}) collective-permute-start(f32[2,4,64]{2,1,0:T(4,128)S(1)} %pad_maximum_fusion.2), channel_id=1, source_target_pairs={{0,8},{4,12},{8,0},{12,4},{1,9},{5,13},{9,1},{13,5},{2,10},{6,14},... | collective-permute-start | bytes 6152 | tf_op jit(solution)/shard_map/ppermute | solution.py:134
  80.6 19.1 %collective-permute-start.19 = (bf16[1,64,2048]{2,1,0:T(8,128)(2,1)}, bf16[1,64,2048]{2,1,0:T(8,128)(2,1)S(1)}, u32[]{:S(2)}, u32[]{:S(2)}) collective-permute-start(bf16[1,64,2048]{2,1,0:T(8,128)(2,1)} %get-tuple-element.36), channel_id=1, source_target_pairs={{0,8},{1,12},{2,10},{3,14},{4,9},{5,13},{6,11},{7,15},{8,0},{9,4},... | collective-permute-start | bytes 786440 | tf_op jit(solution)/shard_map/ppermute | solution.py:92
  93.4 15.3 %collective-permute-start.14 = (bf16[4,32,2048]{2,1,0:T(8,128)(2,1)S(1)}, bf16[4,32,2048]{2,1,0:T(8,128)(2,1)S(1)}, u32[]{:S(2)}, u32[]{:S(2)}) collective-permute-start(bf16[4,32,2048]{2,1,0:T(8,128)(2,1)S(1)} %get-tuple-element.47), channel_id=1, source_target_pairs={{16,0},{17,1},{18,2},{19,3},{20,4},{21,5},{22,6},{23,7},{24,8},{25... | collective-permute-start | bytes 1572872 | tf_op jit(solution)/shard_map/ppermute | solution.py:19
  108.9 14.2 %collective-permute-start.22 = (bf16[4,32,2048]{2,1,0:T(8,128)(2,1)S(1)}, bf16[4,32,2048]{2,1,0:T(8,128)(2,1)S(1)}, u32[]{:S(2)}, u32[]{:S(2)}) collective-permute-start(bf16[4,32,2048]{2,1,0:T(8,128)(2,1)S(1)} %fusion.23.refs_0_), channel_id=1, source_target_pairs={{0,2},{1,3},{2,0},{3,1},{4,6},{5,7},{6,4},{7,5},{8,10},{9,11},{10,... | collective-permute-start | bytes 1572872 | tf_op jit(solution)/shard_map/ppermute | solution.py:34
  110.4 18.8 %collective-permute-start.21 = (bf16[4,32,2048]{2,1,0:T(8,128)(2,1)S(1)}, bf16[4,32,2048]{2,1,0:T(8,128)(2,1)S(1)}, u32[]{:S(2)}, u32[]{:S(2)}) collective-permute-start(bf16[4,32,2048]{2,1,0:T(8,128)(2,1)S(1)} %fusion.23.refs_0_), channel_id=1, source_target_pairs={{0,1},{1,0},{2,3},{3,2},{4,5},{5,4},{6,7},{7,6},{8,9},{9,8},{10,11... | collective-permute-start | bytes 1572872 | tf_op jit(solution)/shard_map/ppermute | solution.py:39
  123.6 17.6 %collective-permute-start.26 = (bf16[4,32,2048]{2,1,0:T(8,128)(2,1)}, bf16[4,32,2048]{2,1,0:T(8,128)(2,1)}, u32[]{:S(2)}, u32[]{:S(2)}) collective-permute-start(bf16[4,32,2048]{2,1,0:T(8,128)(2,1)} %get-tuple-element.46), channel_id=1, source_target_pairs={{16,0},{17,1},{18,2},{19,3},{20,4},{21,5},{22,6},{23,7},{24,8},{25... | collective-permute-start | bytes 1572872 | tf_op jit(solution)/shard_map/ppermute | solution.py:19
  124.9 31.4 %all-to-all-start = ((bf16[4,64,2048]{2,1,0:T(8,128)(2,1)}), bf16[4,64,2048]{2,1,0:T(8,128)(2,1)}, u32[]{:S(2)}, u32[]{:S(2)}) async-start(bf16[4,64,2048]{2,1,0:T(8,128)(2,1)} %fusion.14), calls=%async_computation | async-start | bytes 2097152 | tf_op jit(solution)/shard_map/all_to_all | solution.py:43
  156.4 17.9 %collective-permute-start.24 = (bf16[4,32,2048]{2,1,0:T(8,128)(2,1)}, bf16[4,32,2048]{2,1,0:T(8,128)(2,1)}, u32[]{:S(2)}, u32[]{:S(2)}) collective-permute-start(bf16[4,32,2048]{2,1,0:T(8,128)(2,1)} %dynamic-slice_bitcast_fusion.1), channel_id=1, source_target_pairs={{0,4},{4,8},{8,12},{12,0},{1,5},{5,9},{9,13},{13,1},{2,6},{6,10},{... | collective-permute-start | bytes 1572872 | tf_op jit(solution)/shard_map/ppermute | solution.py:282
  168.2 16.9 %collective-permute-start.31 = (bf16[4,32,2048]{2,1,0:T(8,128)(2,1)}, bf16[4,32,2048]{2,1,0:T(8,128)(2,1)}, u32[]{:S(2)}, u32[]{:S(2)}) collective-permute-start(bf16[4,32,2048]{2,1,0:T(8,128)(2,1)} %dynamic-slice_bitcast_fusion), channel_id=1, source_target_pairs={{0,4},{4,8},{8,12},{12,0},{1,5},{5,9},{9,13},{13,1},{2,6},{6,10},{... | collective-permute-start | bytes 1572872 | tf_op jit(solution)/shard_map/ppermute | solution.py:282
  169.9 18.9 %all-to-all-start.1 = ((bf16[4,64,2048]{2,1,0:T(8,128)(2,1)}), bf16[4,64,2048]{2,1,0:T(8,128)(2,1)}, u32[]{:S(2)}, u32[]{:S(2)}) async-start(bf16[4,64,2048]{2,1,0:T(8,128)(2,1)} %all-to-all-done), calls=%async_computation.1 | async-start | bytes 2097152 | tf_op jit(solution)/shard_map/all_to_all | solution.py:43
  176.4 19.9 %collective-permute-start.25 = (bf16[4,32,2048]{2,1,0:T(8,128)(2,1)}, bf16[4,32,2048]{2,1,0:T(8,128)(2,1)}, u32[]{:S(2)}, u32[]{:S(2)}) collective-permute-start(bf16[4,32,2048]{2,1,0:T(8,128)(2,1)} %fusion.20), channel_id=1, source_target_pairs={{0,4},{4,8},{8,12},{12,0},{1,5},{5,9},{9,13},{13,1},{2,6},{6,10},{... | collective-permute-start | bytes 1572872 | tf_op jit(solution)/shard_map/ppermute | solution.py:282
  187.2 20.3 %collective-permute-start.32 = (bf16[4,32,2048]{2,1,0:T(8,128)(2,1)}, bf16[4,32,2048]{2,1,0:T(8,128)(2,1)}, u32[]{:S(2)}, u32[]{:S(2)}) collective-permute-start(bf16[4,32,2048]{2,1,0:T(8,128)(2,1)} %fusion.17), channel_id=1, source_target_pairs={{0,4},{4,8},{8,12},{12,0},{1,5},{5,9},{9,13},{13,1},{2,6},{6,10},{... | collective-permute-start | bytes 1572872 | tf_op jit(solution)/shard_map/ppermute | solution.py:282
  191.9 28.1 %collective-permute-start.34 = (bf16[256,2048]{1,0:T(8,128)(2,1)}, bf16[256,2048]{1,0:T(8,128)(2,1)}, u32[]{:S(2)}, u32[]{:S(2)}) collective-permute-start(bf16[256,2048]{1,0:T(8,128)(2,1)} %fusion.7), channel_id=1, source_target_pairs={{16,0},{17,1},{18,2},{19,3},{20,4},{21,5},{22,6},{23,7},{24,8},{25... | collective-permute-start | bytes 3145736 | tf_op jit(solution)/shard_map/ppermute | solution.py:19
  198.3 20.5 %collective-permute-start.30 = (bf16[4,32,2048]{2,1,0:T(8,128)(2,1)}, bf16[4,32,2048]{2,1,0:T(8,128)(2,1)}, u32[]{:S(2)}, u32[]{:S(2)}) collective-permute-start(bf16[4,32,2048]{2,1,0:T(8,128)(2,1)} %fusion.21), channel_id=1, source_target_pairs={{0,4},{4,8},{8,12},{12,0},{1,5},{5,9},{9,13},{13,1},{2,6},{6,10},{... | collective-permute-start | bytes 1572872 | tf_op jit(solution)/shard_map/ppermute | solution.py:282
  208.9 20.2 %collective-permute-start.33 = (bf16[4,32,2048]{2,1,0:T(8,128)(2,1)S(1)}, bf16[4,32,2048]{2,1,0:T(8,128)(2,1)S(1)}, u32[]{:S(2)}, u32[]{:S(2)}) collective-permute-start(bf16[4,32,2048]{2,1,0:T(8,128)(2,1)S(1)} %fusion.18), channel_id=1, source_target_pairs={{0,4},{4,8},{8,12},{12,0},{1,5},{5,9},{9,13},{13,1},{2,6},{6,10},{... | collective-permute-start | bytes 1572872 | tf_op jit(solution)/shard_map/ppermute | solution.py:282
  (29 other events, 253.2 us)
Sparse Core Ops, SparseCore 0:
  9.6 16.3 all-gather.2

commit v6 on v5

--- a/solution.py
+++ b/solution.py
@@ -189,7 +189,7 @@
         ),
         scratch_shapes=[pltpu.VMEM((n, seq, depth, width), pieces[0].dtype)],
         compiler_params=pltpu.CompilerParams(
-            dimension_semantics=("arbitrary",), vmem_limit_bytes=44 * 1024 * 1024
+            dimension_semantics=("arbitrary",), vmem_limit_bytes=32 * 1024 * 1024
         ),
     )(*pieces, weight)
 
@@ -206,17 +206,14 @@
     kept = lax.dynamic_index_in_dim(mixed, core, 1, keepdims=False)
     given = lax.dynamic_index_in_dim(mixed, 1 - core, 1, keepdims=False)
     given = over_cores(given)
-    cotangent = gather_seq(
-        jnp.concatenate(
-            [jnp.where(core == 0, kept, given), jnp.where(core == 0, given, kept)], axis=2
-        )
-    )
-    pairs = [[t + core for core in range(CORES)] for t in range(0, tp, CORES)]
-    weights = lax.all_gather(kv_weight[0], "tp", axis=0, axis_index_groups=pairs, tiled=True)
+    cotangent = jnp.concatenate([kept, given], axis=2)
+    mlp = after(mlp_grads[0], cotangent)
+    cotangent = gather_seq(cotangent)
+    weights = jnp.concatenate([kv_weight[0], over_cores(kv_weight[0])], axis=0)
 
     branch = mlp_grads[0].astype(jnp.float32)
     grad_one = output_cotangent.astype(jnp.float32) + branch
-    behind = from_behind(mlp_grads[0], "section", -1)
+    behind = from_behind(mlp, "section", -1)
     by_permutes = seq == tp == 2 * CORES
     gain = gain_slab(norm_gain)
     width = gain.shape[1]
@@ -259,18 +256,26 @@
     leaving = [cut(norm_back, c) for c in range(CHUNKS)]
     arrivals = [from_behind(part, "section", -1) for part in leaving]
     home = mix_features(after(norm_back, leaving[-1]))
-    attn_parts = []
+    blocks_of = []
     for c in range(CHUNKS):
         part = cut(base, c)
-        arriving = arrivals[c] if c == 0 else after(arrivals[c], attn_parts[-1][0])
+        arriving = arrivals[c]
+        if c > 0:
+            arriving = after(arriving, blocks[-1])
         grad_zero = arriving.astype(jnp.float32) + part.astype(jnp.float32)
         grad = jnp.where(upstream, grad_zero.astype(jnp.bfloat16), part)
         blocks = [over_rows(grad, turn) if turn else grad for turn in range(row)]
+        blocks_of.append(blocks)
+    attn_parts = []
+    for c, blocks in enumerate(blocks_of):
+        if c > 0:
+            blocks[-1] = after(blocks[-1], attn_parts[-1][0])
         pieces = [half for block in blocks for half in (block, over_cores(block))]
         terms = product(pieces, out_weight[0])
         first = lax.dynamic_index_in_dim(terms, (place - 1) % seq, 0, keepdims=False)
+        if c == 0:
+            first = after(first, home)
         attn_parts.append([first, terms])
-    attn_parts[0][0] = after(attn_parts[0][0], home)
     home = exchange(after(home, attn_parts[-1][0]), "tp")
     home = home.reshape(tokens, -1).astype(jnp.float32)
     own = (grad_one + home).astype(jnp.bfloat16)

time: 240 us -> 215 us (0.90)
  waiting for transfers between devices: 103 us -> 82.4 us
  between operations: 14.8 us -> 1.37 us
  local copies, waits for them, and re-layouts: 9.94 us -> 19.2 us
  starting transfers between devices: 63.8 us -> 68 us
  Pallas kernels: 15 us -> 12 us
    ppermute x5, waiting for transfers between devices: 25.9 us -> 4.66 us  [over_rows(): lax.ppermute(block, 'tp', [(t, (t + turn * CORES) % tp) for t in range(tp)])]
    unnamed x30 -> x32, local copies, waits for them, and re-layouts: 5.25 us -> 14.1 us
    pallas_call x2, Pallas kernels: 15 us -> 12 us  [product(): pl.pallas_call(product_kernel, out_shape=jax.ShapeDtypeStruct((seq, n, de...]
    all_to_all x2, starting transfers between devices: 8.68 us -> 11.4 us  [exchange(): return lax.all_to_all(block, axis, 0, 0)]
    ppermute x4, waiting for transfers between devices: 8.75 us -> 11.4 us  [from_behind(): return lax.ppermute(block, axis, route)]
  transfers between devices with their start and end apart: 38 -> 38, of which waited for: 16 -> 16; matrix products, arithmetic and copies ran while one was open for 14% -> 15% of each run, Pallas kernels for 6% -> 6%
where the time goes in v6:
time: 215 us; the launch traced here: 214 us
  waiting for transfers between devices  82.4 us (38%)
  starting transfers between devices  68 us (32%)
  other arithmetic  25.1 us (12%)
  local copies, waits for them, and re-layouts  19.2 us (9%)
  Pallas kernels  12 us (6%)
  matrix products  5.71 us (3%)
    ppermute x6, waiting for transfers between devices, body(): total = lax.ppermute(mine, 'seq', [(q, (q + 1) % seq) for q in range(seq)])  37.3 us
    ppermute x8, starting transfers between devices, spread(): moved = lax.ppermute(piece, ('seq', 'tp'), route)  19 us
    ppermute x6, waiting for transfers between devices, gather_seq(): arrived.append(lax.ppermute(block, 'seq', route))  16.1 us
    ppermute x6, starting transfers between devices, gather_seq(): arrived.append(lax.ppermute(block, 'seq', route))  15.1 us
    unnamed x32, local copies, waits for them, and re-layouts  14.1 us
    pallas_call x2, Pallas kernels, product(): pl.pallas_call(product_kernel, out_shape=jax.ShapeDtypeStruct((seq, n, de...  12 us
    all_to_all x2, starting transfers between devices, exchange(): return lax.all_to_all(block, axis, 0, 0)  11.4 us
    ppermute x4, waiting for transfers between devices, from_behind(): return lax.ppermute(block, axis, route)  11.4 us
  transfers between devices with their start and end apart: 38, of which 16 were waited for; matrix products, arithmetic and copies ran while one was open for 15% of the time, Pallas kernels for 6%

profile of v6, /device:TPU:0, one launch (start us, length us, event | category | flops | bytes accessed | tf_op | source)
XLA Modules:
  0.0 213.8 jit_solution(13887789525916324399)
XLA Ops:
  7.4 3.9 %collective-permute-start.2 = (bf16[2,64,1024]{2,1,0:T(8,128)(2,1)S(1)}, bf16[2,64,1024]{2,1,0:T(8,128)(2,1)S(1)}, u32[]{:S(2)}, u32[]{:S(2)}) collective-permute-start(bf16[2,64,1024]{2,1,0:T(8,128)(2,1)S(1)} %pad_maximum_fusion.1), channel_id=1, source_target_pairs={{0,8},{4,12},{8,0},{12,4},{1,9},{5,13},{9,1},{13,5},{2,10},{6,14},... | collective-permute-start | bytes 786440 | tf_op jit(solution)/shard_map/ppermute | solution.py:134
  13.4 11.3 %collective-permute-done.2 = bf16[2,64,1024]{2,1,0:T(8,128)(2,1)S(1)} collective-permute-done((bf16[2,64,1024]{2,1,0:T(8,128)(2,1)S(1)}, bf16[2,64,1024]{2,1,0:T(8,128)(2,1)S(1)}, u32[]{:S(2)}, u32[]{:S(2)}) %collective-permute-start.2) | collective-permute-done | bytes 262176 | tf_op jit(solution)/shard_map/ppermute | solution.py:134
  26.0 4.8 %collective-permute-done.3 = bf16[2,64,1024]{2,1,0:T(8,128)(2,1)S(1)} collective-permute-done((bf16[2,64,1024]{2,1,0:T(8,128)(2,1)S(1)}, bf16[2,64,1024]{2,1,0:T(8,128)(2,1)S(1)}, u32[]{:S(2)}, u32[]{:S(2)}) %collective-permute-start.3) | collective-permute-done | bytes 262176 | tf_op jit(solution)/shard_map/ppermute | solution.py:134
  38.5 5.5 %collective-permute-start.8 = (bf16[1,64,2048]{2,1,0:T(8,128)(2,1)S(1)}, bf16[1,64,2048]{2,1,0:T(8,128)(2,1)S(1)}, u32[]{:S(2)}, u32[]{:S(2)}) collective-permute-start(bf16[1,64,2048]{2,1,0:T(8,128)(2,1)S(1)} %get-tuple-element.44), channel_id=1, source_target_pairs={{0,8},{1,12},{2,10},{3,14},{4,9},{5,13},{6,11},{7,15},{8,0},{9,4},... | collective-permute-start | bytes 786440 | tf_op jit(solution)/shard_map/ppermute | solution.py:92
  46.4 6.2 %collective-permute-done.16 = bf16[256,2048]{1,0:T(8,128)(2,1)S(1)} collective-permute-done((bf16[256,2048]{1,0:T(8,128)(2,1)S(1)}, bf16[256,2048]{1,0:T(8,128)(2,1)S(1)}, u32[]{:S(2)}, u32[]{:S(2)}) %collective-permute-start.16) | collective-permute-done | bytes 1048608 | tf_op jit(solution)/shard_map/ppermute | solution.py:19
  62.4 6.3 %collective-permute-start.13 = (f32[2,4,64]{2,1,0:T(4,128)S(1)}, f32[2,4,64]{2,1,0:T(4,128)S(1)}, u32[]{:S(2)}, u32[]{:S(2)}) collective-permute-start(f32[2,4,64]{2,1,0:T(4,128)S(1)} %pad_maximum_fusion.2), channel_id=1, source_target_pairs={{0,8},{4,12},{8,0},{12,4},{1,9},{5,13},{9,1},{13,5},{2,10},{6,14},... | collective-permute-start | bytes 6152 | tf_op jit(solution)/shard_map/ppermute | solution.py:134
  71.8 5.5 %collective-permute-start.20 = (bf16[1,64,2048]{2,1,0:T(8,128)(2,1)S(1)}, bf16[1,64,2048]{2,1,0:T(8,128)(2,1)S(1)}, u32[]{:S(2)}, u32[]{:S(2)}) collective-permute-start(bf16[1,64,2048]{2,1,0:T(8,128)(2,1)S(1)} %get-tuple-element.40), channel_id=1, source_target_pairs={{0,8},{1,12},{2,10},{3,14},{4,9},{5,13},{6,11},{7,15},{8,0},{9,4},... | collective-permute-start | bytes 786440 | tf_op jit(solution)/shard_map/ppermute | solution.py:92
  77.3 3.3 %collective-permute-start.21 = (bf16[1,64,2048]{2,1,0:T(8,128)(2,1)S(1)}, bf16[1,64,2048]{2,1,0:T(8,128)(2,1)S(1)}, u32[]{:S(2)}, u32[]{:S(2)}) collective-permute-start(bf16[1,64,2048]{2,1,0:T(8,128)(2,1)S(1)} %get-tuple-element.39), channel_id=1, source_target_pairs={{0,9},{1,13},{2,11},{3,15},{4,8},{5,12},{6,10},{7,14},{8,1},{9,5},... | collective-permute-start | bytes 786440 | tf_op jit(solution)/shard_map/ppermute | solution.py:92
  86.5 8.9 %collective-permute-done.20 = bf16[1,64,2048]{2,1,0:T(8,128)(2,1)S(1)} collective-permute-done((bf16[1,64,2048]{2,1,0:T(8,128)(2,1)S(1)}, bf16[1,64,2048]{2,1,0:T(8,128)(2,1)S(1)}, u32[]{:S(2)}, u32[]{:S(2)}) %collective-permute-start.20) | collective-permute-done | bytes 262176 | tf_op jit(solution)/shard_map/ppermute | solution.py:92
  96.7 3.6 %collective-permute-done.15 = bf16[4,32,2048]{2,1,0:T(8,128)(2,1)S(1)} collective-permute-done((bf16[4,32,2048]{2,1,0:T(8,128)(2,1)S(1)}, bf16[4,32,2048]{2,1,0:T(8,128)(2,1)S(1)}, u32[]{:S(2)}, u32[]{:S(2)}) %collective-permute-start.15) | collective-permute-done | bytes 524320 | tf_op jit(solution)/shard_map/ppermute | solution.py:19
  104.3 7.2 %all-to-all-start = ((bf16[4,64,2048]{2,1,0:T(8,128)(2,1)}), bf16[4,64,2048]{2,1,0:T(8,128)(2,1)}, u32[]{:S(2)}, u32[]{:S(2)}) async-start(bf16[4,64,2048]{2,1,0:T(8,128)(2,1)} %fusion.10), calls=%async_computation | async-start | bytes 2097152 | tf_op jit(solution)/shard_map/all_to_all | solution.py:43
  111.5 3.1 %collective-permute-done.23.refs_2_ = bf16[4,32,2048]{2,1,0:T(8,128)(2,1)S(1)} collective-permute-done((bf16[4,32,2048]{2,1,0:T(8,128)(2,1)S(1)}, bf16[4,32,2048]{2,1,0:T(8,128)(2,1)S(1)}, u32[]{:S(2)}, u32[]{:S(2)}) %collective-permute-start.23) | collective-permute-done | bytes 524320 | tf_op jit(solution)/shard_map/ppermute | solution.py:34
  123.5 3.4 %copy-done.1 = bf16[1,2048,2048]{2,1,0:T(8,128)(2,1)S(1)} copy-done((bf16[1,2048,2048]{2,1,0:T(8,128)(2,1)S(1)}, bf16[1,2048,2048]{2,1,0:T(8,128)(2,1)}, u32[]{:S(2)}) %copy-start.1) | copy-done | bytes 8388632
  130.0 5.4 %shard_map.86 = bf16[4,4,32,2048]{3,2,1,0:T(8,128)(2,1)S(1)} custom-call(bf16[4,32,2048]{2,1,0:T(8,128)(2,1)S(1)} %fusion.19.refs_0_, bf16[4,32,2048]{2,1,0:T(8,128)(2,1)S(1)} %copy-done.6, bf16[4,32,2048]{2,1,0:T(8,128)(2,1)S(1)} %copy-done.4, bf16[4,32,2048]{2,1,0:T(8,128)(2,1)S(1)} %copy-done.8, bf16[2048,2048]{1,0:T(8,128)(2,1)S(1)} %bitcast.161), custom_call_target="tpu_custom_call" | custom-call | flops 4294967296 | bytes 10485760 | tf_op jit(solution)/shard_map/pallas_call | solution.py:178
  138.3 3.4 %copy-done.2 = bf16[1,2048,2048]{2,1,0:T(8,128)(2,1)S(1)} copy-done((bf16[1,2048,2048]{2,1,0:T(8,128)(2,1)S(1)}, bf16[1,2048,2048]{2,1,0:T(8,128)(2,1)}, u32[]{:S(2)}) %copy-start.2) | copy-done | bytes 8388632
  141.7 6.6 %shard_map.87 = bf16[4,4,32,2048]{3,2,1,0:T(8,128)(2,1)S(1)} custom-call(bf16[4,32,2048]{2,1,0:T(8,128)(2,1)S(1)} %fusion.20.refs_0_, bf16[4,32,2048]{2,1,0:T(8,128)(2,1)} %collective-permute-done.28.refs_1_, bf16[4,32,2048]{2,1,0:T(8,128)(2,1)} %collective-permute-done.29.refs_2_, bf16[4,32,2048]{2,1,0:T(8,128)(2,1)S(1)} %collective-permute-done.30.refs_3_, ...), custom_call_target="tpu_custom_call" | custom-call | flops 4294967296 | bytes 10485760 | tf_op jit(solution)/shard_map/pallas_call | solution.py:178
  151.8 4.2 %all-to-all-start.1 = ((bf16[4,64,2048]{2,1,0:T(8,128)(2,1)}), bf16[4,64,2048]{2,1,0:T(8,128)(2,1)}, u32[]{:S(2)}, u32[]{:S(2)}) async-start(bf16[4,64,2048]{2,1,0:T(8,128)(2,1)} %all-to-all-done), calls=%async_computation.1 | async-start | bytes 2097152 | tf_op jit(solution)/shard_map/all_to_all | solution.py:43
  158.9 8.6 %collective-permute-done.32 = bf16[4,32,2048]{2,1,0:T(8,128)(2,1)} collective-permute-done((bf16[4,32,2048]{2,1,0:T(8,128)(2,1)}, bf16[4,32,2048]{2,1,0:T(8,128)(2,1)}, u32[]{:S(2)}, u32[]{:S(2)}) %collective-permute-start.32) | collective-permute-done | bytes 524320 | tf_op jit(solution)/shard_map/ppermute | solution.py:287
  170.5 3.1 %fusion.3 = bf16[256,2048]{1,0:T(8,128)(2,1)} fusion(bf16[256,2048]{1,0:T(8,128)(2,1)} %param.12, bf16[4,64,2048]{2,1,0:T(8,128)(2,1)} %all-to-all-done.1, bf16[1,256,2048]{2,1,0:T(8,128)(2,1)S(1)} %copy-done.10), kind=kLoop, calls=%fused_computation.12 | loop fusion | flops 3145728 | bytes 4194304 | tf_op jit(solution)/shard_map/convert_element_type | solution.py:281
  174.9 3.8 %collective-permute-done.26 = bf16[4,32,2048]{2,1,0:T(8,128)(2,1)} collective-permute-done((bf16[4,32,2048]{2,1,0:T(8,128)(2,1)}, bf16[4,32,2048]{2,1,0:T(8,128)(2,1)}, u32[]{:S(2)}, u32[]{:S(2)}) %collective-permute-start.26) | collective-permute-done | bytes 524320 | tf_op jit(solution)/shard_map/ppermute | solution.py:287
  180.6 9.3 %collective-permute-done.33 = bf16[4,32,2048]{2,1,0:T(8,128)(2,1)} collective-permute-done((bf16[4,32,2048]{2,1,0:T(8,128)(2,1)}, bf16[4,32,2048]{2,1,0:T(8,128)(2,1)}, u32[]{:S(2)}, u32[]{:S(2)}) %collective-permute-start.33) | collective-permute-done | bytes 524320 | tf_op jit(solution)/shard_map/ppermute | solution.py:287
  191.3 9.8 %collective-permute-done.31 = bf16[4,32,2048]{2,1,0:T(8,128)(2,1)} collective-permute-done((bf16[4,32,2048]{2,1,0:T(8,128)(2,1)}, bf16[4,32,2048]{2,1,0:T(8,128)(2,1)}, u32[]{:S(2)}, u32[]{:S(2)}) %collective-permute-start.31) | collective-permute-done | bytes 524320 | tf_op jit(solution)/shard_map/ppermute | solution.py:287
  202.3 3.3 %fusion.12 = bf16[256,2048]{1,0:T(8,128)(2,1)} fusion(bf16[256,2048]{1,0:T(8,128)(2,1)} %collective-permute-done.35, bf16[4,64,2048]{2,1,0:T(8,128)(2,1)} %all-to-all-done.1, pred[]{:T(512)S(6)} %eq.79, bf16[1,256,2048]{2,1,0:T(8,128)(2,1)S(1)} %copy-done.10, bf16[256,2048]{1,0:T(8,128)(2,1)S(1)} %copy-done.12), kind=kLoop, calls=%fused_computation.30 | loop fusion | flops 5767168 | bytes 5242881 | tf_op jit(solution)/shard_map/jit(_where)/select_n | solution.py:284
  205.6 5.9 %collective-permute-done.34 = bf16[4,32,2048]{2,1,0:T(8,128)(2,1)S(1)} collective-permute-done((bf16[4,32,2048]{2,1,0:T(8,128)(2,1)S(1)}, bf16[4,32,2048]{2,1,0:T(8,128)(2,1)S(1)}, u32[]{:S(2)}, u32[]{:S(2)}) %collective-permute-start.34) | collective-permute-done | bytes 524320 | tf_op jit(solution)/shard_map/ppermute | solution.py:287
  (126 shorter events, 76.2 us)
Async XLA Ops:
  0.7 30.7 %collective-permute-start.4 = (bf16[512,2048]{1,0:T(8,128)(2,1)}, bf16[512,2048]{1,0:T(8,128)(2,1)}, u32[]{:S(2)}, u32[]{:S(2)}) collective-permute-start(bf16[512,2048]{1,0:T(8,128)(2,1)} %bitcast.176), channel_id=1, source_target_pairs={{0,1},{1,0},{2,3},{3,2},{4,5},{5,4},{6,7},{7,6},{8,9},{9,8},{10,11... | collective-permute-start | bytes 6291464 | tf_op jit(solution)/shard_map/ppermute | solution.py:39
  3.4 34.9 %collective-permute-start.5 = (bf16[2,1,64,2048]{3,2,1,0:T(8,128)(2,1)S(1)}, bf16[2,1,64,2048]{3,2,1,0:T(8,128)(2,1)S(1)}, u32[]{:S(2)}, u32[]{:S(2)}) collective-permute-start(bf16[2,1,64,2048]{3,2,1,0:T(8,128)(2,1)S(1)} %dynamic-slice_bitcast_fusion.3), channel_id=1, source_target_pairs={{0,2},{1,3},{2,0},{3,1},{4,6},{5,7},{6,4},{7,5},{8,10},{9,11},{10,... | collective-permute-start | bytes 1572872 | tf_op jit(solution)/shard_map/ppermute | solution.py:34
  7.4 17.3 %collective-permute-start.2 = (bf16[2,64,1024]{2,1,0:T(8,128)(2,1)S(1)}, bf16[2,64,1024]{2,1,0:T(8,128)(2,1)S(1)}, u32[]{:S(2)}, u32[]{:S(2)}) collective-permute-start(bf16[2,64,1024]{2,1,0:T(8,128)(2,1)S(1)} %pad_maximum_fusion.1), channel_id=1, source_target_pairs={{0,8},{4,12},{8,0},{12,4},{1,9},{5,13},{9,1},{13,5},{2,10},{6,14},... | collective-permute-start | bytes 786440 | tf_op jit(solution)/shard_map/ppermute | solution.py:134
  11.3 19.4 %collective-permute-start.3 = (bf16[2,64,1024]{2,1,0:T(8,128)(2,1)S(1)}, bf16[2,64,1024]{2,1,0:T(8,128)(2,1)S(1)}, u32[]{:S(2)}, u32[]{:S(2)}) collective-permute-start(bf16[2,64,1024]{2,1,0:T(8,128)(2,1)S(1)} %pad_maximum_fusion.1), channel_id=1, source_target_pairs={{0,12},{4,0},{8,4},{12,8},{1,13},{5,1},{9,5},{13,9},{2,14},{6,2},{... | collective-permute-start | bytes 786440 | tf_op jit(solution)/shard_map/ppermute | solution.py:134
  12.7 18.0 %collective-permute-start.1 = (bf16[2,64,1024]{2,1,0:T(8,128)(2,1)S(1)}, bf16[2,64,1024]{2,1,0:T(8,128)(2,1)S(1)}, u32[]{:S(2)}, u32[]{:S(2)}) collective-permute-start(bf16[2,64,1024]{2,1,0:T(8,128)(2,1)S(1)} %pad_maximum_fusion.1), channel_id=1, source_target_pairs={{0,4},{4,8},{8,12},{12,0},{1,5},{5,9},{9,13},{13,1},{2,6},{6,10},{... | collective-permute-start | bytes 786440 | tf_op jit(solution)/shard_map/ppermute | solution.py:134
  24.7 27.9 %collective-permute-start.16 = (bf16[256,2048]{1,0:T(8,128)(2,1)S(1)}, bf16[256,2048]{1,0:T(8,128)(2,1)S(1)}, u32[]{:S(2)}, u32[]{:S(2)}) collective-permute-start(bf16[256,2048]{1,0:T(8,128)(2,1)S(1)} %bitcast.163), channel_id=1, source_target_pairs={{16,0},{17,1},{18,2},{19,3},{20,4},{21,5},{22,6},{23,7},{24,8},{25... | collective-permute-start | bytes 3145736 | tf_op jit(solution)/shard_map/ppermute | solution.py:19
  35.5 26.2 %collective-permute-start.11 = (bf16[4,64,2048]{2,1,0:T(8,128)(2,1)S(1)}, bf16[4,64,2048]{2,1,0:T(8,128)(2,1)S(1)}, u32[]{:S(2)}, u32[]{:S(2)}) collective-permute-start(bf16[4,64,2048]{2,1,0:T(8,128)(2,1)S(1)} %fusion.2), channel_id=1, source_target_pairs={{0,2},{1,3},{2,0},{3,1},{4,6},{5,7},{6,4},{7,5},{8,10},{9,11},{10,... | collective-permute-start | bytes 3145736 | tf_op jit(solution)/shard_map/ppermute | solution.py:34
  38.5 20.5 %collective-permute-start.8 = (bf16[1,64,2048]{2,1,0:T(8,128)(2,1)S(1)}, bf16[1,64,2048]{2,1,0:T(8,128)(2,1)S(1)}, u32[]{:S(2)}, u32[]{:S(2)}) collective-permute-start(bf16[1,64,2048]{2,1,0:T(8,128)(2,1)S(1)} %get-tuple-element.44), channel_id=1, source_target_pairs={{0,8},{1,12},{2,10},{3,14},{4,9},{5,13},{6,11},{7,15},{8,0},{9,4},... | collective-permute-start | bytes 786440 | tf_op jit(solution)/shard_map/ppermute | solution.py:92
  44.0 15.9 %collective-permute-start.9 = (bf16[1,64,2048]{2,1,0:T(8,128)(2,1)S(1)}, bf16[1,64,2048]{2,1,0:T(8,128)(2,1)S(1)}, u32[]{:S(2)}, u32[]{:S(2)}) collective-permute-start(bf16[1,64,2048]{2,1,0:T(8,128)(2,1)S(1)} %get-tuple-element.43), channel_id=1, source_target_pairs={{0,9},{1,13},{2,11},{3,15},{4,8},{5,12},{6,10},{7,14},{8,1},{9,5},... | collective-permute-start | bytes 786440 | tf_op jit(solution)/shard_map/ppermute | solution.py:92
  62.4 18.2 %collective-permute-start.13 = (f32[2,4,64]{2,1,0:T(4,128)S(1)}, f32[2,4,64]{2,1,0:T(4,128)S(1)}, u32[]{:S(2)}, u32[]{:S(2)}) collective-permute-start(f32[2,4,64]{2,1,0:T(4,128)S(1)} %pad_maximum_fusion.2), channel_id=1, source_target_pairs={{0,8},{4,12},{8,0},{12,4},{1,9},{5,13},{9,1},{13,5},{2,10},{6,14},... | collective-permute-start | bytes 6152 | tf_op jit(solution)/shard_map/ppermute | solution.py:134
  71.8 23.7 %collective-permute-start.20 = (bf16[1,64,2048]{2,1,0:T(8,128)(2,1)S(1)}, bf16[1,64,2048]{2,1,0:T(8,128)(2,1)S(1)}, u32[]{:S(2)}, u32[]{:S(2)}) collective-permute-start(bf16[1,64,2048]{2,1,0:T(8,128)(2,1)S(1)} %get-tuple-element.40), channel_id=1, source_target_pairs={{0,8},{1,12},{2,10},{3,14},{4,9},{5,13},{6,11},{7,15},{8,0},{9,4},... | collective-permute-start | bytes 786440 | tf_op jit(solution)/shard_map/ppermute | solution.py:92
  77.3 18.2 %collective-permute-start.21 = (bf16[1,64,2048]{2,1,0:T(8,128)(2,1)S(1)}, bf16[1,64,2048]{2,1,0:T(8,128)(2,1)S(1)}, u32[]{:S(2)}, u32[]{:S(2)}) collective-permute-start(bf16[1,64,2048]{2,1,0:T(8,128)(2,1)S(1)} %get-tuple-element.39), channel_id=1, source_target_pairs={{0,9},{1,13},{2,11},{3,15},{4,8},{5,12},{6,10},{7,14},{8,1},{9,5},... | collective-permute-start | bytes 786440 | tf_op jit(solution)/shard_map/ppermute | solution.py:92
  85.2 15.1 %collective-permute-start.15 = (bf16[4,32,2048]{2,1,0:T(8,128)(2,1)S(1)}, bf16[4,32,2048]{2,1,0:T(8,128)(2,1)S(1)}, u32[]{:S(2)}, u32[]{:S(2)}) collective-permute-start(bf16[4,32,2048]{2,1,0:T(8,128)(2,1)S(1)} %get-tuple-element.51), channel_id=1, source_target_pairs={{16,0},{17,1},{18,2},{19,3},{20,4},{21,5},{22,6},{23,7},{24,8},{25... | collective-permute-start | bytes 1572872 | tf_op jit(solution)/shard_map/ppermute | solution.py:19
  103.0 15.2 %collective-permute-start.27 = (bf16[4,32,2048]{2,1,0:T(8,128)(2,1)S(1)}, bf16[4,32,2048]{2,1,0:T(8,128)(2,1)S(1)}, u32[]{:S(2)}, u32[]{:S(2)}) collective-permute-start(bf16[4,32,2048]{2,1,0:T(8,128)(2,1)S(1)} %get-tuple-element.50), channel_id=1, source_target_pairs={{16,0},{17,1},{18,2},{19,3},{20,4},{21,5},{22,6},{23,7},{24,8},{25... | collective-permute-start | bytes 1572872 | tf_op jit(solution)/shard_map/ppermute | solution.py:19
  104.3 32.0 %all-to-all-start = ((bf16[4,64,2048]{2,1,0:T(8,128)(2,1)}), bf16[4,64,2048]{2,1,0:T(8,128)(2,1)}, u32[]{:S(2)}, u32[]{:S(2)}) async-start(bf16[4,64,2048]{2,1,0:T(8,128)(2,1)} %fusion.10), calls=%async_computation | async-start | bytes 2097152 | tf_op jit(solution)/shard_map/all_to_all | solution.py:43
  119.3 18.3 %collective-permute-start.28 = (bf16[4,32,2048]{2,1,0:T(8,128)(2,1)S(1)}, bf16[4,32,2048]{2,1,0:T(8,128)(2,1)}, u32[]{:S(2)}, u32[]{:S(2)}) collective-permute-start(bf16[4,32,2048]{2,1,0:T(8,128)(2,1)S(1)} %fusion.20.refs_0_), channel_id=1, source_target_pairs={{0,1},{1,0},{2,3},{3,2},{4,5},{5,4},{6,7},{7,6},{8,9},{9,8},{10,11... | collective-permute-start | bytes 1572872 | tf_op jit(solution)/shard_map/ppermute | solution.py:39
  136.2 19.8 %collective-permute-start.25 = (bf16[4,32,2048]{2,1,0:T(8,128)(2,1)}, bf16[4,32,2048]{2,1,0:T(8,128)(2,1)}, u32[]{:S(2)}, u32[]{:S(2)}) collective-permute-start(bf16[4,32,2048]{2,1,0:T(8,128)(2,1)} %dynamic-slice_bitcast_fusion.1), channel_id=1, source_target_pairs={{0,4},{4,8},{8,12},{12,0},{1,5},{5,9},{9,13},{13,1},{2,6},{6,10},{... | collective-permute-start | bytes 1572872 | tf_op jit(solution)/shard_map/ppermute | solution.py:287
  150.5 16.9 %collective-permute-start.32 = (bf16[4,32,2048]{2,1,0:T(8,128)(2,1)}, bf16[4,32,2048]{2,1,0:T(8,128)(2,1)}, u32[]{:S(2)}, u32[]{:S(2)}) collective-permute-start(bf16[4,32,2048]{2,1,0:T(8,128)(2,1)} %dynamic-slice_bitcast_fusion), channel_id=1, source_target_pairs={{0,4},{4,8},{8,12},{12,0},{1,5},{5,9},{9,13},{13,1},{2,6},{6,10},{... | collective-permute-start | bytes 1572872 | tf_op jit(solution)/shard_map/ppermute | solution.py:287
  151.8 18.8 %all-to-all-start.1 = ((bf16[4,64,2048]{2,1,0:T(8,128)(2,1)}), bf16[4,64,2048]{2,1,0:T(8,128)(2,1)}, u32[]{:S(2)}, u32[]{:S(2)}) async-start(bf16[4,64,2048]{2,1,0:T(8,128)(2,1)} %all-to-all-done), calls=%async_computation.1 | async-start | bytes 2097152 | tf_op jit(solution)/shard_map/all_to_all | solution.py:43
  158.1 20.6 %collective-permute-start.26 = (bf16[4,32,2048]{2,1,0:T(8,128)(2,1)}, bf16[4,32,2048]{2,1,0:T(8,128)(2,1)}, u32[]{:S(2)}, u32[]{:S(2)}) collective-permute-start(bf16[4,32,2048]{2,1,0:T(8,128)(2,1)} %fusion.16), channel_id=1, source_target_pairs={{0,4},{4,8},{8,12},{12,0},{1,5},{5,9},{9,13},{13,1},{2,6},{6,10},{... | collective-permute-start | bytes 1572872 | tf_op jit(solution)/shard_map/ppermute | solution.py:287
  169.6 20.3 %collective-permute-start.33 = (bf16[4,32,2048]{2,1,0:T(8,128)(2,1)}, bf16[4,32,2048]{2,1,0:T(8,128)(2,1)}, u32[]{:S(2)}, u32[]{:S(2)}) collective-permute-start(bf16[4,32,2048]{2,1,0:T(8,128)(2,1)} %fusion.13), channel_id=1, source_target_pairs={{0,4},{4,8},{8,12},{12,0},{1,5},{5,9},{9,13},{13,1},{2,6},{6,10},{... | collective-permute-start | bytes 1572872 | tf_op jit(solution)/shard_map/ppermute | solution.py:287
  173.6 28.7 %collective-permute-start.35 = (bf16[256,2048]{1,0:T(8,128)(2,1)}, bf16[256,2048]{1,0:T(8,128)(2,1)}, u32[]{:S(2)}, u32[]{:S(2)}) collective-permute-start(bf16[256,2048]{1,0:T(8,128)(2,1)} %fusion.3), channel_id=1, source_target_pairs={{16,0},{17,1},{18,2},{19,3},{20,4},{21,5},{22,6},{23,7},{24,8},{25... | collective-permute-start | bytes 3145736 | tf_op jit(solution)/shard_map/ppermute | solution.py:19
  180.6 20.5 %collective-permute-start.31 = (bf16[4,32,2048]{2,1,0:T(8,128)(2,1)}, bf16[4,32,2048]{2,1,0:T(8,128)(2,1)}, u32[]{:S(2)}, u32[]{:S(2)}) collective-permute-start(bf16[4,32,2048]{2,1,0:T(8,128)(2,1)} %fusion.17), channel_id=1, source_target_pairs={{0,4},{4,8},{8,12},{12,0},{1,5},{5,9},{9,13},{13,1},{2,6},{6,10},{... | collective-permute-start | bytes 1572872 | tf_op jit(solution)/shard_map/ppermute | solution.py:287
  191.2 20.2 %collective-permute-start.34 = (bf16[4,32,2048]{2,1,0:T(8,128)(2,1)S(1)}, bf16[4,32,2048]{2,1,0:T(8,128)(2,1)S(1)}, u32[]{:S(2)}, u32[]{:S(2)}) collective-permute-start(bf16[4,32,2048]{2,1,0:T(8,128)(2,1)S(1)} %fusion.14), channel_id=1, source_target_pairs={{0,4},{4,8},{8,12},{12,0},{1,5},{5,9},{9,13},{13,1},{2,6},{6,10},{... | collective-permute-start | bytes 1572872 | tf_op jit(solution)/shard_map/ppermute | solution.py:287
  (30 other events, 266.4 us)

commit v7 on v6

--- a/solution.py
+++ b/solution.py
@@ -1,8 +1,6 @@
 import jax
 import jax.numpy as jnp
 from jax import lax
-from jax.experimental import pallas as pl
-from jax.experimental.pallas import tpu as pltpu
 from jax.sharding import PartitionSpec as P
 
 D = 8192
@@ -149,49 +147,15 @@
     )
 
 
-def product_kernel(*refs):
-    *pieces, weight, out, rows = refs
-    seq, depth, width = pieces[0].shape
-
-    @pl.when(pl.program_id(0) == 0)
-    def _():
-        for i, piece in enumerate(pieces):
-            rows[i] = piece[...]
-
+def product(piece, weight):
     terms = lax.dot_general(
-        rows[...].reshape(-1, width),
-        weight[...],
-        (((1,), (1,)), ((), ())),
-        preferred_element_type=jnp.float32,
-    ).astype(out.dtype)
-    for i in range(len(pieces)):
-        for q in range(seq):
-            start = (i * seq + q) * depth
-            out[q, i] = terms[start : start + depth]
-
-
-def product(pieces, weight):
-    seq, depth, width = pieces[0].shape
-    heads = weight.shape[0]
-    block = min(512, heads)
-    n = len(pieces)
-    return pl.pallas_call(
-        product_kernel,
-        out_shape=jax.ShapeDtypeStruct((seq, n, depth, heads), jnp.bfloat16),
-        grid=(heads // block,),
-        in_specs=[pl.BlockSpec((seq, depth, width), lambda i: (0, 0, 0)) for _ in pieces]
-        + [pl.BlockSpec((block, width), lambda i: (i, 0))],
-        out_specs=pl.BlockSpec((seq, n, depth, block), lambda i: (0, 0, 0, i)),
-        cost_estimate=pl.CostEstimate(
-            flops=2 * n * seq * depth * width * heads,
-            bytes_accessed=2 * heads * width + 2 * n * seq * depth * heads,
-            transcendentals=0,
-        ),
-        scratch_shapes=[pltpu.VMEM((n, seq, depth, width), pieces[0].dtype)],
-        compiler_params=pltpu.CompilerParams(
-            dimension_semantics=("arbitrary",), vmem_limit_bytes=32 * 1024 * 1024
-        ),
-    )(*pieces, weight)
+        piece, weight, (((2,), (1,)), ((), ())), preferred_element_type=jnp.float32
+    )
+    return terms.astype(jnp.bfloat16)
+
+
+def pick(terms, at):
+    return jnp.stack([lax.dynamic_index_in_dim(part, at, 0, keepdims=False) for part in terms], axis=0)
 
 
 def body(layer_input, norm_gain, kv_cotangent, kv_weight, mlp_grads, output_cotangent, out_weight):
@@ -254,25 +218,26 @@
         return array[:, c * depth : (c + 1) * depth]
 
     leaving = [cut(norm_back, c) for c in range(CHUNKS)]
+    if by_permutes:
+        leaving[1:] = [after(part, arrived[0]) for part in leaving[1:]]
     arrivals = [from_behind(part, "section", -1) for part in leaving]
-    home = mix_features(after(norm_back, leaving[-1]))
-    blocks_of = []
+    home = mix_features(after(norm_back, leaving[0]))
+    pieces_of = []
     for c in range(CHUNKS):
         part = cut(base, c)
-        arriving = arrivals[c]
-        if c > 0:
-            arriving = after(arriving, blocks[-1])
+        arriving = arrivals[c] if c == 0 else after(arrivals[c], pieces_of[-1][-1])
         grad_zero = arriving.astype(jnp.float32) + part.astype(jnp.float32)
         grad = jnp.where(upstream, grad_zero.astype(jnp.bfloat16), part)
         blocks = [over_rows(grad, turn) if turn else grad for turn in range(row)]
-        blocks_of.append(blocks)
+        pieces_of.append([half for block in blocks for half in (block, over_cores(block))])
     attn_parts = []
-    for c, blocks in enumerate(blocks_of):
+    for c, pieces in enumerate(pieces_of):
         if c > 0:
-            blocks[-1] = after(blocks[-1], attn_parts[-1][0])
-        pieces = [half for block in blocks for half in (block, over_cores(block))]
-        terms = product(pieces, out_weight[0])
-        first = lax.dynamic_index_in_dim(terms, (place - 1) % seq, 0, keepdims=False)
+            pieces = [after(piece, attn_parts[-1][0]) for piece in pieces]
+        terms = []
+        for piece in pieces:
+            terms.append(product(after(piece, *terms[-1:]), out_weight[0]))
+        first = pick(terms, (place - 1) % seq)
         if c == 0:
             first = after(first, home)
         attn_parts.append([first, terms])
@@ -289,7 +254,7 @@
                 total = after(total, own)
             if c == CHUNKS - 1 and step == seq:
                 total = after(total, input_part)
-            mine = lax.dynamic_index_in_dim(terms, (place - step) % seq, 0, keepdims=False)
+            mine = pick(terms, (place - step) % seq)
             mine = mine.astype(jnp.float32) + total.astype(jnp.float32)
             mine = mine.astype(jnp.bfloat16)
         attn_parts[c] = mine

time: 215 us -> 223 us (1.037)
  matrix products: 5.71 us -> 40.7 us
  waiting for transfers between devices: 82.4 us -> 68.9 us
  Pallas kernels: 12 us -> 0 us
  local copies, waits for them, and re-layouts: 19.2 us -> 10.6 us
  starting transfers between devices: 68 us -> 74.1 us
    dot_general x0 -> x8, matrix products: none -> 35 us  [product(): lax.dot_general(piece, weight, (((2,), (1,)), ((), ())), preferred_elemen...]
    unnamed x32 -> x30, local copies, waits for them, and re-layouts: 14.1 us -> 1.33 us
    pallas_call x2 -> x0, Pallas kernels: 12 us -> none  [product(): pl.pallas_call(product_kernel, out_shape=jax.ShapeDtypeStruct((seq, n, de...]
    ppermute x8, waiting for transfers between devices: 11.2 us -> 6.36 us  [spread(): moved = lax.ppermute(piece, ('seq', 'tp'), route)]
    dynamic_slice x0 -> x6, local copies, waits for them, and re-layouts: none -> 4.85 us  [pick(): lax.dynamic_index_in_dim(part, at, 0, keepdims=False)]
    ppermute x6, starting transfers between devices: 4.47 us -> 9.15 us  [over_cores(): return lax.ppermute(block, 'tp', [(t, t ^ 1) for t in range(tp)])]
    ppermute x6, starting transfers between devices: 3.43 us -> 7.71 us  [body(): total = lax.ppermute(mine, 'seq', [(q, (q + 1) % seq) for q in range(seq)])]
    all_to_all x2, starting transfers between devices: 11.4 us -> 7.8 us  [exchange(): return lax.all_to_all(block, axis, 0, 0)]
  transfers between devices with their start and end apart: 38 -> 38, of which waited for: 16 -> 14; matrix products, arithmetic and copies ran while one was open for 15% -> 34% of each run, Pallas kernels for 6% -> 0%
where the time goes in v7:
time: 223 us; the launch traced here: 222 us
  starting transfers between devices  74.1 us (33%)
  waiting for transfers between devices  68.9 us (31%)
  matrix products  40.7 us (18%)
  other arithmetic  26.2 us (12%)
  local copies, waits for them, and re-layouts  10.6 us (5%)
    ppermute x6, waiting for transfers between devices, body(): total = lax.ppermute(mine, 'seq', [(q, (q + 1) % seq) for q in range(seq)])  35.5 us
    dot_general x8, matrix products, product(): lax.dot_general(piece, weight, (((2,), (1,)), ((), ())), preferred_elemen...  35 us
    ppermute x8, starting transfers between devices, spread(): moved = lax.ppermute(piece, ('seq', 'tp'), route)  18.9 us
    ppermute x6, waiting for transfers between devices, gather_seq(): arrived.append(lax.ppermute(block, 'seq', route))  16.1 us
    ppermute x6, starting transfers between devices, gather_seq(): arrived.append(lax.ppermute(block, 'seq', route))  15.1 us
    ppermute x5, starting transfers between devices, over_rows(): lax.ppermute(block, 'tp', [(t, (t + turn * CORES) % tp) for t in range(tp)])  9.5 us
    ppermute x6, starting transfers between devices, over_cores(): return lax.ppermute(block, 'tp', [(t, t ^ 1) for t in range(tp)])  9.15 us
    convert_element_type x6, other arithmetic, body(): mine = mine.astype(jnp.bfloat16)  9.13 us
  transfers between devices with their start and end apart: 38, of which 14 were waited for; matrix products, arithmetic and copies ran while one was open for 34% of the time, Pallas kernels for 0%

profile of v7, /device:TPU:0, one launch (start us, length us, event | category | flops | bytes accessed | tf_op | source)
XLA Modules:
  0.0 222.0 jit_solution(7759613484176029244)
XLA Ops:
  3.4 3.0 %collective-permute-start.5 = (bf16[2,1,64,2048]{3,2,1,0:T(8,128)(2,1)S(1)}, bf16[2,1,64,2048]{3,2,1,0:T(8,128)(2,1)S(1)}, u32[]{:S(2)}, u32[]{:S(2)}) collective-permute-start(bf16[2,1,64,2048]{3,2,1,0:T(8,128)(2,1)S(1)} %dynamic-slice_bitcast_fusion.1), channel_id=1, source_target_pairs={{0,2},{1,3},{2,0},{3,1},{4,6},{5,7},{6,4},{7,5},{8,10},{9,11},{10,... | collective-permute-start | bytes 1572872 | tf_op jit(solution)/shard_map/ppermute | solution.py:32
  7.5 3.9 %collective-permute-start.2 = (bf16[2,64,1024]{2,1,0:T(8,128)(2,1)S(1)}, bf16[2,64,1024]{2,1,0:T(8,128)(2,1)S(1)}, u32[]{:S(2)}, u32[]{:S(2)}) collective-permute-start(bf16[2,64,1024]{2,1,0:T(8,128)(2,1)S(1)} %pad_maximum_fusion.3), channel_id=1, source_target_pairs={{0,8},{4,12},{8,0},{12,4},{1,9},{5,13},{9,1},{13,5},{2,10},{6,14},... | collective-permute-start | bytes 786440 | tf_op jit(solution)/shard_map/ppermute | solution.py:132
  13.4 11.3 %collective-permute-done.2 = bf16[2,64,1024]{2,1,0:T(8,128)(2,1)S(1)} collective-permute-done((bf16[2,64,1024]{2,1,0:T(8,128)(2,1)S(1)}, bf16[2,64,1024]{2,1,0:T(8,128)(2,1)S(1)}, u32[]{:S(2)}, u32[]{:S(2)}) %collective-permute-start.2) | collective-permute-done | bytes 262176 | tf_op jit(solution)/shard_map/ppermute | solution.py:132
  26.0 4.8 %collective-permute-done.3 = bf16[2,64,1024]{2,1,0:T(8,128)(2,1)S(1)} collective-permute-done((bf16[2,64,1024]{2,1,0:T(8,128)(2,1)S(1)}, bf16[2,64,1024]{2,1,0:T(8,128)(2,1)S(1)}, u32[]{:S(2)}, u32[]{:S(2)}) %collective-permute-start.3) | collective-permute-done | bytes 262176 | tf_op jit(solution)/shard_map/ppermute | solution.py:132
  38.5 5.5 %collective-permute-start.8 = (bf16[1,64,2048]{2,1,0:T(8,128)(2,1)S(1)}, bf16[1,64,2048]{2,1,0:T(8,128)(2,1)S(1)}, u32[]{:S(2)}, u32[]{:S(2)}) collective-permute-start(bf16[1,64,2048]{2,1,0:T(8,128)(2,1)S(1)} %get-tuple-element.64), channel_id=1, source_target_pairs={{0,8},{1,12},{2,10},{3,14},{4,9},{5,13},{6,11},{7,15},{8,0},{9,4},... | collective-permute-start | bytes 786440 | tf_op jit(solution)/shard_map/ppermute | solution.py:90
  46.4 6.1 %collective-permute-done.16 = bf16[256,2048]{1,0:T(8,128)(2,1)S(1)} collective-permute-done((bf16[256,2048]{1,0:T(8,128)(2,1)S(1)}, bf16[256,2048]{1,0:T(8,128)(2,1)S(1)}, u32[]{:S(2)}, u32[]{:S(2)}) %collective-permute-start.16) | collective-permute-done | bytes 1048608 | tf_op jit(solution)/shard_map/ppermute | solution.py:17
  62.5 6.3 %collective-permute-start.13 = (f32[2,4,64]{2,1,0:T(4,128)S(1)}, f32[2,4,64]{2,1,0:T(4,128)S(1)}, u32[]{:S(2)}, u32[]{:S(2)}) collective-permute-start(f32[2,4,64]{2,1,0:T(4,128)S(1)} %pad_maximum_fusion.4), channel_id=1, source_target_pairs={{0,8},{4,12},{8,0},{12,4},{1,9},{5,13},{9,1},{13,5},{2,10},{6,14},... | collective-permute-start | bytes 6152 | tf_op jit(solution)/shard_map/ppermute | solution.py:132
  72.6 5.5 %collective-permute-start.20 = (bf16[1,64,2048]{2,1,0:T(8,128)(2,1)}, bf16[1,64,2048]{2,1,0:T(8,128)(2,1)}, u32[]{:S(2)}, u32[]{:S(2)}) collective-permute-start(bf16[1,64,2048]{2,1,0:T(8,128)(2,1)} %get-tuple-element.60), channel_id=1, source_target_pairs={{0,8},{1,12},{2,10},{3,14},{4,9},{5,13},{6,11},{7,15},{8,0},{9,4},... | collective-permute-start | bytes 786440 | tf_op jit(solution)/shard_map/ppermute | solution.py:90
  78.1 3.3 %collective-permute-start.21 = (bf16[1,64,2048]{2,1,0:T(8,128)(2,1)}, bf16[1,64,2048]{2,1,0:T(8,128)(2,1)}, u32[]{:S(2)}, u32[]{:S(2)}) collective-permute-start(bf16[1,64,2048]{2,1,0:T(8,128)(2,1)} %get-tuple-element.59), channel_id=1, source_target_pairs={{0,9},{1,13},{2,11},{3,15},{4,8},{5,12},{6,10},{7,14},{8,1},{9,5},... | collective-permute-start | bytes 786440 | tf_op jit(solution)/shard_map/ppermute | solution.py:90
  88.3 4.3 %all-to-all-start = ((bf16[4,64,2048]{2,1,0:T(8,128)(2,1)}), bf16[4,64,2048]{2,1,0:T(8,128)(2,1)S(1)}, u32[]{:S(2)}, u32[]{:S(2)}) async-start(bf16[4,64,2048]{2,1,0:T(8,128)(2,1)} %fusion.50), calls=%async_computation | async-start | bytes 2097152 | tf_op jit(solution)/shard_map/all_to_all | solution.py:41
  92.6 4.0 %collective-permute-done.20 = bf16[1,64,2048]{2,1,0:T(8,128)(2,1)} collective-permute-done((bf16[1,64,2048]{2,1,0:T(8,128)(2,1)}, bf16[1,64,2048]{2,1,0:T(8,128)(2,1)}, u32[]{:S(2)}, u32[]{:S(2)}) %collective-permute-start.20) | collective-permute-done | bytes 262176 | tf_op jit(solution)/shard_map/ppermute | solution.py:90
  105.2 8.0 %collective-permute-start.22 = (bf16[4,32,2048]{2,1,0:T(8,128)(2,1)S(1)}, bf16[4,32,2048]{2,1,0:T(8,128)(2,1)S(1)}, u32[]{:S(2)}, u32[]{:S(2)}) collective-permute-start(bf16[4,32,2048]{2,1,0:T(8,128)(2,1)S(1)} %fusion.53), channel_id=1, source_target_pairs={{0,1},{1,0},{2,3},{3,2},{4,5},{5,4},{6,7},{7,6},{8,9},{9,8},{10,11... | collective-permute-start | bytes 1572872 | tf_op jit(solution)/shard_map/ppermute | solution.py:37
  113.2 6.3 %fusion.19 = bf16[4,32,2048]{2,1,0:T(8,128)(2,1)S(1)} fusion(bf16[4,32,2048]{2,1,0:T(8,128)(2,1)S(1)} %fusion.53, bf16[1,2048,2048]{2,1,0:T(8,128)(2,1)} %param.13), kind=kOutput, calls=%fused_computation.28 | convolution fusion | flops 1074003968 | bytes 9437184 | tf_op jit(solution)/shard_map/dot_general | solution.py:151
  136.2 6.6 %fusion.31 = bf16[4,32,2048]{2,1,0:T(8,128)(2,1)S(1)} fusion(bf16[4,32,2048]{2,1,0:T(8,128)(2,1)} %fusion.54, bf16[1,2048,2048]{2,1,0:T(8,128)(2,1)} %param.13), kind=kOutput, calls=%fused_computation.32 | convolution fusion | flops 1074003968 | bytes 9437184 | tf_op jit(solution)/shard_map/dot_general | solution.py:151
  143.3 6.7 %fusion.34 = bf16[4,32,2048]{2,1,0:T(8,128)(2,1)S(1)} fusion(bf16[4,32,2048]{2,1,0:T(8,128)(2,1)} %collective-permute-done.28, bf16[1,2048,2048]{2,1,0:T(8,128)(2,1)} %param.13), kind=kOutput, calls=%fused_computation.33 | convolution fusion | flops 1074003968 | bytes 9437184 | tf_op jit(solution)/shard_map/dot_general | solution.py:151
  150.9 3.9 %fusion.37 = bf16[4,32,2048]{2,1,0:T(8,128)(2,1)S(1)} fusion(bf16[4,32,2048]{2,1,0:T(8,128)(2,1)} %collective-permute-done.29, bf16[1,2048,2048]{2,1,0:T(8,128)(2,1)S(1)} %bitcast.183), kind=kOutput, calls=%fused_computation.34 | convolution fusion | flops 1074003968 | bytes 9437184 | tf_op jit(solution)/shard_map/dot_general | solution.py:151
  154.8 2.9 %fusion.40 = bf16[4,32,2048]{2,1,0:T(8,128)(2,1)S(1)} fusion(bf16[4,32,2048]{2,1,0:T(8,128)(2,1)S(1)} %collective-permute-done.30, bf16[1,2048,2048]{2,1,0:T(8,128)(2,1)S(1)} %bitcast.183), kind=kOutput, calls=%fused_computation.35 | convolution fusion | flops 1074003968 | bytes 9437184 | tf_op jit(solution)/shard_map/dot_general | solution.py:151
  162.0 3.5 %all-to-all-start.1 = ((bf16[4,64,2048]{2,1,0:T(8,128)(2,1)}), bf16[4,64,2048]{2,1,0:T(8,128)(2,1)S(1)}, u32[]{:S(2)}, u32[]{:S(2)}) async-start(bf16[4,64,2048]{2,1,0:T(8,128)(2,1)} %copy-done.2), calls=%async_computation.1 | async-start | bytes 2097152 | tf_op jit(solution)/shard_map/all_to_all | solution.py:41
  169.5 6.8 %collective-permute-done.32 = bf16[4,32,2048]{2,1,0:T(8,128)(2,1)} collective-permute-done((bf16[4,32,2048]{2,1,0:T(8,128)(2,1)}, bf16[4,32,2048]{2,1,0:T(8,128)(2,1)}, u32[]{:S(2)}, u32[]{:S(2)}) %collective-permute-start.32) | collective-permute-done | bytes 524320 | tf_op jit(solution)/shard_map/ppermute | solution.py:252
  182.8 4.7 %collective-permute-done.26 = bf16[4,32,2048]{2,1,0:T(8,128)(2,1)} collective-permute-done((bf16[4,32,2048]{2,1,0:T(8,128)(2,1)}, bf16[4,32,2048]{2,1,0:T(8,128)(2,1)}, u32[]{:S(2)}, u32[]{:S(2)}) %collective-permute-start.26) | collective-permute-done | bytes 524320 | tf_op jit(solution)/shard_map/ppermute | solution.py:252
  190.2 8.5 %collective-permute-done.33 = bf16[4,32,2048]{2,1,0:T(8,128)(2,1)} collective-permute-done((bf16[4,32,2048]{2,1,0:T(8,128)(2,1)}, bf16[4,32,2048]{2,1,0:T(8,128)(2,1)}, u32[]{:S(2)}, u32[]{:S(2)}) %collective-permute-start.33) | collective-permute-done | bytes 524320 | tf_op jit(solution)/shard_map/ppermute | solution.py:252
  200.9 9.1 %collective-permute-done.31 = bf16[4,32,2048]{2,1,0:T(8,128)(2,1)} collective-permute-done((bf16[4,32,2048]{2,1,0:T(8,128)(2,1)}, bf16[4,32,2048]{2,1,0:T(8,128)(2,1)}, u32[]{:S(2)}, u32[]{:S(2)}) %collective-permute-start.31) | collective-permute-done | bytes 524320 | tf_op jit(solution)/shard_map/ppermute | solution.py:252
  211.4 3.0 %fusion.52 = bf16[256,2048]{1,0:T(8,128)(2,1)} fusion(bf16[256,2048]{1,0:T(8,128)(2,1)} %collective-permute-done.35, bf16[4,64,2048]{2,1,0:T(8,128)(2,1)S(1)} %all-to-all-done.1, pred[]{:T(512)S(6)} %eq.79, bf16[1,256,2048]{2,1,0:T(8,128)(2,1)S(1)} %copy-done, bf16[256,2048]{1,0:T(8,128)(2,1)S(1)} %copy-done.1), kind=kLoop, calls=%fused_computation.54 | loop fusion | flops 5767168 | bytes 5242881 | tf_op jit(solution)/shard_map/jit(_where)/select_n | solution.py:249
  214.3 6.4 %collective-permute-done.34 = bf16[4,32,2048]{2,1,0:T(8,128)(2,1)S(1)} collective-permute-done((bf16[4,32,2048]{2,1,0:T(8,128)(2,1)S(1)}, bf16[4,32,2048]{2,1,0:T(8,128)(2,1)S(1)}, u32[]{:S(2)}, u32[]{:S(2)}) %collective-permute-start.34) | collective-permute-done | bytes 524320 | tf_op jit(solution)/shard_map/ppermute | solution.py:252
  (138 shorter events, 86.4 us)
Async XLA Ops:
  0.7 30.7 %collective-permute-start.4 = (bf16[512,2048]{1,0:T(8,128)(2,1)}, bf16[512,2048]{1,0:T(8,128)(2,1)}, u32[]{:S(2)}, u32[]{:S(2)}) collective-permute-start(bf16[512,2048]{1,0:T(8,128)(2,1)} %bitcast.197), channel_id=1, source_target_pairs={{0,1},{1,0},{2,3},{3,2},{4,5},{5,4},{6,7},{7,6},{8,9},{9,8},{10,11... | collective-permute-start | bytes 6291464 | tf_op jit(solution)/shard_map/ppermute | solution.py:37
  3.4 34.9 %collective-permute-start.5 = (bf16[2,1,64,2048]{3,2,1,0:T(8,128)(2,1)S(1)}, bf16[2,1,64,2048]{3,2,1,0:T(8,128)(2,1)S(1)}, u32[]{:S(2)}, u32[]{:S(2)}) collective-permute-start(bf16[2,1,64,2048]{3,2,1,0:T(8,128)(2,1)S(1)} %dynamic-slice_bitcast_fusion.1), channel_id=1, source_target_pairs={{0,2},{1,3},{2,0},{3,1},{4,6},{5,7},{6,4},{7,5},{8,10},{9,11},{10,... | collective-permute-start | bytes 1572872 | tf_op jit(solution)/shard_map/ppermute | solution.py:32
  7.5 17.2 %collective-permute-start.2 = (bf16[2,64,1024]{2,1,0:T(8,128)(2,1)S(1)}, bf16[2,64,1024]{2,1,0:T(8,128)(2,1)S(1)}, u32[]{:S(2)}, u32[]{:S(2)}) collective-permute-start(bf16[2,64,1024]{2,1,0:T(8,128)(2,1)S(1)} %pad_maximum_fusion.3), channel_id=1, source_target_pairs={{0,8},{4,12},{8,0},{12,4},{1,9},{5,13},{9,1},{13,5},{2,10},{6,14},... | collective-permute-start | bytes 786440 | tf_op jit(solution)/shard_map/ppermute | solution.py:132
  11.4 19.4 %collective-permute-start.3 = (bf16[2,64,1024]{2,1,0:T(8,128)(2,1)S(1)}, bf16[2,64,1024]{2,1,0:T(8,128)(2,1)S(1)}, u32[]{:S(2)}, u32[]{:S(2)}) collective-permute-start(bf16[2,64,1024]{2,1,0:T(8,128)(2,1)S(1)} %pad_maximum_fusion.3), channel_id=1, source_target_pairs={{0,12},{4,0},{8,4},{12,8},{1,13},{5,1},{9,5},{13,9},{2,14},{6,2},{... | collective-permute-start | bytes 786440 | tf_op jit(solution)/shard_map/ppermute | solution.py:132
  12.7 18.0 %collective-permute-start.1 = (bf16[2,64,1024]{2,1,0:T(8,128)(2,1)S(1)}, bf16[2,64,1024]{2,1,0:T(8,128)(2,1)S(1)}, u32[]{:S(2)}, u32[]{:S(2)}) collective-permute-start(bf16[2,64,1024]{2,1,0:T(8,128)(2,1)S(1)} %pad_maximum_fusion.3), channel_id=1, source_target_pairs={{0,4},{4,8},{8,12},{12,0},{1,5},{5,9},{9,13},{13,1},{2,6},{6,10},{... | collective-permute-start | bytes 786440 | tf_op jit(solution)/shard_map/ppermute | solution.py:132
  24.7 27.8 %collective-permute-start.16 = (bf16[256,2048]{1,0:T(8,128)(2,1)S(1)}, bf16[256,2048]{1,0:T(8,128)(2,1)S(1)}, u32[]{:S(2)}, u32[]{:S(2)}) collective-permute-start(bf16[256,2048]{1,0:T(8,128)(2,1)S(1)} %bitcast.184), channel_id=1, source_target_pairs={{16,0},{17,1},{18,2},{19,3},{20,4},{21,5},{22,6},{23,7},{24,8},{25... | collective-permute-start | bytes 3145736 | tf_op jit(solution)/shard_map/ppermute | solution.py:17
  35.5 26.2 %collective-permute-start.11 = (bf16[4,64,2048]{2,1,0:T(8,128)(2,1)S(1)}, bf16[4,64,2048]{2,1,0:T(8,128)(2,1)S(1)}, u32[]{:S(2)}, u32[]{:S(2)}) collective-permute-start(bf16[4,64,2048]{2,1,0:T(8,128)(2,1)S(1)} %fusion.18), channel_id=1, source_target_pairs={{0,2},{1,3},{2,0},{3,1},{4,6},{5,7},{6,4},{7,5},{8,10},{9,11},{10,... | collective-permute-start | bytes 3145736 | tf_op jit(solution)/shard_map/ppermute | solution.py:32
  38.5 20.5 %collective-permute-start.8 = (bf16[1,64,2048]{2,1,0:T(8,128)(2,1)S(1)}, bf16[1,64,2048]{2,1,0:T(8,128)(2,1)S(1)}, u32[]{:S(2)}, u32[]{:S(2)}) collective-permute-start(bf16[1,64,2048]{2,1,0:T(8,128)(2,1)S(1)} %get-tuple-element.64), channel_id=1, source_target_pairs={{0,8},{1,12},{2,10},{3,14},{4,9},{5,13},{6,11},{7,15},{8,0},{9,4},... | collective-permute-start | bytes 786440 | tf_op jit(solution)/shard_map/ppermute | solution.py:90
  44.0 15.8 %collective-permute-start.9 = (bf16[1,64,2048]{2,1,0:T(8,128)(2,1)S(1)}, bf16[1,64,2048]{2,1,0:T(8,128)(2,1)S(1)}, u32[]{:S(2)}, u32[]{:S(2)}) collective-permute-start(bf16[1,64,2048]{2,1,0:T(8,128)(2,1)S(1)} %get-tuple-element.63), channel_id=1, source_target_pairs={{0,9},{1,13},{2,11},{3,15},{4,8},{5,12},{6,10},{7,14},{8,1},{9,5},... | collective-permute-start | bytes 786440 | tf_op jit(solution)/shard_map/ppermute | solution.py:90
  62.5 18.9 %collective-permute-start.13 = (f32[2,4,64]{2,1,0:T(4,128)S(1)}, f32[2,4,64]{2,1,0:T(4,128)S(1)}, u32[]{:S(2)}, u32[]{:S(2)}) collective-permute-start(f32[2,4,64]{2,1,0:T(4,128)S(1)} %pad_maximum_fusion.4), channel_id=1, source_target_pairs={{0,8},{4,12},{8,0},{12,4},{1,9},{5,13},{9,1},{13,5},{2,10},{6,14},... | collective-permute-start | bytes 6152 | tf_op jit(solution)/shard_map/ppermute | solution.py:132
  72.6 23.9 %collective-permute-start.20 = (bf16[1,64,2048]{2,1,0:T(8,128)(2,1)}, bf16[1,64,2048]{2,1,0:T(8,128)(2,1)}, u32[]{:S(2)}, u32[]{:S(2)}) collective-permute-start(bf16[1,64,2048]{2,1,0:T(8,128)(2,1)} %get-tuple-element.60), channel_id=1, source_target_pairs={{0,8},{1,12},{2,10},{3,14},{4,9},{5,13},{6,11},{7,15},{8,0},{9,4},... | collective-permute-start | bytes 786440 | tf_op jit(solution)/shard_map/ppermute | solution.py:90
  78.1 18.5 %collective-permute-start.21 = (bf16[1,64,2048]{2,1,0:T(8,128)(2,1)}, bf16[1,64,2048]{2,1,0:T(8,128)(2,1)}, u32[]{:S(2)}, u32[]{:S(2)}) collective-permute-start(bf16[1,64,2048]{2,1,0:T(8,128)(2,1)} %get-tuple-element.59), channel_id=1, source_target_pairs={{0,9},{1,13},{2,11},{3,15},{4,8},{5,12},{6,10},{7,14},{8,1},{9,5},... | collective-permute-start | bytes 786440 | tf_op jit(solution)/shard_map/ppermute | solution.py:90
  87.0 15.4 %collective-permute-start.15 = (bf16[4,32,2048]{2,1,0:T(8,128)(2,1)}, bf16[4,32,2048]{2,1,0:T(8,128)(2,1)}, u32[]{:S(2)}, u32[]{:S(2)}) collective-permute-start(bf16[4,32,2048]{2,1,0:T(8,128)(2,1)} %get-tuple-element.71), channel_id=1, source_target_pairs={{16,0},{17,1},{18,2},{19,3},{20,4},{21,5},{22,6},{23,7},{24,8},{25... | collective-permute-start | bytes 1572872 | tf_op jit(solution)/shard_map/ppermute | solution.py:17
  88.3 46.8 %all-to-all-start = ((bf16[4,64,2048]{2,1,0:T(8,128)(2,1)}), bf16[4,64,2048]{2,1,0:T(8,128)(2,1)S(1)}, u32[]{:S(2)}, u32[]{:S(2)}) async-start(bf16[4,64,2048]{2,1,0:T(8,128)(2,1)} %fusion.50), calls=%async_computation | async-start | bytes 2097152 | tf_op jit(solution)/shard_map/all_to_all | solution.py:41
  97.6 30.2 %collective-permute-start.27 = (bf16[4,32,2048]{2,1,0:T(8,128)(2,1)}, bf16[4,32,2048]{2,1,0:T(8,128)(2,1)S(1)}, u32[]{:S(2)}, u32[]{:S(2)}) collective-permute-start(bf16[4,32,2048]{2,1,0:T(8,128)(2,1)} %get-tuple-element.40), channel_id=1, source_target_pairs={{16,0},{17,1},{18,2},{19,3},{20,4},{21,5},{22,6},{23,7},{24,8},{25... | collective-permute-start | bytes 1572872 | tf_op jit(solution)/shard_map/ppermute | solution.py:17
  103.8 19.4 %collective-permute-start.23 = (bf16[4,32,2048]{2,1,0:T(8,128)(2,1)S(1)}, bf16[4,32,2048]{2,1,0:T(8,128)(2,1)S(1)}, u32[]{:S(2)}, u32[]{:S(2)}) collective-permute-start(bf16[4,32,2048]{2,1,0:T(8,128)(2,1)S(1)} %fusion.53), channel_id=1, source_target_pairs={{0,2},{1,3},{2,0},{3,1},{4,6},{5,7},{6,4},{7,5},{8,10},{9,11},{10,... | collective-permute-start | bytes 1572872 | tf_op jit(solution)/shard_map/ppermute | solution.py:32
  135.1 30.4 %collective-permute-start.25 = (bf16[4,32,2048]{2,1,0:T(8,128)(2,1)}, bf16[4,32,2048]{2,1,0:T(8,128)(2,1)}, u32[]{:S(2)}, u32[]{:S(2)}) collective-permute-start(bf16[4,32,2048]{2,1,0:T(8,128)(2,1)} %pad_maximum_fusion.1), channel_id=1, source_target_pairs={{0,4},{4,8},{8,12},{12,0},{1,5},{5,9},{9,13},{13,1},{2,6},{6,10},{... | collective-permute-start | bytes 1572872 | tf_op jit(solution)/shard_map/ppermute | solution.py:252
  159.4 16.8 %collective-permute-start.32 = (bf16[4,32,2048]{2,1,0:T(8,128)(2,1)}, bf16[4,32,2048]{2,1,0:T(8,128)(2,1)}, u32[]{:S(2)}, u32[]{:S(2)}) collective-permute-start(bf16[4,32,2048]{2,1,0:T(8,128)(2,1)} %pad_maximum_fusion.2), channel_id=1, source_target_pairs={{0,4},{4,8},{8,12},{12,0},{1,5},{5,9},{9,13},{13,1},{2,6},{6,10},{... | collective-permute-start | bytes 1572872 | tf_op jit(solution)/shard_map/ppermute | solution.py:252
  162.0 18.0 %all-to-all-start.1 = ((bf16[4,64,2048]{2,1,0:T(8,128)(2,1)}), bf16[4,64,2048]{2,1,0:T(8,128)(2,1)S(1)}, u32[]{:S(2)}, u32[]{:S(2)}) async-start(bf16[4,64,2048]{2,1,0:T(8,128)(2,1)} %copy-done.2), calls=%async_computation.1 | async-start | bytes 2097152 | tf_op jit(solution)/shard_map/all_to_all | solution.py:41
  167.7 19.8 %collective-permute-start.26 = (bf16[4,32,2048]{2,1,0:T(8,128)(2,1)}, bf16[4,32,2048]{2,1,0:T(8,128)(2,1)}, u32[]{:S(2)}, u32[]{:S(2)}) collective-permute-start(bf16[4,32,2048]{2,1,0:T(8,128)(2,1)} %add_convert_fusion.6), channel_id=1, source_target_pairs={{0,4},{4,8},{8,12},{12,0},{1,5},{5,9},{9,13},{13,1},{2,6},{6,10},{... | collective-permute-start | bytes 1572872 | tf_op jit(solution)/shard_map/ppermute | solution.py:252
  178.4 20.3 %collective-permute-start.33 = (bf16[4,32,2048]{2,1,0:T(8,128)(2,1)}, bf16[4,32,2048]{2,1,0:T(8,128)(2,1)}, u32[]{:S(2)}, u32[]{:S(2)}) collective-permute-start(bf16[4,32,2048]{2,1,0:T(8,128)(2,1)} %add_convert_fusion.2), channel_id=1, source_target_pairs={{0,4},{4,8},{8,12},{12,0},{1,5},{5,9},{9,13},{13,1},{2,6},{6,10},{... | collective-permute-start | bytes 1572872 | tf_op jit(solution)/shard_map/ppermute | solution.py:252
  181.5 29.8 %collective-permute-start.35 = (bf16[256,2048]{1,0:T(8,128)(2,1)}, bf16[256,2048]{1,0:T(8,128)(2,1)}, u32[]{:S(2)}, u32[]{:S(2)}) collective-permute-start(bf16[256,2048]{1,0:T(8,128)(2,1)} %fusion.43), channel_id=1, source_target_pairs={{16,0},{17,1},{18,2},{19,3},{20,4},{21,5},{22,6},{23,7},{24,8},{25... | collective-permute-start | bytes 3145736 | tf_op jit(solution)/shard_map/ppermute | solution.py:17
  189.5 20.5 %collective-permute-start.31 = (bf16[4,32,2048]{2,1,0:T(8,128)(2,1)}, bf16[4,32,2048]{2,1,0:T(8,128)(2,1)}, u32[]{:S(2)}, u32[]{:S(2)}) collective-permute-start(bf16[4,32,2048]{2,1,0:T(8,128)(2,1)} %add_convert_fusion.4), channel_id=1, source_target_pairs={{0,4},{4,8},{8,12},{12,0},{1,5},{5,9},{9,13},{13,1},{2,6},{6,10},{... | collective-permute-start | bytes 1572872 | tf_op jit(solution)/shard_map/ppermute | solution.py:252
  200.1 20.6 %collective-permute-start.34 = (bf16[4,32,2048]{2,1,0:T(8,128)(2,1)S(1)}, bf16[4,32,2048]{2,1,0:T(8,128)(2,1)S(1)}, u32[]{:S(2)}, u32[]{:S(2)}) collective-permute-start(bf16[4,32,2048]{2,1,0:T(8,128)(2,1)S(1)} %add_convert_fusion.1), channel_id=1, source_target_pairs={{0,4},{4,8},{8,12},{12,0},{1,5},{5,9},{9,13},{13,1},{2,6},{6,10},{... | collective-permute-start | bytes 1572872 | tf_op jit(solution)/shard_map/ppermute | solution.py:252
  (29 other events, 318.4 us)

commit v8 on v6

--- a/solution.py
+++ b/solution.py
@@ -149,49 +149,43 @@
     )
 
 
-def product_kernel(*refs):
-    *pieces, weight, out, rows = refs
-    seq, depth, width = pieces[0].shape
-
-    @pl.when(pl.program_id(0) == 0)
-    def _():
-        for i, piece in enumerate(pieces):
-            rows[i] = piece[...]
-
+def product_kernel(rows, weight, out):
+    n, seq, depth, width = rows.shape
     terms = lax.dot_general(
         rows[...].reshape(-1, width),
         weight[...],
         (((1,), (1,)), ((), ())),
         preferred_element_type=jnp.float32,
     ).astype(out.dtype)
-    for i in range(len(pieces)):
+    for i in range(n):
         for q in range(seq):
             start = (i * seq + q) * depth
             out[q, i] = terms[start : start + depth]
 
 
 def product(pieces, weight):
-    seq, depth, width = pieces[0].shape
+    rows = jnp.stack(pieces, axis=0)
+    n, seq, depth, width = rows.shape
     heads = weight.shape[0]
     block = min(512, heads)
-    n = len(pieces)
     return pl.pallas_call(
         product_kernel,
         out_shape=jax.ShapeDtypeStruct((seq, n, depth, heads), jnp.bfloat16),
         grid=(heads // block,),
-        in_specs=[pl.BlockSpec((seq, depth, width), lambda i: (0, 0, 0)) for _ in pieces]
-        + [pl.BlockSpec((block, width), lambda i: (i, 0))],
+        in_specs=[
+            pl.BlockSpec((n, seq, depth, width), lambda i: (0, 0, 0, 0)),
+            pl.BlockSpec((block, width), lambda i: (i, 0)),
+        ],
         out_specs=pl.BlockSpec((seq, n, depth, block), lambda i: (0, 0, 0, i)),
         cost_estimate=pl.CostEstimate(
             flops=2 * n * seq * depth * width * heads,
             bytes_accessed=2 * heads * width + 2 * n * seq * depth * heads,
             transcendentals=0,
         ),
-        scratch_shapes=[pltpu.VMEM((n, seq, depth, width), pieces[0].dtype)],
         compiler_params=pltpu.CompilerParams(
-            dimension_semantics=("arbitrary",), vmem_limit_bytes=32 * 1024 * 1024
+            dimension_semantics=("arbitrary",), vmem_limit_bytes=44 * 1024 * 1024
         ),
-    )(*pieces, weight)
+    )(rows, weight)
 
 
 def body(layer_input, norm_gain, kv_cotangent, kv_weight, mlp_grads, output_cotangent, out_weight):
@@ -254,8 +248,10 @@
         return array[:, c * depth : (c + 1) * depth]
 
     leaving = [cut(norm_back, c) for c in range(CHUNKS)]
+    if by_permutes:
+        leaving[1:] = [after(part, arrived[0]) for part in leaving[1:]]
     arrivals = [from_behind(part, "section", -1) for part in leaving]
-    home = mix_features(after(norm_back, leaving[-1]))
+    home = mix_features(after(norm_back, leaving[0]))
     blocks_of = []
     for c in range(CHUNKS):
         part = cut(base, c)
@@ -271,10 +267,10 @@
         if c > 0:
             blocks[-1] = after(blocks[-1], attn_parts[-1][0])
         pieces = [half for block in blocks for half in (block, over_cores(block))]
+        if c == 0:
+            pieces[-1] = after(pieces[-1], home)
         terms = product(pieces, out_weight[0])
         first = lax.dynamic_index_in_dim(terms, (place - 1) % seq, 0, keepdims=False)
-        if c == 0:
-            first = after(first, home)
         attn_parts.append([first, terms])
     home = exchange(after(home, attn_parts[-1][0]), "tp")
     home = home.reshape(tokens, -1).astype(jnp.float32)

time: 215 us -> 215 us (level)
  starting transfers between devices: 68 us -> 84.3 us
  waiting for transfers between devices: 82.4 us -> 69.5 us
  local copies, waits for them, and re-layouts: 19.2 us -> 8.7 us
  other arithmetic: 25.1 us -> 30.3 us
  Pallas kernels: 12 us -> 14.4 us
    ppermute x6, starting transfers between devices: 3.43 us -> 17.3 us  [body(): total = lax.ppermute(mine, 'seq', [(q, (q + 1) % seq) for q in range(seq)])]
    ppermute x6, waiting for transfers between devices: 37.3 us -> 23.7 us  [body(): total = lax.ppermute(mine, 'seq', [(q, (q + 1) % seq) for q in range(seq)])]
    unnamed x32 -> x16, local copies, waits for them, and re-layouts: 14.1 us -> 2.62 us
    ppermute x6, starting transfers between devices: 4.47 us -> 9.51 us  [over_cores(): return lax.ppermute(block, 'tp', [(t, t ^ 1) for t in range(tp)])]
    ppermute x8, waiting for transfers between devices: 11.2 us -> 6.2 us  [spread(): moved = lax.ppermute(piece, ('seq', 'tp'), route)]
    ppermute x5, waiting for transfers between devices: 4.66 us -> 8.74 us  [over_rows(): lax.ppermute(block, 'tp', [(t, (t + turn * CORES) % tp) for t in range(tp)])]
    another operation x0 -> x2, other arithmetic: none -> 3.78 us  [product(): rows = jnp.stack(pieces, axis=0)]
    all_to_all x2, starting transfers between devices: 11.4 us -> 8.51 us  [exchange(): return lax.all_to_all(block, axis, 0, 0)]
  transfers between devices with their start and end apart: 38 -> 38, of which waited for: 16 -> 16; matrix products, arithmetic and copies ran while one was open for 15% -> 19% of each run, Pallas kernels for 6% -> 7%
where the time goes in v8:
time: 215 us; the launch traced here: 214 us
  starting transfers between devices  84.3 us (39%)
  waiting for transfers between devices  69.5 us (32%)
  other arithmetic  30.3 us (14%)
  Pallas kernels  14.4 us (7%)
  local copies, waits for them, and re-layouts  8.7 us (4%)
  matrix products  5.72 us (3%)
    ppermute x6, waiting for transfers between devices, body(): total = lax.ppermute(mine, 'seq', [(q, (q + 1) % seq) for q in range(seq)])  23.7 us
    ppermute x8, starting transfers between devices, spread(): moved = lax.ppermute(piece, ('seq', 'tp'), route)  18.9 us
    ppermute x6, starting transfers between devices, body(): total = lax.ppermute(mine, 'seq', [(q, (q + 1) % seq) for q in range(seq)])  17.3 us
    ppermute x6, waiting for transfers between devices, gather_seq(): arrived.append(lax.ppermute(block, 'seq', route))  16.1 us
    ppermute x6, starting transfers between devices, gather_seq(): arrived.append(lax.ppermute(block, 'seq', route))  15.1 us
    pallas_call x2, Pallas kernels, product(): pl.pallas_call(product_kernel, out_shape=jax.ShapeDtypeStruct((seq, n, de...  14.4 us
    ppermute x4, waiting for transfers between devices, from_behind(): return lax.ppermute(block, axis, route)  13.2 us
    convert_element_type x6, other arithmetic, body(): mine = mine.astype(jnp.bfloat16)  9.71 us
  transfers between devices with their start and end apart: 38, of which 16 were waited for; matrix products, arithmetic and copies ran while one was open for 19% of the time, Pallas kernels for 7%

profile of v8, /device:TPU:0, one launch (start us, length us, event | category | flops | bytes accessed | tf_op | source)
XLA Modules:
  0.0 214.3 jit_solution(11196144062717369698)
XLA Ops:
  3.4 3.0 %collective-permute-start.5 = (bf16[2,1,64,2048]{3,2,1,0:T(8,128)(2,1)S(1)}, bf16[2,1,64,2048]{3,2,1,0:T(8,128)(2,1)S(1)}, u32[]{:S(2)}, u32[]{:S(2)}) collective-permute-start(bf16[2,1,64,2048]{3,2,1,0:T(8,128)(2,1)S(1)} %dynamic-slice_bitcast_fusion.3), channel_id=1, source_target_pairs={{0,2},{1,3},{2,0},{3,1},{4,6},{5,7},{6,4},{7,5},{8,10},{9,11},{10,... | collective-permute-start | bytes 1572872 | tf_op jit(solution)/shard_map/ppermute | solution.py:34
  7.4 3.9 %collective-permute-start.2 = (bf16[2,64,1024]{2,1,0:T(8,128)(2,1)S(1)}, bf16[2,64,1024]{2,1,0:T(8,128)(2,1)S(1)}, u32[]{:S(2)}, u32[]{:S(2)}) collective-permute-start(bf16[2,64,1024]{2,1,0:T(8,128)(2,1)S(1)} %pad_maximum_fusion.3), channel_id=1, source_target_pairs={{0,8},{4,12},{8,0},{12,4},{1,9},{5,13},{9,1},{13,5},{2,10},{6,14},... | collective-permute-start | bytes 786440 | tf_op jit(solution)/shard_map/ppermute | solution.py:134
  13.4 11.3 %collective-permute-done.2 = bf16[2,64,1024]{2,1,0:T(8,128)(2,1)S(1)} collective-permute-done((bf16[2,64,1024]{2,1,0:T(8,128)(2,1)S(1)}, bf16[2,64,1024]{2,1,0:T(8,128)(2,1)S(1)}, u32[]{:S(2)}, u32[]{:S(2)}) %collective-permute-start.2) | collective-permute-done | bytes 262176 | tf_op jit(solution)/shard_map/ppermute | solution.py:134
  26.0 4.8 %collective-permute-done.3 = bf16[2,64,1024]{2,1,0:T(8,128)(2,1)S(1)} collective-permute-done((bf16[2,64,1024]{2,1,0:T(8,128)(2,1)S(1)}, bf16[2,64,1024]{2,1,0:T(8,128)(2,1)S(1)}, u32[]{:S(2)}, u32[]{:S(2)}) %collective-permute-start.3) | collective-permute-done | bytes 262176 | tf_op jit(solution)/shard_map/ppermute | solution.py:134
  38.5 5.5 %collective-permute-start.8 = (bf16[1,64,2048]{2,1,0:T(8,128)(2,1)S(1)}, bf16[1,64,2048]{2,1,0:T(8,128)(2,1)S(1)}, u32[]{:S(2)}, u32[]{:S(2)}) collective-permute-start(bf16[1,64,2048]{2,1,0:T(8,128)(2,1)S(1)} %get-tuple-element.46), channel_id=1, source_target_pairs={{0,8},{1,12},{2,10},{3,14},{4,9},{5,13},{6,11},{7,15},{8,0},{9,4},... | collective-permute-start | bytes 786440 | tf_op jit(solution)/shard_map/ppermute | solution.py:92
  46.4 6.2 %collective-permute-done.16 = bf16[256,2048]{1,0:T(8,128)(2,1)S(1)} collective-permute-done((bf16[256,2048]{1,0:T(8,128)(2,1)S(1)}, bf16[256,2048]{1,0:T(8,128)(2,1)S(1)}, u32[]{:S(2)}, u32[]{:S(2)}) %collective-permute-start.16) | collective-permute-done | bytes 1048608 | tf_op jit(solution)/shard_map/ppermute | solution.py:19
  62.4 6.3 %collective-permute-start.13 = (f32[2,4,64]{2,1,0:T(4,128)S(1)}, f32[2,4,64]{2,1,0:T(4,128)S(1)}, u32[]{:S(2)}, u32[]{:S(2)}) collective-permute-start(f32[2,4,64]{2,1,0:T(4,128)S(1)} %pad_maximum_fusion.4), channel_id=1, source_target_pairs={{0,8},{4,12},{8,0},{12,4},{1,9},{5,13},{9,1},{13,5},{2,10},{6,14},... | collective-permute-start | bytes 6152 | tf_op jit(solution)/shard_map/ppermute | solution.py:134
  72.7 5.4 %collective-permute-start.20 = (bf16[1,64,2048]{2,1,0:T(8,128)(2,1)}, bf16[1,64,2048]{2,1,0:T(8,128)(2,1)S(1)}, u32[]{:S(2)}, u32[]{:S(2)}) collective-permute-start(bf16[1,64,2048]{2,1,0:T(8,128)(2,1)} %get-tuple-element.42), channel_id=1, source_target_pairs={{0,8},{1,12},{2,10},{3,14},{4,9},{5,13},{6,11},{7,15},{8,0},{9,4},... | collective-permute-start | bytes 786440 | tf_op jit(solution)/shard_map/ppermute | solution.py:92
  78.1 3.3 %collective-permute-start.21 = (bf16[1,64,2048]{2,1,0:T(8,128)(2,1)}, bf16[1,64,2048]{2,1,0:T(8,128)(2,1)S(1)}, u32[]{:S(2)}, u32[]{:S(2)}) collective-permute-start(bf16[1,64,2048]{2,1,0:T(8,128)(2,1)} %get-tuple-element.41), channel_id=1, source_target_pairs={{0,9},{1,13},{2,11},{3,15},{4,8},{5,12},{6,10},{7,14},{8,1},{9,5},... | collective-permute-start | bytes 786440 | tf_op jit(solution)/shard_map/ppermute | solution.py:92
  88.3 4.2 %all-to-all-start = ((bf16[4,64,2048]{2,1,0:T(8,128)(2,1)}), bf16[4,64,2048]{2,1,0:T(8,128)(2,1)S(1)}, u32[]{:S(2)}, u32[]{:S(2)}) async-start(bf16[4,64,2048]{2,1,0:T(8,128)(2,1)} %fusion.10), calls=%async_computation | async-start | bytes 2097152 | tf_op jit(solution)/shard_map/all_to_all | solution.py:43
  92.6 3.8 %collective-permute-done.20 = bf16[1,64,2048]{2,1,0:T(8,128)(2,1)S(1)} collective-permute-done((bf16[1,64,2048]{2,1,0:T(8,128)(2,1)}, bf16[1,64,2048]{2,1,0:T(8,128)(2,1)S(1)}, u32[]{:S(2)}, u32[]{:S(2)}) %collective-permute-start.20) | collective-permute-done | bytes 262176 | tf_op jit(solution)/shard_map/ppermute | solution.py:92
  96.8 5.7 %collective-permute-done.15 = bf16[4,32,2048]{2,1,0:T(8,128)(2,1)} collective-permute-done((bf16[4,32,2048]{2,1,0:T(8,128)(2,1)}, bf16[4,32,2048]{2,1,0:T(8,128)(2,1)}, u32[]{:S(2)}, u32[]{:S(2)}) %collective-permute-start.15) | collective-permute-done | bytes 524320 | tf_op jit(solution)/shard_map/ppermute | solution.py:19
  107.1 7.2 %collective-permute-done.23 = bf16[4,32,2048]{2,1,0:T(8,128)(2,1)} collective-permute-done((bf16[4,32,2048]{2,1,0:T(8,128)(2,1)}, bf16[4,32,2048]{2,1,0:T(8,128)(2,1)}, u32[]{:S(2)}, u32[]{:S(2)}) %collective-permute-start.23) | collective-permute-done | bytes 524320 | tf_op jit(solution)/shard_map/ppermute | solution.py:34
  114.2 5.4 %collective-permute-start.24 = (bf16[4,32,2048]{2,1,0:T(8,128)(2,1)}, bf16[4,32,2048]{2,1,0:T(8,128)(2,1)}, u32[]{:S(2)}, u32[]{:S(2)}) collective-permute-start(bf16[4,32,2048]{2,1,0:T(8,128)(2,1)} %collective-permute-done.23), channel_id=1, source_target_pairs={{0,1},{1,0},{2,3},{3,2},{4,5},{5,4},{6,7},{7,6},{8,9},{9,8},{10,11... | collective-permute-start | bytes 1572872 | tf_op jit(solution)/shard_map/ppermute | solution.py:39
  127.5 7.2 %shard_map.86 = bf16[4,4,32,2048]{3,2,1,0:T(8,128)(2,1)S(1)} custom-call(bf16[4,4,32,2048]{3,2,1,0:T(8,128)(2,1)S(1)} %pad_maximum_fusion.rows, bf16[2048,2048]{1,0:T(8,128)(2,1)} %bitcast.183), custom_call_target="tpu_custom_call" | custom-call | flops 4294967296 | bytes 10485760 | tf_op jit(solution)/shard_map/pallas_call | solution.py:171
  140.1 7.2 %shard_map.87 = bf16[4,4,32,2048]{3,2,1,0:T(8,128)(2,1)S(1)} custom-call(bf16[4,4,32,2048]{3,2,1,0:T(8,128)(2,1)S(1)} %pad_maximum_fusion.1.rows, bf16[2048,2048]{1,0:T(8,128)(2,1)} %bitcast.184), custom_call_target="tpu_custom_call" | custom-call | flops 4294967296 | bytes 10485760 | tf_op jit(solution)/shard_map/pallas_call | solution.py:171
  149.5 5.8 %collective-permute-start.32 = (bf16[4,32,2048]{2,1,0:T(8,128)(2,1)}, bf16[4,32,2048]{2,1,0:T(8,128)(2,1)}, u32[]{:S(2)}, u32[]{:S(2)}) collective-permute-start(bf16[4,32,2048]{2,1,0:T(8,128)(2,1)} %dynamic-slice_bitcast_fusion), channel_id=1, source_target_pairs={{0,4},{4,8},{8,12},{12,0},{1,5},{5,9},{9,13},{13,1},{2,6},{6,10},{... | collective-permute-start | bytes 1572872 | tf_op jit(solution)/shard_map/ppermute | solution.py:283
  155.3 4.3 %all-to-all-start.1 = ((bf16[4,64,2048]{2,1,0:T(8,128)(2,1)}), bf16[4,64,2048]{2,1,0:T(8,128)(2,1)}, u32[]{:S(2)}, u32[]{:S(2)}) async-start(bf16[4,64,2048]{2,1,0:T(8,128)(2,1)} %copy-done.4), calls=%async_computation.1 | async-start | bytes 2097152 | tf_op jit(solution)/shard_map/all_to_all | solution.py:43
  163.7 4.2 %collective-permute-done.32 = bf16[4,32,2048]{2,1,0:T(8,128)(2,1)} collective-permute-done((bf16[4,32,2048]{2,1,0:T(8,128)(2,1)}, bf16[4,32,2048]{2,1,0:T(8,128)(2,1)}, u32[]{:S(2)}, u32[]{:S(2)}) %collective-permute-start.32) | collective-permute-done | bytes 524320 | tf_op jit(solution)/shard_map/ppermute | solution.py:283
  174.1 3.1 %fusion.3 = bf16[256,2048]{1,0:T(8,128)(2,1)} fusion(bf16[256,2048]{1,0:T(8,128)(2,1)} %param.12, bf16[4,64,2048]{2,1,0:T(8,128)(2,1)} %all-to-all-done.1, bf16[1,256,2048]{2,1,0:T(8,128)(2,1)S(1)} %copy-done.1), kind=kLoop, calls=%fused_computation.12 | loop fusion | flops 3145728 | bytes 4194304 | tf_op jit(solution)/shard_map/convert_element_type | solution.py:277
  183.6 6.8 %collective-permute-done.33 = bf16[4,32,2048]{2,1,0:T(8,128)(2,1)} collective-permute-done((bf16[4,32,2048]{2,1,0:T(8,128)(2,1)}, bf16[4,32,2048]{2,1,0:T(8,128)(2,1)}, u32[]{:S(2)}, u32[]{:S(2)}) %collective-permute-start.33) | collective-permute-done | bytes 524320 | tf_op jit(solution)/shard_map/ppermute | solution.py:283
  194.2 7.4 %collective-permute-done.31 = bf16[4,32,2048]{2,1,0:T(8,128)(2,1)} collective-permute-done((bf16[4,32,2048]{2,1,0:T(8,128)(2,1)}, bf16[4,32,2048]{2,1,0:T(8,128)(2,1)}, u32[]{:S(2)}, u32[]{:S(2)}) %collective-permute-start.31) | collective-permute-done | bytes 524320 | tf_op jit(solution)/shard_map/ppermute | solution.py:283
  204.1 3.3 %fusion.12 = bf16[256,2048]{1,0:T(8,128)(2,1)} fusion(bf16[256,2048]{1,0:T(8,128)(2,1)} %collective-permute-done.35, bf16[4,64,2048]{2,1,0:T(8,128)(2,1)} %all-to-all-done.1, pred[]{:T(512)S(6)} %eq.79, bf16[1,256,2048]{2,1,0:T(8,128)(2,1)S(1)} %copy-done.1, bf16[256,2048]{1,0:T(8,128)(2,1)S(1)} %copy-done.3), kind=kLoop, calls=%fused_computation.32 | loop fusion | flops 5767168 | bytes 5242881 | tf_op jit(solution)/shard_map/jit(_where)/select_n | solution.py:280
  207.4 4.7 %collective-permute-done.34 = bf16[4,32,2048]{2,1,0:T(8,128)(2,1)S(1)} collective-permute-done((bf16[4,32,2048]{2,1,0:T(8,128)(2,1)S(1)}, bf16[4,32,2048]{2,1,0:T(8,128)(2,1)S(1)}, u32[]{:S(2)}, u32[]{:S(2)}) %collective-permute-start.34) | collective-permute-done | bytes 524320 | tf_op jit(solution)/shard_map/ppermute | solution.py:283
  (112 shorter events, 83.1 us)
Async XLA Ops:
  0.7 30.7 %collective-permute-start.4 = (bf16[512,2048]{1,0:T(8,128)(2,1)}, bf16[512,2048]{1,0:T(8,128)(2,1)}, u32[]{:S(2)}, u32[]{:S(2)}) collective-permute-start(bf16[512,2048]{1,0:T(8,128)(2,1)} %bitcast.185), channel_id=1, source_target_pairs={{0,1},{1,0},{2,3},{3,2},{4,5},{5,4},{6,7},{7,6},{8,9},{9,8},{10,11... | collective-permute-start | bytes 6291464 | tf_op jit(solution)/shard_map/ppermute | solution.py:39
  3.4 34.9 %collective-permute-start.5 = (bf16[2,1,64,2048]{3,2,1,0:T(8,128)(2,1)S(1)}, bf16[2,1,64,2048]{3,2,1,0:T(8,128)(2,1)S(1)}, u32[]{:S(2)}, u32[]{:S(2)}) collective-permute-start(bf16[2,1,64,2048]{3,2,1,0:T(8,128)(2,1)S(1)} %dynamic-slice_bitcast_fusion.3), channel_id=1, source_target_pairs={{0,2},{1,3},{2,0},{3,1},{4,6},{5,7},{6,4},{7,5},{8,10},{9,11},{10,... | collective-permute-start | bytes 1572872 | tf_op jit(solution)/shard_map/ppermute | solution.py:34
  7.4 17.3 %collective-permute-start.2 = (bf16[2,64,1024]{2,1,0:T(8,128)(2,1)S(1)}, bf16[2,64,1024]{2,1,0:T(8,128)(2,1)S(1)}, u32[]{:S(2)}, u32[]{:S(2)}) collective-permute-start(bf16[2,64,1024]{2,1,0:T(8,128)(2,1)S(1)} %pad_maximum_fusion.3), channel_id=1, source_target_pairs={{0,8},{4,12},{8,0},{12,4},{1,9},{5,13},{9,1},{13,5},{2,10},{6,14},... | collective-permute-start | bytes 786440 | tf_op jit(solution)/shard_map/ppermute | solution.py:134
  11.3 19.4 %collective-permute-start.3 = (bf16[2,64,1024]{2,1,0:T(8,128)(2,1)S(1)}, bf16[2,64,1024]{2,1,0:T(8,128)(2,1)S(1)}, u32[]{:S(2)}, u32[]{:S(2)}) collective-permute-start(bf16[2,64,1024]{2,1,0:T(8,128)(2,1)S(1)} %pad_maximum_fusion.3), channel_id=1, source_target_pairs={{0,12},{4,0},{8,4},{12,8},{1,13},{5,1},{9,5},{13,9},{2,14},{6,2},{... | collective-permute-start | bytes 786440 | tf_op jit(solution)/shard_map/ppermute | solution.py:134
  12.7 18.0 %collective-permute-start.1 = (bf16[2,64,1024]{2,1,0:T(8,128)(2,1)S(1)}, bf16[2,64,1024]{2,1,0:T(8,128)(2,1)S(1)}, u32[]{:S(2)}, u32[]{:S(2)}) collective-permute-start(bf16[2,64,1024]{2,1,0:T(8,128)(2,1)S(1)} %pad_maximum_fusion.3), channel_id=1, source_target_pairs={{0,4},{4,8},{8,12},{12,0},{1,5},{5,9},{9,13},{13,1},{2,6},{6,10},{... | collective-permute-start | bytes 786440 | tf_op jit(solution)/shard_map/ppermute | solution.py:134
  24.7 27.9 %collective-permute-start.16 = (bf16[256,2048]{1,0:T(8,128)(2,1)S(1)}, bf16[256,2048]{1,0:T(8,128)(2,1)S(1)}, u32[]{:S(2)}, u32[]{:S(2)}) collective-permute-start(bf16[256,2048]{1,0:T(8,128)(2,1)S(1)} %bitcast.169), channel_id=1, source_target_pairs={{16,0},{17,1},{18,2},{19,3},{20,4},{21,5},{22,6},{23,7},{24,8},{25... | collective-permute-start | bytes 3145736 | tf_op jit(solution)/shard_map/ppermute | solution.py:19
  35.5 26.2 %collective-permute-start.11 = (bf16[4,64,2048]{2,1,0:T(8,128)(2,1)S(1)}, bf16[4,64,2048]{2,1,0:T(8,128)(2,1)S(1)}, u32[]{:S(2)}, u32[]{:S(2)}) collective-permute-start(bf16[4,64,2048]{2,1,0:T(8,128)(2,1)S(1)} %fusion.2), channel_id=1, source_target_pairs={{0,2},{1,3},{2,0},{3,1},{4,6},{5,7},{6,4},{7,5},{8,10},{9,11},{10,... | collective-permute-start | bytes 3145736 | tf_op jit(solution)/shard_map/ppermute | solution.py:34
  38.5 20.6 %collective-permute-start.8 = (bf16[1,64,2048]{2,1,0:T(8,128)(2,1)S(1)}, bf16[1,64,2048]{2,1,0:T(8,128)(2,1)S(1)}, u32[]{:S(2)}, u32[]{:S(2)}) collective-permute-start(bf16[1,64,2048]{2,1,0:T(8,128)(2,1)S(1)} %get-tuple-element.46), channel_id=1, source_target_pairs={{0,8},{1,12},{2,10},{3,14},{4,9},{5,13},{6,11},{7,15},{8,0},{9,4},... | collective-permute-start | bytes 786440 | tf_op jit(solution)/shard_map/ppermute | solution.py:92
  44.0 15.9 %collective-permute-start.9 = (bf16[1,64,2048]{2,1,0:T(8,128)(2,1)S(1)}, bf16[1,64,2048]{2,1,0:T(8,128)(2,1)S(1)}, u32[]{:S(2)}, u32[]{:S(2)}) collective-permute-start(bf16[1,64,2048]{2,1,0:T(8,128)(2,1)S(1)} %get-tuple-element.45), channel_id=1, source_target_pairs={{0,9},{1,13},{2,11},{3,15},{4,8},{5,12},{6,10},{7,14},{8,1},{9,5},... | collective-permute-start | bytes 786440 | tf_op jit(solution)/shard_map/ppermute | solution.py:92
  62.4 19.0 %collective-permute-start.13 = (f32[2,4,64]{2,1,0:T(4,128)S(1)}, f32[2,4,64]{2,1,0:T(4,128)S(1)}, u32[]{:S(2)}, u32[]{:S(2)}) collective-permute-start(f32[2,4,64]{2,1,0:T(4,128)S(1)} %pad_maximum_fusion.4), channel_id=1, source_target_pairs={{0,8},{4,12},{8,0},{12,4},{1,9},{5,13},{9,1},{13,5},{2,10},{6,14},... | collective-permute-start | bytes 6152 | tf_op jit(solution)/shard_map/ppermute | solution.py:134
  72.7 23.8 %collective-permute-start.20 = (bf16[1,64,2048]{2,1,0:T(8,128)(2,1)}, bf16[1,64,2048]{2,1,0:T(8,128)(2,1)S(1)}, u32[]{:S(2)}, u32[]{:S(2)}) collective-permute-start(bf16[1,64,2048]{2,1,0:T(8,128)(2,1)} %get-tuple-element.42), channel_id=1, source_target_pairs={{0,8},{1,12},{2,10},{3,14},{4,9},{5,13},{6,11},{7,15},{8,0},{9,4},... | collective-permute-start | bytes 786440 | tf_op jit(solution)/shard_map/ppermute | solution.py:92
  78.1 18.4 %collective-permute-start.21 = (bf16[1,64,2048]{2,1,0:T(8,128)(2,1)}, bf16[1,64,2048]{2,1,0:T(8,128)(2,1)S(1)}, u32[]{:S(2)}, u32[]{:S(2)}) collective-permute-start(bf16[1,64,2048]{2,1,0:T(8,128)(2,1)} %get-tuple-element.41), channel_id=1, source_target_pairs={{0,9},{1,13},{2,11},{3,15},{4,8},{5,12},{6,10},{7,14},{8,1},{9,5},... | collective-permute-start | bytes 786440 | tf_op jit(solution)/shard_map/ppermute | solution.py:92
  81.4 15.0 %collective-permute-start.19 = (bf16[1,64,2048]{2,1,0:T(8,128)(2,1)S(1)}, bf16[1,64,2048]{2,1,0:T(8,128)(2,1)S(1)}, u32[]{:S(2)}, u32[]{:S(2)}) collective-permute-start(bf16[1,64,2048]{2,1,0:T(8,128)(2,1)S(1)} %get-tuple-element.43), channel_id=1, source_target_pairs={{0,1},{1,5},{2,3},{3,7},{4,0},{5,4},{6,2},{7,6},{8,9},{9,13},{10,1... | collective-permute-start | bytes 786440 | tf_op jit(solution)/shard_map/ppermute | solution.py:92
  87.0 15.4 %collective-permute-start.15 = (bf16[4,32,2048]{2,1,0:T(8,128)(2,1)}, bf16[4,32,2048]{2,1,0:T(8,128)(2,1)}, u32[]{:S(2)}, u32[]{:S(2)}) collective-permute-start(bf16[4,32,2048]{2,1,0:T(8,128)(2,1)} %get-tuple-element.53), channel_id=1, source_target_pairs={{16,0},{17,1},{18,2},{19,3},{20,4},{21,5},{22,6},{23,7},{24,8},{25... | collective-permute-start | bytes 1572872 | tf_op jit(solution)/shard_map/ppermute | solution.py:19
  88.3 36.9 %all-to-all-start = ((bf16[4,64,2048]{2,1,0:T(8,128)(2,1)}), bf16[4,64,2048]{2,1,0:T(8,128)(2,1)S(1)}, u32[]{:S(2)}, u32[]{:S(2)}) async-start(bf16[4,64,2048]{2,1,0:T(8,128)(2,1)} %fusion.10), calls=%async_computation | async-start | bytes 2097152 | tf_op jit(solution)/shard_map/all_to_all | solution.py:43
  122.9 15.5 %collective-permute-start.28 = (bf16[4,32,2048]{2,1,0:T(8,128)(2,1)}, bf16[4,32,2048]{2,1,0:T(8,128)(2,1)}, u32[]{:S(2)}, u32[]{:S(2)}) collective-permute-start(bf16[4,32,2048]{2,1,0:T(8,128)(2,1)} %fusion.20), channel_id=1, source_target_pairs={{0,1},{1,0},{2,3},{3,2},{4,5},{5,4},{6,7},{7,6},{8,9},{9,8},{10,11... | collective-permute-start | bytes 1572872 | tf_op jit(solution)/shard_map/ppermute | solution.py:39
  136.6 23.0 %collective-permute-start.25 = (bf16[4,32,2048]{2,1,0:T(8,128)(2,1)}, bf16[4,32,2048]{2,1,0:T(8,128)(2,1)}, u32[]{:S(2)}, u32[]{:S(2)}) collective-permute-start(bf16[4,32,2048]{2,1,0:T(8,128)(2,1)} %dynamic-slice_bitcast_fusion.1), channel_id=1, source_target_pairs={{0,4},{4,8},{8,12},{12,0},{1,5},{5,9},{9,13},{13,1},{2,6},{6,10},{... | collective-permute-start | bytes 1572872 | tf_op jit(solution)/shard_map/ppermute | solution.py:283
  149.5 18.4 %collective-permute-start.32 = (bf16[4,32,2048]{2,1,0:T(8,128)(2,1)}, bf16[4,32,2048]{2,1,0:T(8,128)(2,1)}, u32[]{:S(2)}, u32[]{:S(2)}) collective-permute-start(bf16[4,32,2048]{2,1,0:T(8,128)(2,1)} %dynamic-slice_bitcast_fusion), channel_id=1, source_target_pairs={{0,4},{4,8},{8,12},{12,0},{1,5},{5,9},{9,13},{13,1},{2,6},{6,10},{... | collective-permute-start | bytes 1572872 | tf_op jit(solution)/shard_map/ppermute | solution.py:283
  155.3 18.8 %all-to-all-start.1 = ((bf16[4,64,2048]{2,1,0:T(8,128)(2,1)}), bf16[4,64,2048]{2,1,0:T(8,128)(2,1)}, u32[]{:S(2)}, u32[]{:S(2)}) async-start(bf16[4,64,2048]{2,1,0:T(8,128)(2,1)} %copy-done.4), calls=%async_computation.1 | async-start | bytes 2097152 | tf_op jit(solution)/shard_map/all_to_all | solution.py:43
  161.5 17.6 %collective-permute-start.26 = (bf16[4,32,2048]{2,1,0:T(8,128)(2,1)}, bf16[4,32,2048]{2,1,0:T(8,128)(2,1)}, u32[]{:S(2)}, u32[]{:S(2)}) collective-permute-start(bf16[4,32,2048]{2,1,0:T(8,128)(2,1)} %fusion.16), channel_id=1, source_target_pairs={{0,4},{4,8},{8,12},{12,0},{1,5},{5,9},{9,13},{13,1},{2,6},{6,10},{... | collective-permute-start | bytes 1572872 | tf_op jit(solution)/shard_map/ppermute | solution.py:283
  170.0 20.3 %collective-permute-start.33 = (bf16[4,32,2048]{2,1,0:T(8,128)(2,1)}, bf16[4,32,2048]{2,1,0:T(8,128)(2,1)}, u32[]{:S(2)}, u32[]{:S(2)}) collective-permute-start(bf16[4,32,2048]{2,1,0:T(8,128)(2,1)} %fusion.13), channel_id=1, source_target_pairs={{0,4},{4,8},{8,12},{12,0},{1,5},{5,9},{9,13},{13,1},{2,6},{6,10},{... | collective-permute-start | bytes 1572872 | tf_op jit(solution)/shard_map/ppermute | solution.py:283
  177.2 26.9 %collective-permute-start.35 = (bf16[256,2048]{1,0:T(8,128)(2,1)}, bf16[256,2048]{1,0:T(8,128)(2,1)}, u32[]{:S(2)}, u32[]{:S(2)}) collective-permute-start(bf16[256,2048]{1,0:T(8,128)(2,1)} %fusion.3), channel_id=1, source_target_pairs={{16,0},{17,1},{18,2},{19,3},{20,4},{21,5},{22,6},{23,7},{24,8},{25... | collective-permute-start | bytes 3145736 | tf_op jit(solution)/shard_map/ppermute | solution.py:19
  181.1 20.5 %collective-permute-start.31 = (bf16[4,32,2048]{2,1,0:T(8,128)(2,1)}, bf16[4,32,2048]{2,1,0:T(8,128)(2,1)}, u32[]{:S(2)}, u32[]{:S(2)}) collective-permute-start(bf16[4,32,2048]{2,1,0:T(8,128)(2,1)} %fusion.17), channel_id=1, source_target_pairs={{0,4},{4,8},{8,12},{12,0},{1,5},{5,9},{9,13},{13,1},{2,6},{6,10},{... | collective-permute-start | bytes 1572872 | tf_op jit(solution)/shard_map/ppermute | solution.py:283
  191.7 20.3 %collective-permute-start.34 = (bf16[4,32,2048]{2,1,0:T(8,128)(2,1)S(1)}, bf16[4,32,2048]{2,1,0:T(8,128)(2,1)S(1)}, u32[]{:S(2)}, u32[]{:S(2)}) collective-permute-start(bf16[4,32,2048]{2,1,0:T(8,128)(2,1)S(1)} %fusion.14), channel_id=1, source_target_pairs={{0,4},{4,8},{8,12},{12,0},{1,5},{5,9},{9,13},{13,1},{2,6},{6,10},{... | collective-permute-start | bytes 1572872 | tf_op jit(solution)/shard_map/ppermute | solution.py:283
  (22 other events, 228.9 us)

commit v9 on v8

--- a/solution.py
+++ b/solution.py
@@ -267,20 +267,16 @@
         if c > 0:
             blocks[-1] = after(blocks[-1], attn_parts[-1][0])
         pieces = [half for block in blocks for half in (block, over_cores(block))]
-        if c == 0:
-            pieces[-1] = after(pieces[-1], home)
         terms = product(pieces, out_weight[0])
         first = lax.dynamic_index_in_dim(terms, (place - 1) % seq, 0, keepdims=False)
+        if c == 0:
+            first = after(first, home)
         attn_parts.append([first, terms])
-    home = exchange(after(home, attn_parts[-1][0]), "tp")
-    home = home.reshape(tokens, -1).astype(jnp.float32)
-    own = (grad_one + home).astype(jnp.bfloat16)
-    arrived = from_behind(own, "section", -1)
-    input_zero = (arrived.astype(jnp.float32) + branch + home).astype(jnp.bfloat16)
-    input_part = jnp.where(upstream, input_zero, own)
     for c, (mine, terms) in enumerate(attn_parts):
         for step in range(2, seq + 1):
             total = lax.ppermute(mine, "seq", [(q, (q + 1) % seq) for q in range(seq)])
+            if c == 0 and step == 2:
+                total = after(total, attn_parts[-1][0])
             if c == 0 and step == 3:
                 total = after(total, own)
             if c == CHUNKS - 1 and step == seq:
@@ -288,6 +284,13 @@
             mine = lax.dynamic_index_in_dim(terms, (place - step) % seq, 0, keepdims=False)
             mine = mine.astype(jnp.float32) + total.astype(jnp.float32)
             mine = mine.astype(jnp.bfloat16)
+            if c == 0 and step == 2:
+                home = exchange(after(home, mine), "tp")
+                home = home.reshape(tokens, -1).astype(jnp.float32)
+                own = (grad_one + home).astype(jnp.bfloat16)
+                arrived = from_behind(own, "section", -1)
+                input_zero = (arrived.astype(jnp.float32) + branch + home).astype(jnp.bfloat16)
+                input_part = jnp.where(upstream, input_zero, own)
         attn_parts[c] = mine
     attn_part = jnp.concatenate(attn_parts, axis=1)
     order = []

time: 215 us -> 211 us (0.981)
  waiting for transfers between devices: 69.5 us -> 114 us
  starting transfers between devices: 84.3 us -> 43.8 us
  other arithmetic: 30.3 us -> 25.1 us
  matrix products: 5.72 us -> 2.52 us
    ppermute x8, waiting for transfers between devices: 6.2 us -> 33 us  [spread(): moved = lax.ppermute(piece, ('seq', 'tp'), route)]
    ppermute x6, starting transfers between devices: 17.3 us -> 0.13 us  [body(): total = lax.ppermute(mine, 'seq', [(q, (q + 1) % seq) for q in range(seq)])]
    ppermute x6, waiting for transfers between devices: 23.7 us -> 36.9 us  [body(): total = lax.ppermute(mine, 'seq', [(q, (q + 1) % seq) for q in range(seq)])]
    ppermute x8, starting transfers between devices: 18.9 us -> 9.35 us  [spread(): moved = lax.ppermute(piece, ('seq', 'tp'), route)]
    ppermute x4, waiting for transfers between devices: 13.2 us -> 4.33 us  [from_behind(): return lax.ppermute(block, axis, route)]
    ppermute x6, starting transfers between devices: 15.1 us -> 7.31 us  [gather_seq(): arrived.append(lax.ppermute(block, 'seq', route))]
    all_to_all x2, waiting for transfers between devices: 1.6 us -> 8.54 us  [exchange(): return lax.all_to_all(block, axis, 0, 0)]
    ppermute x6, starting transfers between devices: 9.51 us -> 4.75 us  [over_cores(): return lax.ppermute(block, 'tp', [(t, t ^ 1) for t in range(tp)])]
  transfers between devices with their start and end apart: 38 -> 38, of which waited for: 16 -> 19; matrix products, arithmetic and copies ran while one was open for 19% -> 15% of each run, Pallas kernels for 7% -> 7%
where the time goes in v9:
time: 211 us; the launch traced here: 210 us
  waiting for transfers between devices  114 us (54%)
  starting transfers between devices  43.8 us (21%)
  other arithmetic  25.1 us (12%)
  Pallas kernels  14.4 us (7%)
  local copies, waits for them, and re-layouts  8.39 us (4%)
  matrix products  2.52 us (1%)
    ppermute x6, waiting for transfers between devices, body(): total = lax.ppermute(mine, 'seq', [(q, (q + 1) % seq) for q in range(seq)])  36.9 us
    ppermute x8, waiting for transfers between devices, spread(): moved = lax.ppermute(piece, ('seq', 'tp'), route)  33 us
    ppermute x6, waiting for transfers between devices, gather_seq(): arrived.append(lax.ppermute(block, 'seq', route))  18.1 us
    pallas_call x2, Pallas kernels, product(): pl.pallas_call(product_kernel, out_shape=jax.ShapeDtypeStruct((seq, n, de...  14.4 us
    ppermute x5, waiting for transfers between devices, over_rows(): lax.ppermute(block, 'tp', [(t, (t + turn * CORES) % tp) for t in range(tp)])  11.1 us
    ppermute x8, starting transfers between devices, spread(): moved = lax.ppermute(piece, ('seq', 'tp'), route)  9.35 us
    convert_element_type x6, other arithmetic, body(): mine = mine.astype(jnp.bfloat16)  8.65 us
    all_to_all x2, waiting for transfers between devices, exchange(): return lax.all_to_all(block, axis, 0, 0)  8.54 us
  transfers between devices with their start and end apart: 38, of which 19 were waited for; matrix products, arithmetic and copies ran while one was open for 15% of the time, Pallas kernels for 7%

profile of v9, /device:TPU:0, one launch (start us, length us, event | category | flops | bytes accessed | tf_op | source)
XLA Modules:
  0.0 209.6 jit_solution(12841408091392859103)
XLA Ops:
  2.9 4.2 %collective-permute-start = (bf16[2,64,512]{2,1,0:T(8,128)(2,1)S(1)}, bf16[2,64,512]{2,1,0:T(8,128)(2,1)S(1)}, u32[]{:S(2)}, u32[]{:S(2)}) collective-permute-start(bf16[2,64,512]{2,1,0:T(8,128)(2,1)S(1)} %get-tuple-element.66), channel_id=1, source_target_pairs={{0,1},{1,0},{2,3},{3,2},{4,5},{5,4},{6,7},{7,6},{8,9},{9,8},{10,11... | collective-permute-start | bytes 393224 | tf_op jit(solution)/shard_map/ppermute | solution.py:39
  8.1 3.5 %collective-permute-start.3 = (bf16[2,64,1024]{2,1,0:T(8,128)(2,1)S(1)}, bf16[2,64,1024]{2,1,0:T(8,128)(2,1)S(1)}, u32[]{:S(2)}, u32[]{:S(2)}) collective-permute-start(bf16[2,64,1024]{2,1,0:T(8,128)(2,1)S(1)} %pad_maximum_fusion.3), channel_id=1, source_target_pairs={{0,12},{4,0},{8,4},{12,8},{1,13},{5,1},{9,5},{13,9},{2,14},{6,2},{... | collective-permute-start | bytes 786440 | tf_op jit(solution)/shard_map/ppermute | solution.py:134
  14.1 4.3 %collective-permute-done.3 = bf16[2,64,1024]{2,1,0:T(8,128)(2,1)S(1)} collective-permute-done((bf16[2,64,1024]{2,1,0:T(8,128)(2,1)S(1)}, bf16[2,64,1024]{2,1,0:T(8,128)(2,1)S(1)}, u32[]{:S(2)}, u32[]{:S(2)}) %collective-permute-start.3) | collective-permute-done | bytes 262176 | tf_op jit(solution)/shard_map/ppermute | solution.py:134
  20.5 13.8 %collective-permute-done.2 = bf16[2,64,1024]{2,1,0:T(8,128)(2,1)S(1)} collective-permute-done((bf16[2,64,1024]{2,1,0:T(8,128)(2,1)S(1)}, bf16[2,64,1024]{2,1,0:T(8,128)(2,1)S(1)}, u32[]{:S(2)}, u32[]{:S(2)}) %collective-permute-start.2) | collective-permute-done | bytes 262176 | tf_op jit(solution)/shard_map/ppermute | solution.py:134
  37.3 2.8 %collective-permute-start.11 = (bf16[4,64,2048]{2,1,0:T(8,128)(2,1)S(1)}, bf16[4,64,2048]{2,1,0:T(8,128)(2,1)S(1)}, u32[]{:S(2)}, u32[]{:S(2)}) collective-permute-start(bf16[4,64,2048]{2,1,0:T(8,128)(2,1)S(1)} %fusion.2), channel_id=1, source_target_pairs={{0,2},{1,3},{2,0},{3,1},{4,6},{5,7},{6,4},{7,5},{8,10},{9,11},{10,... | collective-permute-start | bytes 3145736 | tf_op jit(solution)/shard_map/ppermute | solution.py:34
  46.9 5.1 %collective-permute-done.9 = bf16[1,64,2048]{2,1,0:T(8,128)(2,1)S(1)} collective-permute-done((bf16[1,64,2048]{2,1,0:T(8,128)(2,1)S(1)}, bf16[1,64,2048]{2,1,0:T(8,128)(2,1)S(1)}, u32[]{:S(2)}, u32[]{:S(2)}) %collective-permute-start.9) | collective-permute-done | bytes 262176 | tf_op jit(solution)/shard_map/ppermute | solution.py:92
  52.6 12.9 %collective-permute-done.8 = bf16[1,64,2048]{2,1,0:T(8,128)(2,1)S(1)} collective-permute-done((bf16[1,64,2048]{2,1,0:T(8,128)(2,1)S(1)}, bf16[1,64,2048]{2,1,0:T(8,128)(2,1)S(1)}, u32[]{:S(2)}, u32[]{:S(2)}) %collective-permute-start.8) | collective-permute-done | bytes 262176 | tf_op jit(solution)/shard_map/ppermute | solution.py:92
  69.2 4.4 %collective-permute-done.17 = bf16[2,1,64,2048]{3,2,1,0:T(8,128)(2,1)S(1)} collective-permute-done((bf16[2,1,64,2048]{3,2,1,0:T(8,128)(2,1)S(1)}, bf16[2,1,64,2048]{3,2,1,0:T(8,128)(2,1)S(1)}, u32[]{:S(2)}, u32[]{:S(2)}) %collective-permute-start.17) | collective-permute-done | bytes 524320 | tf_op jit(solution)/shard_map/ppermute | solution.py:34
  85.0 13.6 %collective-permute-done.20 = bf16[1,64,2048]{2,1,0:T(8,128)(2,1)S(1)} collective-permute-done((bf16[1,64,2048]{2,1,0:T(8,128)(2,1)S(1)}, bf16[1,64,2048]{2,1,0:T(8,128)(2,1)S(1)}, u32[]{:S(2)}, u32[]{:S(2)}) %collective-permute-start.20) | collective-permute-done | bytes 262176 | tf_op jit(solution)/shard_map/ppermute | solution.py:92
  102.5 4.3 %all-to-all-start = ((bf16[4,64,2048]{2,1,0:T(8,128)(2,1)}), bf16[4,64,2048]{2,1,0:T(8,128)(2,1)}, u32[]{:S(2)}, u32[]{:S(2)}) async-start(bf16[4,64,2048]{2,1,0:T(8,128)(2,1)} %fusion.10), calls=%async_computation | async-start | bytes 2097152 | tf_op jit(solution)/shard_map/all_to_all | solution.py:43
  106.9 6.7 %collective-permute-done.23 = bf16[4,32,2048]{2,1,0:T(8,128)(2,1)} collective-permute-done((bf16[4,32,2048]{2,1,0:T(8,128)(2,1)S(1)}, bf16[4,32,2048]{2,1,0:T(8,128)(2,1)}, u32[]{:S(2)}, u32[]{:S(2)}) %collective-permute-start.23) | collective-permute-done | bytes 524320 | tf_op jit(solution)/shard_map/ppermute | solution.py:34
  113.6 3.4 %collective-permute-done.26 = bf16[4,32,2048]{2,1,0:T(8,128)(2,1)S(1)} collective-permute-done((bf16[4,32,2048]{2,1,0:T(8,128)(2,1)}, bf16[4,32,2048]{2,1,0:T(8,128)(2,1)S(1)}, u32[]{:S(2)}, u32[]{:S(2)}) %collective-permute-start.26) | collective-permute-done | bytes 524320 | tf_op jit(solution)/shard_map/ppermute | solution.py:19
  119.9 7.2 %shard_map.86 = bf16[4,4,32,2048]{3,2,1,0:T(8,128)(2,1)S(1)} custom-call(bf16[4,4,32,2048]{3,2,1,0:T(8,128)(2,1)S(1)} %pad_maximum_fusion.rows, bf16[2048,2048]{1,0:T(8,128)(2,1)} %bitcast.183), custom_call_target="tpu_custom_call" | custom-call | flops 4294967296 | bytes 10485760 | tf_op jit(solution)/shard_map/pallas_call | solution.py:171
  128.0 4.9 %all-to-all-done = bf16[4,64,2048]{2,1,0:T(8,128)(2,1)} async-done(((bf16[4,64,2048]{2,1,0:T(8,128)(2,1)}), bf16[4,64,2048]{2,1,0:T(8,128)(2,1)}, u32[]{:S(2)}, u32[]{:S(2)}) %all-to-all-start) | async-done | bytes 1048608 | tf_op jit(solution)/shard_map/all_to_all | solution.py:43
  136.9 7.2 %shard_map.87 = bf16[4,4,32,2048]{3,2,1,0:T(8,128)(2,1)S(1)} custom-call(bf16[4,4,32,2048]{3,2,1,0:T(8,128)(2,1)S(1)} %pad_maximum_fusion.1.rows, bf16[2048,2048]{1,0:T(8,128)(2,1)} %bitcast.184), custom_call_target="tpu_custom_call" | custom-call | flops 4294967296 | bytes 10485760 | tf_op jit(solution)/shard_map/pallas_call | solution.py:171
  146.3 2.9 %collective-permute-done.25 = bf16[4,32,2048]{2,1,0:T(8,128)(2,1)S(1)} collective-permute-done((bf16[4,32,2048]{2,1,0:T(8,128)(2,1)}, bf16[4,32,2048]{2,1,0:T(8,128)(2,1)S(1)}, u32[]{:S(2)}, u32[]{:S(2)}) %collective-permute-start.25) | collective-permute-done | bytes 524320 | tf_op jit(solution)/shard_map/ppermute | solution.py:277
  150.2 4.2 %all-to-all-start.1 = ((bf16[4,64,2048]{2,1,0:T(8,128)(2,1)}), bf16[4,64,2048]{2,1,0:T(8,128)(2,1)}, u32[]{:S(2)}, u32[]{:S(2)}) async-start(bf16[4,64,2048]{2,1,0:T(8,128)(2,1)} %all-to-all-done), calls=%async_computation.1 | async-start | bytes 2097152 | tf_op jit(solution)/shard_map/all_to_all | solution.py:43
  154.5 8.7 %collective-permute-done.32 = bf16[4,32,2048]{2,1,0:T(8,128)(2,1)} collective-permute-done((bf16[4,32,2048]{2,1,0:T(8,128)(2,1)}, bf16[4,32,2048]{2,1,0:T(8,128)(2,1)}, u32[]{:S(2)}, u32[]{:S(2)}) %collective-permute-start.32) | collective-permute-done | bytes 524320 | tf_op jit(solution)/shard_map/ppermute | solution.py:277
  165.3 3.6 %all-to-all-done.1 = bf16[4,64,2048]{2,1,0:T(8,128)(2,1)} async-done(((bf16[4,64,2048]{2,1,0:T(8,128)(2,1)}), bf16[4,64,2048]{2,1,0:T(8,128)(2,1)}, u32[]{:S(2)}, u32[]{:S(2)}) %all-to-all-start.1) | async-done | bytes 1048608 | tf_op jit(solution)/shard_map/all_to_all | solution.py:43
  168.9 3.1 %fusion.3 = bf16[256,2048]{1,0:T(8,128)(2,1)} fusion(bf16[256,2048]{1,0:T(8,128)(2,1)} %param.12, bf16[4,64,2048]{2,1,0:T(8,128)(2,1)} %all-to-all-done.1, bf16[1,256,2048]{2,1,0:T(8,128)(2,1)S(1)} %copy-done.1), kind=kLoop, calls=%fused_computation.12 | loop fusion | flops 3145728 | bytes 4194304 | tf_op jit(solution)/shard_map/convert_element_type | solution.py:290
  176.4 9.3 %collective-permute-done.33 = bf16[4,32,2048]{2,1,0:T(8,128)(2,1)} collective-permute-done((bf16[4,32,2048]{2,1,0:T(8,128)(2,1)}, bf16[4,32,2048]{2,1,0:T(8,128)(2,1)}, u32[]{:S(2)}, u32[]{:S(2)}) %collective-permute-start.33) | collective-permute-done | bytes 524320 | tf_op jit(solution)/shard_map/ppermute | solution.py:277
  187.1 9.8 %collective-permute-done.31 = bf16[4,32,2048]{2,1,0:T(8,128)(2,1)} collective-permute-done((bf16[4,32,2048]{2,1,0:T(8,128)(2,1)}, bf16[4,32,2048]{2,1,0:T(8,128)(2,1)}, u32[]{:S(2)}, u32[]{:S(2)}) %collective-permute-start.31) | collective-permute-done | bytes 524320 | tf_op jit(solution)/shard_map/ppermute | solution.py:277
  199.0 3.3 %fusion.12 = bf16[256,2048]{1,0:T(8,128)(2,1)} fusion(bf16[256,2048]{1,0:T(8,128)(2,1)} %collective-permute-done.35, bf16[4,64,2048]{2,1,0:T(8,128)(2,1)} %all-to-all-done.1, pred[]{:T(512)S(6)} %eq.79, bf16[1,256,2048]{2,1,0:T(8,128)(2,1)S(1)} %copy-done.1, bf16[256,2048]{1,0:T(8,128)(2,1)S(1)} %copy-done.3), kind=kLoop, calls=%fused_computation.32 | loop fusion | flops 5767168 | bytes 5242881 | tf_op jit(solution)/shard_map/jit(_where)/select_n | solution.py:293
  202.2 5.0 %collective-permute-done.34 = bf16[4,32,2048]{2,1,0:T(8,128)(2,1)S(1)} collective-permute-done((bf16[4,32,2048]{2,1,0:T(8,128)(2,1)S(1)}, bf16[4,32,2048]{2,1,0:T(8,128)(2,1)S(1)}, u32[]{:S(2)}, u32[]{:S(2)}) %collective-permute-start.34) | collective-permute-done | bytes 524320 | tf_op jit(solution)/shard_map/ppermute | solution.py:277
  (110 shorter events, 60.2 us)
Async XLA Ops:
  0.7 34.2 %collective-permute-start.4 = (bf16[512,2048]{1,0:T(8,128)(2,1)}, bf16[512,2048]{1,0:T(8,128)(2,1)S(1)}, u32[]{:S(2)}, u32[]{:S(2)}) collective-permute-start(bf16[512,2048]{1,0:T(8,128)(2,1)} %bitcast.185), channel_id=1, source_target_pairs={{0,1},{1,0},{2,3},{3,2},{4,5},{5,4},{6,7},{7,6},{8,9},{9,8},{10,11... | collective-permute-start | bytes 6291464 | tf_op jit(solution)/shard_map/ppermute | solution.py:39
  11.6 22.7 %collective-permute-start.2 = (bf16[2,64,1024]{2,1,0:T(8,128)(2,1)S(1)}, bf16[2,64,1024]{2,1,0:T(8,128)(2,1)S(1)}, u32[]{:S(2)}, u32[]{:S(2)}) collective-permute-start(bf16[2,64,1024]{2,1,0:T(8,128)(2,1)S(1)} %pad_maximum_fusion.3), channel_id=1, source_target_pairs={{0,8},{4,12},{8,0},{12,4},{1,9},{5,13},{9,1},{13,5},{2,10},{6,14},... | collective-permute-start | bytes 786440 | tf_op jit(solution)/shard_map/ppermute | solution.py:134
  11.6 22.7 %collective-permute-start.1 = (bf16[2,64,1024]{2,1,0:T(8,128)(2,1)S(1)}, bf16[2,64,1024]{2,1,0:T(8,128)(2,1)S(1)}, u32[]{:S(2)}, u32[]{:S(2)}) collective-permute-start(bf16[2,64,1024]{2,1,0:T(8,128)(2,1)S(1)} %pad_maximum_fusion.3), channel_id=1, source_target_pairs={{0,4},{4,8},{8,12},{12,0},{1,5},{5,9},{9,13},{13,1},{2,6},{6,10},{... | collective-permute-start | bytes 786440 | tf_op jit(solution)/shard_map/ppermute | solution.py:134
  12.8 27.4 %collective-permute-start.16 = (bf16[256,2048]{1,0:T(8,128)(2,1)S(1)}, bf16[256,2048]{1,0:T(8,128)(2,1)S(1)}, u32[]{:S(2)}, u32[]{:S(2)}) collective-permute-start(bf16[256,2048]{1,0:T(8,128)(2,1)S(1)} %bitcast.169), channel_id=1, source_target_pairs={{16,0},{17,1},{18,2},{19,3},{20,4},{21,5},{22,6},{23,7},{24,8},{25... | collective-permute-start | bytes 3145736 | tf_op jit(solution)/shard_map/ppermute | solution.py:19
  18.4 22.4 %collective-permute-start.5 = (bf16[2,1,64,2048]{3,2,1,0:T(8,128)(2,1)S(1)}, bf16[2,1,64,2048]{3,2,1,0:T(8,128)(2,1)S(1)}, u32[]{:S(2)}, u32[]{:S(2)}) collective-permute-start(bf16[2,1,64,2048]{3,2,1,0:T(8,128)(2,1)S(1)} %dynamic-slice_bitcast_fusion.3), channel_id=1, source_target_pairs={{0,2},{1,3},{2,0},{3,1},{4,6},{5,7},{6,4},{7,5},{8,10},{9,11},{10,... | collective-permute-start | bytes 1572872 | tf_op jit(solution)/shard_map/ppermute | solution.py:34
  37.3 28.5 %collective-permute-start.11 = (bf16[4,64,2048]{2,1,0:T(8,128)(2,1)S(1)}, bf16[4,64,2048]{2,1,0:T(8,128)(2,1)S(1)}, u32[]{:S(2)}, u32[]{:S(2)}) collective-permute-start(bf16[4,64,2048]{2,1,0:T(8,128)(2,1)S(1)} %fusion.2), channel_id=1, source_target_pairs={{0,2},{1,3},{2,0},{3,1},{4,6},{5,7},{6,4},{7,5},{8,10},{9,11},{10,... | collective-permute-start | bytes 3145736 | tf_op jit(solution)/shard_map/ppermute | solution.py:34
  41.8 23.7 %collective-permute-start.8 = (bf16[1,64,2048]{2,1,0:T(8,128)(2,1)S(1)}, bf16[1,64,2048]{2,1,0:T(8,128)(2,1)S(1)}, u32[]{:S(2)}, u32[]{:S(2)}) collective-permute-start(bf16[1,64,2048]{2,1,0:T(8,128)(2,1)S(1)} %get-tuple-element.48), channel_id=1, source_target_pairs={{0,8},{1,12},{2,10},{3,14},{4,9},{5,13},{6,11},{7,15},{8,0},{9,4},... | collective-permute-start | bytes 786440 | tf_op jit(solution)/shard_map/ppermute | solution.py:92
  42.8 22.7 %collective-permute-start.7 = (bf16[1,64,2048]{2,1,0:T(8,128)(2,1)S(1)}, bf16[1,64,2048]{2,1,0:T(8,128)(2,1)S(1)}, u32[]{:S(2)}, u32[]{:S(2)}) collective-permute-start(bf16[1,64,2048]{2,1,0:T(8,128)(2,1)S(1)} %get-tuple-element.49), channel_id=1, source_target_pairs={{0,1},{1,5},{2,3},{3,7},{4,0},{5,4},{6,2},{7,6},{8,9},{9,13},{10,1... | collective-permute-start | bytes 786440 | tf_op jit(solution)/shard_map/ppermute | solution.py:92
  44.9 20.6 %collective-permute-start.6 = (bf16[1,64,2048]{2,1,0:T(8,128)(2,1)S(1)}, bf16[1,64,2048]{2,1,0:T(8,128)(2,1)S(1)}, u32[]{:S(2)}, u32[]{:S(2)}) collective-permute-start(bf16[1,64,2048]{2,1,0:T(8,128)(2,1)S(1)} %get-tuple-element.46), channel_id=1, source_target_pairs={{1,4},{3,6},{4,1},{6,3},{9,12},{11,14},{12,9},{14,11},{17,20},{19,... | collective-permute-start | bytes 786440 | tf_op jit(solution)/shard_map/ppermute | solution.py:92
  52.0 21.6 %collective-permute-start.17 = (bf16[2,1,64,2048]{3,2,1,0:T(8,128)(2,1)S(1)}, bf16[2,1,64,2048]{3,2,1,0:T(8,128)(2,1)S(1)}, u32[]{:S(2)}, u32[]{:S(2)}) collective-permute-start(bf16[2,1,64,2048]{3,2,1,0:T(8,128)(2,1)S(1)} %dynamic-slice_bitcast_fusion.2), channel_id=1, source_target_pairs={{0,2},{1,3},{2,0},{3,1},{4,6},{5,7},{6,4},{7,5},{8,10},{9,11},{10,... | collective-permute-start | bytes 1572872 | tf_op jit(solution)/shard_map/ppermute | solution.py:34
  74.7 23.9 %collective-permute-start.20 = (bf16[1,64,2048]{2,1,0:T(8,128)(2,1)S(1)}, bf16[1,64,2048]{2,1,0:T(8,128)(2,1)S(1)}, u32[]{:S(2)}, u32[]{:S(2)}) collective-permute-start(bf16[1,64,2048]{2,1,0:T(8,128)(2,1)S(1)} %get-tuple-element.44), channel_id=1, source_target_pairs={{0,8},{1,12},{2,10},{3,14},{4,9},{5,13},{6,11},{7,15},{8,0},{9,4},... | collective-permute-start | bytes 786440 | tf_op jit(solution)/shard_map/ppermute | solution.py:92
  76.9 21.8 %collective-permute-start.19 = (bf16[1,64,2048]{2,1,0:T(8,128)(2,1)S(1)}, bf16[1,64,2048]{2,1,0:T(8,128)(2,1)S(1)}, u32[]{:S(2)}, u32[]{:S(2)}) collective-permute-start(bf16[1,64,2048]{2,1,0:T(8,128)(2,1)S(1)} %get-tuple-element.45), channel_id=1, source_target_pairs={{0,1},{1,5},{2,3},{3,7},{4,0},{5,4},{6,2},{7,6},{8,9},{9,13},{10,1... | collective-permute-start | bytes 786440 | tf_op jit(solution)/shard_map/ppermute | solution.py:92
  77.8 20.8 %collective-permute-start.18 = (bf16[1,64,2048]{2,1,0:T(8,128)(2,1)S(1)}, bf16[1,64,2048]{2,1,0:T(8,128)(2,1)S(1)}, u32[]{:S(2)}, u32[]{:S(2)}) collective-permute-start(bf16[1,64,2048]{2,1,0:T(8,128)(2,1)S(1)} %get-tuple-element.42), channel_id=1, source_target_pairs={{1,4},{3,6},{4,1},{6,3},{9,12},{11,14},{12,9},{14,11},{17,20},{19,... | collective-permute-start | bytes 786440 | tf_op jit(solution)/shard_map/ppermute | solution.py:92
  82.3 16.6 %collective-permute-start.15 = (bf16[4,32,2048]{2,1,0:T(8,128)(2,1)S(1)}, bf16[4,32,2048]{2,1,0:T(8,128)(2,1)S(1)}, u32[]{:S(2)}, u32[]{:S(2)}) collective-permute-start(bf16[4,32,2048]{2,1,0:T(8,128)(2,1)S(1)} %get-tuple-element.55), channel_id=1, source_target_pairs={{16,0},{17,1},{18,2},{19,3},{20,4},{21,5},{22,6},{23,7},{24,8},{25... | collective-permute-start | bytes 1572872 | tf_op jit(solution)/shard_map/ppermute | solution.py:19
  101.2 15.8 %collective-permute-start.26 = (bf16[4,32,2048]{2,1,0:T(8,128)(2,1)}, bf16[4,32,2048]{2,1,0:T(8,128)(2,1)S(1)}, u32[]{:S(2)}, u32[]{:S(2)}) collective-permute-start(bf16[4,32,2048]{2,1,0:T(8,128)(2,1)} %get-tuple-element.29), channel_id=1, source_target_pairs={{16,0},{17,1},{18,2},{19,3},{20,4},{21,5},{22,6},{23,7},{24,8},{25... | collective-permute-start | bytes 1572872 | tf_op jit(solution)/shard_map/ppermute | solution.py:19
  102.5 30.4 %all-to-all-start = ((bf16[4,64,2048]{2,1,0:T(8,128)(2,1)}), bf16[4,64,2048]{2,1,0:T(8,128)(2,1)}, u32[]{:S(2)}, u32[]{:S(2)}) async-start(bf16[4,64,2048]{2,1,0:T(8,128)(2,1)} %fusion.10), calls=%async_computation | async-start | bytes 2097152 | tf_op jit(solution)/shard_map/all_to_all | solution.py:43
  132.9 16.3 %collective-permute-start.25 = (bf16[4,32,2048]{2,1,0:T(8,128)(2,1)}, bf16[4,32,2048]{2,1,0:T(8,128)(2,1)S(1)}, u32[]{:S(2)}, u32[]{:S(2)}) collective-permute-start(bf16[4,32,2048]{2,1,0:T(8,128)(2,1)} %dynamic-slice_bitcast_fusion.1), channel_id=1, source_target_pairs={{0,4},{4,8},{8,12},{12,0},{1,5},{5,9},{9,13},{13,1},{2,6},{6,10},{... | collective-permute-start | bytes 1572872 | tf_op jit(solution)/shard_map/ppermute | solution.py:277
  146.3 16.9 %collective-permute-start.32 = (bf16[4,32,2048]{2,1,0:T(8,128)(2,1)}, bf16[4,32,2048]{2,1,0:T(8,128)(2,1)}, u32[]{:S(2)}, u32[]{:S(2)}) collective-permute-start(bf16[4,32,2048]{2,1,0:T(8,128)(2,1)} %dynamic-slice_bitcast_fusion), channel_id=1, source_target_pairs={{0,4},{4,8},{8,12},{12,0},{1,5},{5,9},{9,13},{13,1},{2,6},{6,10},{... | collective-permute-start | bytes 1572872 | tf_op jit(solution)/shard_map/ppermute | solution.py:277
  150.2 18.8 %all-to-all-start.1 = ((bf16[4,64,2048]{2,1,0:T(8,128)(2,1)}), bf16[4,64,2048]{2,1,0:T(8,128)(2,1)}, u32[]{:S(2)}, u32[]{:S(2)}) async-start(bf16[4,64,2048]{2,1,0:T(8,128)(2,1)} %all-to-all-done), calls=%async_computation.1 | async-start | bytes 2097152 | tf_op jit(solution)/shard_map/all_to_all | solution.py:43
  154.4 20.0 %collective-permute-start.30 = (bf16[4,32,2048]{2,1,0:T(8,128)(2,1)}, bf16[4,32,2048]{2,1,0:T(8,128)(2,1)}, u32[]{:S(2)}, u32[]{:S(2)}) collective-permute-start(bf16[4,32,2048]{2,1,0:T(8,128)(2,1)} %fusion.16), channel_id=1, source_target_pairs={{0,4},{4,8},{8,12},{12,0},{1,5},{5,9},{9,13},{13,1},{2,6},{6,10},{... | collective-permute-start | bytes 1572872 | tf_op jit(solution)/shard_map/ppermute | solution.py:277
  165.3 20.4 %collective-permute-start.33 = (bf16[4,32,2048]{2,1,0:T(8,128)(2,1)}, bf16[4,32,2048]{2,1,0:T(8,128)(2,1)}, u32[]{:S(2)}, u32[]{:S(2)}) collective-permute-start(bf16[4,32,2048]{2,1,0:T(8,128)(2,1)} %fusion.13), channel_id=1, source_target_pairs={{0,4},{4,8},{8,12},{12,0},{1,5},{5,9},{9,13},{13,1},{2,6},{6,10},{... | collective-permute-start | bytes 1572872 | tf_op jit(solution)/shard_map/ppermute | solution.py:277
  172.0 26.9 %collective-permute-start.35 = (bf16[256,2048]{1,0:T(8,128)(2,1)}, bf16[256,2048]{1,0:T(8,128)(2,1)}, u32[]{:S(2)}, u32[]{:S(2)}) collective-permute-start(bf16[256,2048]{1,0:T(8,128)(2,1)} %fusion.3), channel_id=1, source_target_pairs={{16,0},{17,1},{18,2},{19,3},{20,4},{21,5},{22,6},{23,7},{24,8},{25... | collective-permute-start | bytes 3145736 | tf_op jit(solution)/shard_map/ppermute | solution.py:19
  176.4 20.5 %collective-permute-start.31 = (bf16[4,32,2048]{2,1,0:T(8,128)(2,1)}, bf16[4,32,2048]{2,1,0:T(8,128)(2,1)}, u32[]{:S(2)}, u32[]{:S(2)}) collective-permute-start(bf16[4,32,2048]{2,1,0:T(8,128)(2,1)} %fusion.17), channel_id=1, source_target_pairs={{0,4},{4,8},{8,12},{12,0},{1,5},{5,9},{9,13},{13,1},{2,6},{6,10},{... | collective-permute-start | bytes 1572872 | tf_op jit(solution)/shard_map/ppermute | solution.py:277
  187.0 20.2 %collective-permute-start.34 = (bf16[4,32,2048]{2,1,0:T(8,128)(2,1)S(1)}, bf16[4,32,2048]{2,1,0:T(8,128)(2,1)S(1)}, u32[]{:S(2)}, u32[]{:S(2)}) collective-permute-start(bf16[4,32,2048]{2,1,0:T(8,128)(2,1)S(1)} %fusion.14), channel_id=1, source_target_pairs={{0,4},{4,8},{8,12},{12,0},{1,5},{5,9},{9,13},{13,1},{2,6},{6,10},{... | collective-permute-start | bytes 1572872 | tf_op jit(solution)/shard_map/ppermute | solution.py:277
  (21 other events, 203.4 us)
